TPU v7x, 32 devices: a whole 2x2x4 slice. The times are simulated.
32 devices in a mesh: dom: 4 (over x, core), blk: 8 (over z, y).
Axes of the slice: x: 2, y: 2, z: 4, core: 2. Of those that a mesh axis runs over, the one named last changes fastest.
Arguments:
- incident: bfloat16 [256, 512, 192], P(('dom', 'blk')), may hold values from -6 to 6
- t_matrices: bfloat16 [256, 512, 512], P(('dom', 'blk')), may hold values from -0.25 to 0.25
- translations: bfloat16 [4, 512, 512], replicated, may hold values from -0.125 to 0.125
- near_index: int32 [256, 6], P(('dom', 'blk')), may hold values from 0 to 255, as said below
- near_count: int32 [256], P(('dom', 'blk')), may hold values from 1 to 6, as said below
- near_type: int32 [256, 6], P(('dom', 'blk')), may hold values from 0 to 3
- phases: bfloat16 [256, 2048], P(('dom', 'blk')), may hold values from -1 to 1
- wave_basis: bfloat16 [2048, 512], replicated, may hold values from -0.25 to 0.25
- grating_blocks: float32 [16, 128, 128], P('blk'), may hold values from -0.0234375 to 0.0234375
Outputs:
- coeffs: bfloat16 [256, 512, 192], P(('dom', 'blk'))
Inputs may be any that keep to these rules, and one draw needn't show every extreme that they name: `near_index`: the first near_count[p] entries of row p are distinct particles other than p, each within 4 of p, ascending; the remaining entries equal p and carry no weight. `near_count`: some particle has exactly 6 live neighbours.
All inputs are finite; a program needn't handle non-finite values.
Results may differ from a plain program's by a relative error of at most 0.015.
Values may be sent and summed in bfloat16 or wider, within the bound.
No kernel may reach another device: no remote copies, remote signals or barrier semaphores. Data moves between devices by JAX's collectives and lax.ppermute only.
A program may use at most 64 MiB of HBM per device.

v0:
```python
import jax
import jax.numpy as jnp
from jax import lax
from jax.sharding import PartitionSpec as P

ITERS = 2


def padded(array, sides, width):
    for axis, dim in sides:
        peers, length = (lax.axis_size(axis), array.shape[dim])
        up = [(i, (i + 1) % peers) for i in range(peers - 1)]
        down = [(j, i) for i, j in up]
        last = lax.slice_in_dim(array, length - width, length, axis=dim)
        initial = lax.slice_in_dim(array, 0, width, axis=dim)
        before = lax.ppermute(last, axis, up)
        after = lax.ppermute(initial, axis, down)
        array = jnp.concatenate([before, array, after], axis=dim)
    return array


def local(
    incident,
    t_matrices,
    translations,
    near_index,
    near_count,
    near_type,
    phases,
    wave_basis,
    grating_blocks,
):
    local_count = incident.shape[0]
    reach = local_count // 2
    kinds = translations.shape[0]
    most = near_index.shape[1]
    total_rows = wave_basis.shape[0]
    block_rows = total_rows // lax.axis_size("blk")
    order = grating_blocks.shape[1]
    first_index = lax.axis_index(("dom", "blk")) * local_count
    slots = near_index - first_index + reach
    live = jnp.arange(most)[None, :] < near_count[:, None]
    kind_hit = (near_type[None] == jnp.arange(kinds)[:, None, None]) & live[None]
    place_hit = slots[:, :, None] == jnp.arange(local_count + 2 * reach)[None, None, :]
    selector = jnp.sum((kind_hit[..., None] & place_hit[None]).astype(jnp.float32), axis=2).astype(
        jnp.bfloat16
    )
    phase_wide = phases.astype(jnp.float32)

    def scatter_solve(source):
        return jnp.einsum(
            "pab,pbm->pam", t_matrices, source, preferred_element_type=jnp.float32
        ).astype(jnp.bfloat16)

    coeffs = scatter_solve(incident)
    for sweep in range(ITERS):
        current = coeffs
        extended = padded(current, ((("dom", "blk"), 0),), reach)
        grouped = jnp.einsum(
            "tij,jlm->tilm", selector, extended, preferred_element_type=jnp.float32
        ).astype(jnp.bfloat16)
        near_field = jnp.einsum(
            "tab,tibm->iam", translations, grouped, preferred_element_type=jnp.float32
        )
        spread = jnp.einsum("gl,plm->pgm", wave_basis, current, preferred_element_type=jnp.float32)
        partial_rows = lax.psum_scatter(
            jnp.einsum("pg,pgm->gm", phase_wide, spread).astype(jnp.bfloat16),
            "blk",
            scatter_dimension=0,
            tiled=True,
        )
        sums = lax.psum_scatter(partial_rows, "dom", scatter_dimension=1, tiled=True).astype(
            jnp.float32
        )
        columns = sums.shape[1]
        shaped = sums.reshape(grating_blocks.shape[0], order, columns)
        result = jnp.einsum("bij,bjm->bim", grating_blocks, shaped, precision=lax.Precision.HIGHEST)
        reflected = lax.all_gather(
            result.reshape(block_rows, columns).astype(jnp.bfloat16), "dom", axis=1, tiled=True
        )
        weighted = (
            phase_wide[:, :, None]
            * lax.all_gather(reflected, "blk", axis=0, tiled=True).astype(jnp.float32)[None]
        ).astype(jnp.bfloat16)
        returned = jnp.einsum(
            "gl,pgm->plm", wave_basis, weighted, preferred_element_type=jnp.float32
        )
        source = (incident.astype(jnp.float32) + near_field + returned).astype(jnp.bfloat16)
        coeffs = scatter_solve(source)
    return coeffs


def solution(mesh):
    placed = (
        P(("dom", "blk"), None, None),
        P(("dom", "blk"), None, None),
        P(),
        P(("dom", "blk"), None),
        P(("dom", "blk")),
        P(("dom", "blk"), None),
        P(("dom", "blk"), None),
        P(),
        P("blk", None, None),
    )
    return jax.shard_map(
        local, mesh=mesh, in_specs=placed, out_specs=P(("dom", "blk"), None, None), check_vma=False
    )
```

profile of v0, /device:TPU:0, one launch (start us, length us, event | category | flops | bytes accessed | tf_op | source)
XLA Modules:
  0.0 340.5 jit_solution(9729539308603017054)
XLA Ops:
  6.5 0.0 copy-start
  6.5 0.0 reduce-scatter.5.cloned.1.call-start
  6.5 0.9 fusion.65
  7.5 4.2 %convolution_convert_fusion.4 = bf16[8,512,192]{1,2,0:T(8,128)(2,1)S(1)} fusion(bf16[8,512,512]{2,1,0:T(8,128)(2,1)} %param.10, bf16[8,512,192]{1,2,0:T(8,128)(2,1)} %param.9), kind=kOutput, calls=%fused_computation.38 | convolution fusion | flops 806092800 | bytes 7340032 | tf_op jit(solution)/shard_map/pab,pbm->pam/dot_general | solution.py:51
  11.7 0.0 copy-start.1
  11.7 1.1 copy-done.1
  12.8 0.0 copy-done
  12.8 4.8 %fusion.1 = bf16[2048,192]{0,1:T(8,128)(2,1)} fusion(f32[2048,8]{0,1:T(8,128)S(1)} %get-tuple-element.10, bf16[8,512,192]{1,2,0:T(8,128)(2,1)S(1)} %convolution_convert_fusion.4, bf16[2048,512]{1,0:T(8,128)(2,1)S(1)} %copy-done), kind=kOutput, calls=%fused_computation.3 | convolution fusion | flops 3227123712 | bytes 4521984 | tf_op jit(solution)/shard_map/gl,plm->pgm/dot_general | solution.py:65
  17.6 0.0 copy-start.4
  17.6 0.0 copy-start.5
  17.6 0.0 copy-start.6
  17.6 0.0 reduce-scatter.5.cloned.1.call-update
  17.6 0.0 reduce-scatter.7.cloned.1.call-start
  17.7 2.6 fusion.64
  20.3 4.9 %collective-permute-start = (bf16[4,512,192]{1,2,0:T(8,128)(2,1)}, bf16[4,512,192]{1,2,0:T(8,128)(2,1)S(1)}, u32[]{:S(2)}, u32[]{:S(2)}) collective-permute-start(bf16[4,512,192]{1,2,0:T(8,128)(2,1)} %get-tuple-element.7), channel_id=1, source_target_pairs={{0,1},{1,2},{2,3},{3,4},{4,5},{5,6},{6,7},{7,8},{8,9},{9,10},{10,1... | collective-permute-start | bytes 2359304 | tf_op jit(solution)/shard_map/ppermute | solution.py:16
  25.2 1.3 collective-permute-start.1
  26.5 0.0 copy-done.4
  26.5 0.1 copy.17
  26.6 0.0 copy-done.5
  26.6 0.1 copy.16
  26.7 0.0 copy-done.6
  26.7 0.1 iota_compare_fusion
  26.8 0.1 convert_reduce_fusion
  26.9 35.4 %collective-permute-done = bf16[4,512,192]{1,2,0:T(8,128)(2,1)S(1)} collective-permute-done((bf16[4,512,192]{1,2,0:T(8,128)(2,1)}, bf16[4,512,192]{1,2,0:T(8,128)(2,1)S(1)}, u32[]{:S(2)}, u32[]{:S(2)}) %collective-permute-start) | collective-permute-done | bytes 786464 | tf_op jit(solution)/shard_map/ppermute | solution.py:16
  62.3 0.0 collective-permute-done.1
  62.3 3.1 pad_maximum_fusion
  65.4 30.6 %reduce-scatter.5.cloned.1.call-done = bf16[256,192]{0,1:T(8,128)(2,1)} async-done(((bf16[2048,192]{0,1:T(8,128)(2,1)}), bf16[256,192]{0,1:T(8,128)(2,1)}) %reduce-scatter.5.cloned.1.call-update) | async-done | bytes 98320 | tf_op jit(solution)/shard_map/reduce_scatter | solution.py:66
  96.1 0.0 reduce-scatter.7.cloned.1.call-update
  96.1 0.0 copy-start.3
  96.1 0.0 reduce-scatter.9.cloned.1.call-start
  96.1 6.8 %convolution_convert_fusion.1 = bf16[4,8,512,192]{2,1,3,0:T(8,128)(2,1)} fusion(bf16[16,512,192]{1,2,0:T(8,128)(2,1)} %pad_maximum_fusion, bf16[4,8,16]{2,1,0:T(8,128)(2,1)S(1)} %convert_reduce_fusion), kind=kOutput, calls=%fused_computation.19 | convolution fusion | flops 103809024 | bytes 9438208 | tf_op jit(solution)/shard_map/tij,jlm->tilm/dot_general | solution.py:59
  102.9 14.2 %reduce-scatter.7.cloned.1.call-done = bf16[256,48]{0,1:T(8,128)(2,1)} async-done(((bf16[256,192]{0,1:T(8,128)(2,1)}), bf16[256,48]{0,1:T(8,128)(2,1)}) %reduce-scatter.7.cloned.1.call-update) | async-done | bytes 24592 | tf_op jit(solution)/shard_map/reduce_scatter | solution.py:72
  117.1 0.0 copy-done.3
  117.1 0.9 fusion.52
  118.1 5.3 %all_gather.12 = bf16[256,192]{0,1:T(8,128)(2,1)S(1)} all-gather(bf16[256,48]{0,1:T(8,128)(2,1)S(1)} %bitcast.122), channel_id=1, replica_groups=mesh['dom'=4,'blk'=8] {'dom'}, dimensions={1}, use_global_device_ids=true | all-gather | bytes 122880 | tf_op jit(solution)/shard_map/all_gather | solution.py:78
  123.4 32.2 %all_gather.13 = bf16[2048,192]{0,1:T(8,128)(2,1)S(1)} all-gather(bf16[256,192]{0,1:T(8,128)(2,1)S(1)} %all_gather.12), channel_id=1, replica_groups=mesh['dom'=4,'blk'=8] {'blk'}, dimensions={0}, use_global_device_ids=true | all-gather | bytes 884736 | tf_op jit(solution)/shard_map/all_gather | solution.py:83
  155.7 0.2 convert_element_type.88
  155.9 5.2 %fusion.2 = f32[8,192,512]{2,1,0:T(8,128)} fusion(f32[2048,192]{0,1:T(8,128)S(1)} %convert_element_type.88, f32[8,2048]{1,0:T(8,128)S(1)} %get-tuple-element.9, bf16[2048,512]{1,0:T(8,128)(2,1)S(1)} %copy-done), kind=kOutput, calls=%fused_computation.6 | convolution fusion | flops 3227516928 | bytes 6881280 | tf_op jit(solution)/shard_map/gl,pgm->plm/dot_general | solution.py:85
  161.0 13.0 %fusion.42 = bf16[8,512,192]{1,2,0:T(8,128)(2,1)} fusion(bf16[8,512,512]{2,1,0:T(8,128)(2,1)} %param.10, bf16[8,512,192]{1,2,0:T(8,128)(2,1)} %param.9, f32[8,192,512]{2,1,0:T(8,128)} %fusion.2, bf16[4,512,512]{2,1,0:T(8,128)(2,1)} %param.11, bf16[4,8,512,192]{2,1,3,0:T(8,128)(2,1)} %convolution_convert_fusion.1), kind=kOutput, calls=%fused_computation.39 | convolution fusion | flops 4030464000 | bytes 18874368 | tf_op jit(solution)/shard_map/pab,pbm->pam/dot_general | solution.py:51
  174.1 6.2 %fusion = bf16[2048,192]{0,1:T(8,128)(2,1)} fusion(f32[2048,8]{0,1:T(8,128)S(1)} %get-tuple-element.10, bf16[8,512,192]{1,2,0:T(8,128)(2,1)} %fusion.42, bf16[2048,512]{1,0:T(8,128)(2,1)S(1)} %copy-done), kind=kOutput, calls=%fused_computation.1 | convolution fusion | flops 3227123712 | bytes 4521984 | tf_op jit(solution)/shard_map/gl,plm->pgm/dot_general | solution.py:65
  180.2 0.0 reduce-scatter.9.cloned.1.call-update
  180.3 0.0 reduce-scatter.11.cloned.1.call-start
  180.3 0.0 copy-start.2
  180.3 1.6 fusion.63
  181.9 3.6 %collective-permute-start.2 = (bf16[4,512,192]{1,2,0:T(8,128)(2,1)S(1)}, bf16[4,512,192]{1,2,0:T(8,128)(2,1)S(1)}, u32[]{:S(2)}, u32[]{:S(2)}) collective-permute-start(bf16[4,512,192]{1,2,0:T(8,128)(2,1)S(1)} %get-tuple-element.5), channel_id=1, source_target_pairs={{0,1},{1,2},{2,3},{3,4},{4,5},{5,6},{6,7},{7,8},{8,9},{9,10},{10,1... | collective-permute-start | bytes 2359304 | tf_op jit(solution)/shard_map/ppermute | solution.py:16
  185.5 1.5 collective-permute-start.3
  187.0 28.5 %collective-permute-done.2 = bf16[4,512,192]{1,2,0:T(8,128)(2,1)S(1)} collective-permute-done((bf16[4,512,192]{1,2,0:T(8,128)(2,1)S(1)}, bf16[4,512,192]{1,2,0:T(8,128)(2,1)S(1)}, u32[]{:S(2)}, u32[]{:S(2)}) %collective-permute-start.2) | collective-permute-done | bytes 786464 | tf_op jit(solution)/shard_map/ppermute | solution.py:16
  215.5 0.0 collective-permute-done.3
  215.5 0.0 copy-done.2
  215.5 1.9 pad_maximum_fusion.1
  217.4 39.0 %reduce-scatter.9.cloned.1.call-done = bf16[256,192]{0,1:T(8,128)(2,1)} async-done(((bf16[2048,192]{0,1:T(8,128)(2,1)}), bf16[256,192]{0,1:T(8,128)(2,1)}) %reduce-scatter.9.cloned.1.call-update) | async-done | bytes 98320 | tf_op jit(solution)/shard_map/reduce_scatter | solution.py:66
  256.3 0.0 reduce-scatter.11.cloned.1.call-update
  256.4 6.7 %convolution_convert_fusion = bf16[4,8,512,192]{2,1,3,0:T(8,128)(2,1)} fusion(bf16[16,512,192]{1,2,0:T(8,128)(2,1)} %pad_maximum_fusion.1, bf16[4,8,16]{2,1,0:T(8,128)(2,1)S(1)} %convert_reduce_fusion), kind=kOutput, calls=%fused_computation.18 | convolution fusion | flops 103809024 | bytes 9438208 | tf_op jit(solution)/shard_map/tij,jlm->tilm/dot_general | solution.py:59
  263.1 14.1 %reduce-scatter.11.cloned.1.call-done = bf16[256,48]{0,1:T(8,128)(2,1)} async-done(((bf16[256,192]{0,1:T(8,128)(2,1)}), bf16[256,48]{0,1:T(8,128)(2,1)}) %reduce-scatter.11.cloned.1.call-update) | async-done | bytes 24592 | tf_op jit(solution)/shard_map/reduce_scatter | solution.py:72
  277.2 0.9 fusion.53
  278.1 5.3 %all_gather.14 = bf16[256,192]{0,1:T(8,128)(2,1)S(1)} all-gather(bf16[256,48]{0,1:T(8,128)(2,1)S(1)} %bitcast.123), channel_id=1, replica_groups=mesh['dom'=4,'blk'=8] {'dom'}, dimensions={1}, use_global_device_ids=true | all-gather | bytes 122880 | tf_op jit(solution)/shard_map/all_gather | solution.py:78
  283.5 32.1 %all_gather.15 = bf16[2048,192]{0,1:T(8,128)(2,1)S(1)} all-gather(bf16[256,192]{0,1:T(8,128)(2,1)S(1)} %all_gather.14), channel_id=1, replica_groups=mesh['dom'=4,'blk'=8] {'blk'}, dimensions={0}, use_global_device_ids=true | all-gather | bytes 884736 | tf_op jit(solution)/shard_map/all_gather | solution.py:83
  315.6 0.2 convert_element_type.98
  315.7 5.2 %fusion.3 = f32[8,192,512]{2,1,0:T(8,128)} fusion(f32[2048,192]{0,1:T(8,128)S(1)} %convert_element_type.98, f32[8,2048]{1,0:T(8,128)S(1)} %get-tuple-element.9, bf16[2048,512]{1,0:T(8,128)(2,1)S(1)} %copy-done), kind=kOutput, calls=%fused_computation.7 | convolution fusion | flops 3227516928 | bytes 6881280 | tf_op jit(solution)/shard_map/gl,pgm->plm/dot_general | solution.py:85
  320.9 13.0 %fusion.47 = bf16[8,512,192]{1,2,0:T(8,128)(2,1)} fusion(bf16[8,512,512]{2,1,0:T(8,128)(2,1)} %param.10, bf16[8,512,192]{1,2,0:T(8,128)(2,1)} %param.9, f32[8,192,512]{2,1,0:T(8,128)} %fusion.3, bf16[4,512,512]{2,1,0:T(8,128)(2,1)} %param.11, bf16[4,8,512,192]{2,1,3,0:T(8,128)(2,1)} %convolution_convert_fusion), kind=kOutput, calls=%fused_computation.40 | convolution fusion | flops 4030464000 | bytes 18874368 | tf_op jit(solution)/shard_map/pab,pbm->pam/dot_general | solution.py:51
  (5 shorter events, 0.1 us)
Async XLA Ops:
  6.5 6.3 %copy-start = (bf16[2048,512]{1,0:T(8,128)(2,1)S(1)}, bf16[2048,512]{1,0:T(8,128)(2,1)}, u32[]{:S(2)}) copy-start(bf16[2048,512]{1,0:T(8,128)(2,1)} %param.16) | copy-start | bytes 6291460
  6.5 89.5 %reduce-scatter.5.cloned.1.call-start = ((), (), s32[]{:S(2)}) async-start(), calls=%async_computation.4 | async-start | bytes 884736 | tf_op jit(solution)/shard_map/reduce_scatter | solution.py:66
  11.7 1.1 copy-start.1
  17.6 8.9 %copy-start.4 = (s32[8,6]{1,0:T(8,128)S(1)}, s32[8,6]{1,0:T(8,128)}, u32[]{:S(2)}) copy-start(s32[8,6]{1,0:T(8,128)} %param.12) | copy-start | bytes 580
  17.6 9.0 %copy-start.5 = (s32[8,6]{1,0:T(8,128)S(1)}, s32[8,6]{1,0:T(8,128)}, u32[]{:S(2)}) copy-start(s32[8,6]{1,0:T(8,128)} %param.14) | copy-start | bytes 580
  17.6 9.1 %copy-start.6 = (s32[8]{0:T(128)S(1)}, s32[8]{0:T(128)}, u32[]{:S(2)}) copy-start(s32[8]{0:T(128)} %param.13) | copy-start | bytes 100
  17.6 99.5 %reduce-scatter.7.cloned.1.call-start = ((), (), s32[]{:S(2)}) async-start(), calls=%async_computation.5 | async-start | bytes 122880 | tf_op jit(solution)/shard_map/reduce_scatter | solution.py:72
  20.3 42.0 %collective-permute-start = (bf16[4,512,192]{1,2,0:T(8,128)(2,1)}, bf16[4,512,192]{1,2,0:T(8,128)(2,1)S(1)}, u32[]{:S(2)}, u32[]{:S(2)}) collective-permute-start(bf16[4,512,192]{1,2,0:T(8,128)(2,1)} %get-tuple-element.7), channel_id=1, source_target_pairs={{0,1},{1,2},{2,3},{3,4},{4,5},{5,6},{6,7},{7,8},{8,9},{9,10},{10,1... | collective-permute-start | bytes 2359304 | tf_op jit(solution)/shard_map/ppermute | solution.py:16
  25.2 37.1 %collective-permute-start.1 = (bf16[4,512,192]{1,2,0:T(8,128)(2,1)}, bf16[4,512,192]{1,2,0:T(8,128)(2,1)}, u32[]{:S(2)}, u32[]{:S(2)}) collective-permute-start(bf16[4,512,192]{1,2,0:T(8,128)(2,1)} %get-tuple-element.8), channel_id=1, source_target_pairs={{1,0},{2,1},{3,2},{4,3},{5,4},{6,5},{7,6},{8,7},{9,8},{10,9},{11,1... | collective-permute-start | bytes 2359304 | tf_op jit(solution)/shard_map/ppermute | solution.py:17
  96.1 21.0 %copy-start.3 = (f32[2,128,128]{2,1,0:T(8,128)S(1)}, f32[2,128,128]{2,1,0:T(8,128)}, u32[]{:S(2)}) copy-start(f32[2,128,128]{2,1,0:T(8,128)} %param.17) | copy-start | bytes 393220
  96.1 160.2 %reduce-scatter.9.cloned.1.call-start = ((), (), s32[]{:S(2)}) async-start(), calls=%async_computation.6 | async-start | bytes 884736 | tf_op jit(solution)/shard_map/reduce_scatter | solution.py:66
  180.3 96.9 %reduce-scatter.11.cloned.1.call-start = ((), (), s32[]{:S(2)}) async-start(), calls=%async_computation.7 | async-start | bytes 122880 | tf_op jit(solution)/shard_map/reduce_scatter | solution.py:72
  180.3 35.2 %copy-start.2 = (bf16[8,512,192]{1,2,0:T(8,128)(2,1)S(1)}, bf16[8,512,192]{1,2,0:T(8,128)(2,1)}, u32[]{:S(2)}) copy-start(bf16[8,512,192]{1,2,0:T(8,128)(2,1)} %fusion.42) | copy-start | bytes 4718596
  181.9 33.6 %collective-permute-start.2 = (bf16[4,512,192]{1,2,0:T(8,128)(2,1)S(1)}, bf16[4,512,192]{1,2,0:T(8,128)(2,1)S(1)}, u32[]{:S(2)}, u32[]{:S(2)}) collective-permute-start(bf16[4,512,192]{1,2,0:T(8,128)(2,1)S(1)} %get-tuple-element.5), channel_id=1, source_target_pairs={{0,1},{1,2},{2,3},{3,4},{4,5},{5,6},{6,7},{7,8},{8,9},{9,10},{10,1... | collective-permute-start | bytes 2359304 | tf_op jit(solution)/shard_map/ppermute | solution.py:16
  185.5 30.0 %collective-permute-start.3 = (bf16[4,512,192]{1,2,0:T(8,128)(2,1)S(1)}, bf16[4,512,192]{1,2,0:T(8,128)(2,1)S(1)}, u32[]{:S(2)}, u32[]{:S(2)}) collective-permute-start(bf16[4,512,192]{1,2,0:T(8,128)(2,1)S(1)} %get-tuple-element.6), channel_id=1, source_target_pairs={{1,0},{2,1},{3,2},{4,3},{5,4},{6,5},{7,6},{8,7},{9,8},{10,9},{11,1... | collective-permute-start | bytes 2359304 | tf_op jit(solution)/shard_map/ppermute | solution.py:17
Sparse Core Ops, SparseCore 0:
  17.7 78.2 reduce-scatter.4
  98.6 18.4 reduce-scatter.6
  180.4 75.8 reduce-scatter.8
  258.6 18.5 reduce-scatter.10
where the time goes:
time: 341 us; the launch traced here: 340 us
  waiting for transfers between devices  162 us (48%)
  blocking collectives  75 us (22%)
  matrix products  67 us (20%)
  between operations  13.3 us (4%)
  starting transfers between devices  11.4 us (3%)
  other arithmetic  6.48 us (2%)
  local copies, waits for them, and re-layouts  5.57 us (2%)
    reduce_scatter x2, waiting for transfers between devices, local(): lax.psum_scatter(jnp.einsum('pg,pgm->gm', phase_wide, spread).astype(jnp....  69.6 us
    all_gather x2, blocking collectives, local(): lax.all_gather(reflected, 'blk', axis=0, tiled=True).astype(jnp.float32)  64.3 us
    ppermute x2, waiting for transfers between devices, padded(): before = lax.ppermute(last, axis, up)  63.8 us
    dot_general x3, matrix products, scatter_solve(): jnp.einsum('pab,pbm->pam', t_matrices, source, preferred_element_type=jnp...  30.2 us
    reduce_scatter x2, waiting for transfers between devices, local(): lax.psum_scatter(partial_rows, 'dom', scatter_dimension=1, tiled=True)  28.3 us
    dot_general x2, matrix products, local(): jnp.einsum('tij,jlm->tilm', selector, extended, preferred_element_type=jn...  13.5 us
    dot_general x2, matrix products, local(): jnp.einsum('gl,plm->pgm', wave_basis, current, preferred_element_type=jnp...  11 us
    all_gather x2, blocking collectives, local(): lax.all_gather(result.reshape(block_rows, columns).astype(jnp.bfloat16),...  10.7 us
  transfers between devices with their start and end apart: 8, of which 6 were waited for; matrix products, arithmetic and copies ran while one was open for 7% of the time, Pallas kernels for 0%

commit v1 on v0

v1 whole, which is shorter than its diff:
```python
import jax
import jax.numpy as jnp
from jax import lax
from jax.experimental import pallas as pl
from jax.experimental.pallas import tpu as pltpu
from jax.sharding import PartitionSpec as P

ITERS = 2
AXES = ("dom", "blk")
F32 = jnp.float32
BF16 = jnp.bfloat16
LAST = (((1,), (1,)), ((), ()))
MIB = 1 << 20


def params(mib):
    return pltpu.CompilerParams(vmem_limit_bytes=mib * MIB)


def cost(macs, moved):
    return pl.CostEstimate(flops=2 * macs, bytes_accessed=moved, transcendentals=0)


def solve_kernel(source_ref, t_ref, out_ref):
    out_ref[0] = lax.dot_general(
        source_ref[0], t_ref[0], LAST, preferred_element_type=F32
    ).astype(BF16)


def solve(source, t_matrices, start, count):
    m, size = source.shape[1:]
    return pl.pallas_call(
        solve_kernel,
        grid=(count,),
        in_specs=[
            pl.BlockSpec((1, m, size), lambda p: (start + p, 0, 0)),
            pl.BlockSpec((1, size, size), lambda p: (start + p, 0, 0)),
        ],
        out_specs=pl.BlockSpec((1, m, size), lambda p: (p, 0, 0)),
        out_shape=jax.ShapeDtypeStruct((count, m, size), BF16),
        compiler_params=params(16),
        cost_estimate=cost(count * m * size * size, 2 * count * size * (2 * m + size)),
        name="solve",
    )(source, t_matrices)


def outward_kernel(part_ref, low_ref, high_ref, basis_ref, phase_ref, out_ref):
    half, rows, size = low_ref.shape
    width = basis_ref.shape[0]
    total = jnp.zeros((rows, width), F32)
    for index, ref in ((0, low_ref), (half, high_ref)):
        spread = lax.dot_general(
            ref[...].reshape(half * rows, size),
            basis_ref[...],
            LAST,
            preferred_element_type=F32,
        )
        for p in range(half):
            phase = phase_ref[index + p, :].astype(F32)[None, :]
            total = total + phase * spread[p * rows : (p + 1) * rows]
    out_ref[0] = total.astype(BF16)


def outward(part, low, high, basis, phases, parts, chunks):
    half, m, size = low.shape
    total_rows = basis.shape[0]
    width = total_rows // chunks
    rows = m // parts
    return pl.pallas_call(
        outward_kernel,
        grid_spec=pltpu.PrefetchScalarGridSpec(
            num_scalar_prefetch=1,
            grid=(chunks,),
            in_specs=[
                pl.BlockSpec((half, rows, size), lambda g, part: (0, part[0], 0)),
                pl.BlockSpec((half, rows, size), lambda g, part: (0, part[0], 0)),
                pl.BlockSpec((width, size), lambda g, part: (g, 0)),
                pl.BlockSpec((2 * half, width), lambda g, part: (0, g)),
            ],
            out_specs=pl.BlockSpec((1, rows, width), lambda g, part: (g, 0, 0)),
        ),
        out_shape=jax.ShapeDtypeStruct((chunks, rows, width), BF16),
        compiler_params=params(24),
        cost_estimate=cost(
            2 * half * rows * size * total_rows, 2 * size * (total_rows + 2 * half * rows)
        ),
        name="outward",
    )(part, low, high, basis, phases)


def near_kernel(
    slot_ref,
    count_ref,
    type_ref,
    before_ref,
    low_ref,
    high_ref,
    after_ref,
    incident_ref,
    translations_ref,
    out_ref,
    extended,
    sums,
):
    group, m, size = incident_ref.shape
    reach = low_ref.shape[0]
    kinds = translations_ref.shape[0]
    most = slot_ref.shape[1]
    step = pl.program_id(0)

    @pl.when(step == 0)
    def _():
        for index, ref in enumerate((before_ref, low_ref, high_ref, after_ref)):
            extended[pl.ds(index * reach, reach)] = ref[...]

    sums[...] = jnp.zeros(sums.shape, F32)
    for i in range(group):
        p = step * group + i
        for k in range(most):

            @pl.when(k < count_ref[p])
            def _():
                place = type_ref[p, k]
                sums[place, i] += extended[slot_ref[p, k]].astype(F32)

    total = incident_ref[...].astype(F32).reshape(group * m, size)
    for t in range(kinds):
        total = total + lax.dot_general(
            sums[t].astype(BF16).reshape(group * m, size),
            translations_ref[t],
            LAST,
            preferred_element_type=F32,
        )
    out_ref[...] = total.reshape(group, m, size)


def near(slots, counts, types, before, low, high, after, incident, translations):
    count, m, size = incident.shape
    reach = low.shape[0]
    kinds = translations.shape[0]
    group = 4
    whole = pl.BlockSpec((reach, m, size), lambda p, *_: (0, 0, 0))
    return pl.pallas_call(
        near_kernel,
        grid_spec=pltpu.PrefetchScalarGridSpec(
            num_scalar_prefetch=3,
            grid=(count // group,),
            in_specs=[
                whole,
                whole,
                whole,
                whole,
                pl.BlockSpec((group, m, size), lambda p, *_: (p, 0, 0)),
                pl.BlockSpec((kinds, size, size), lambda p, *_: (0, 0, 0)),
            ],
            out_specs=pl.BlockSpec((group, m, size), lambda p, *_: (p, 0, 0)),
            scratch_shapes=[
                pltpu.VMEM((4 * reach, m, size), BF16),
                pltpu.VMEM((kinds, group, m, size), F32),
            ],
        ),
        out_shape=jax.ShapeDtypeStruct((count, m, size), F32),
        compiler_params=params(40),
        cost_estimate=cost(kinds * count * m * size * size, 2 * size * size * kinds),
        name="near",
    )(slots, counts, types, before, low, high, after, incident, translations)


def back_kernel(phase_ref, waves_ref, basis_ref, partial_ref, t_ref, out_ref):
    group, m, size = partial_ref.shape
    chunks, _, width = waves_ref.shape
    total = partial_ref[...].reshape(group * m, size)
    for c in range(chunks):
        weighted = []
        for i in range(group):
            weighted.append(phase_ref[i, :, pl.ds(c * width, width)] * waves_ref[c])
        total = total + jnp.dot(
            jnp.concatenate(weighted, axis=0),
            basis_ref[pl.ds(c * width, width), :],
            preferred_element_type=F32,
        )
    source = total.astype(BF16)
    for i in range(group):
        out_ref[i] = lax.dot_general(
            source[i * m : (i + 1) * m], t_ref[i], LAST, preferred_element_type=F32
        ).astype(BF16)


def back(phases, waves, basis, partial, t_matrices, start, count):
    chunks, m, width = waves.shape
    size = basis.shape[1]
    total_rows = basis.shape[0]
    group = 2
    first = start // group
    return pl.pallas_call(
        back_kernel,
        grid=(count // group,),
        in_specs=[
            pl.BlockSpec((group, 1, total_rows), lambda p: (first + p, 0, 0)),
            pl.BlockSpec((chunks, m, width), lambda p: (0, 0, 0)),
            pl.BlockSpec((total_rows, size), lambda p: (0, 0)),
            pl.BlockSpec((group, m, size), lambda p: (first + p, 0, 0)),
            pl.BlockSpec((group, size, size), lambda p: (first + p, 0, 0)),
        ],
        out_specs=pl.BlockSpec((group, m, size), lambda p: (p, 0, 0)),
        out_shape=jax.ShapeDtypeStruct((count, m, size), BF16),
        compiler_params=params(32),
        cost_estimate=cost(
            count * m * size * (total_rows + size), 2 * size * (total_rows + count * size)
        ),
        name="back",
    )(phases[:, None, :], waves, basis, partial, t_matrices)


def add(*terms):
    total = terms[0].astype(F32)
    for term in terms[1:]:
        total = total + term.astype(F32)
    return total.astype(BF16)


def local(
    incident,
    t_matrices,
    translations,
    near_index,
    near_count,
    near_type,
    phases,
    wave_basis,
    grating_blocks,
):
    doms, blks = lax.axis_size("dom"), lax.axis_size("blk")
    devices = doms * blks
    x_count, z_count = doms // 2, min(4, blks)
    y_count = blks // z_count
    count, size, m = incident.shape
    reach = count // 2
    me = lax.axis_index(AXES)
    core = lax.axis_index("dom") % 2
    x = lax.axis_index("dom") // 2
    z = lax.axis_index("blk") // y_count
    y = lax.axis_index("blk") % y_count

    def flip(array, mask):
        return lax.ppermute(array, AXES, [(i, i ^ mask) for i in range(devices)])

    def mask_of(dx, dy):
        return dx * 2 * blks + dy

    core_mask = blks
    plane = [
        (dx, dy) for dx in range(x_count) for dy in range(y_count) if (dx, dy) != (0, 0)
    ]
    plane.sort(key=lambda pair: -(pair[0] > 0) - (pair[1] > 0))
    column = [d for d in (2, 3, 1) if d < z_count]

    def reduce_reflect_gather(send, keep):
        width = keep.shape[2]
        rows = m // 2 // x_count
        got = flip(send, core_mask)
        split = (z_count, y_count, x_count, rows, width)

        def shaped(array):
            return array.reshape(blks, x_count, rows, width).reshape(split)

        def part(array, at_x, at_y):
            return lax.dynamic_slice(
                array, (0, at_y, at_x, 0, 0), (z_count, 1, 1, rows, width)
            )[:, 0, 0]

        keep, got = shaped(keep), shaped(got)

        def summed(at_x, at_y):
            return add(part(keep, at_x, at_y), part(got, at_x, at_y))

        arrived = [flip(summed(x ^ dx, y ^ dy), mask_of(dx, dy)) for dx, dy in plane]
        plane_sum = add(part(keep, x, y), part(got, x, y), *arrived)

        def row(at_z):
            return lax.dynamic_slice_in_dim(plane_sum, at_z, 1, axis=0)[0]

        arrived = [flip(row(z ^ dz), dz * y_count) for dz in column]
        sums = row(z).astype(F32)
        for term in arrived:
            sums = sums + term.astype(F32)
        owned, order = grating_blocks.shape[:2]
        reflected = jnp.concatenate(
            [
                lax.dot_general(
                    sums[:, b * order : (b + 1) * order],
                    grating_blocks[b],
                    LAST,
                    precision=lax.Precision.HIGHEST,
                )
                for b in range(owned)
            ],
            axis=1,
        ).astype(BF16)

        stack = jnp.zeros((z_count, rows, width), BF16)
        stack = lax.dynamic_update_slice(stack, reflected[None], (z, 0, 0))
        for dz in column:
            stack = lax.dynamic_update_slice(
                stack, flip(reflected, dz * y_count)[None], (z ^ dz, 0, 0)
            )
        waves = jnp.zeros(split, BF16)
        for dx, dy in [(0, 0)] + plane:
            piece = stack if (dx, dy) == (0, 0) else flip(stack, mask_of(dx, dy))
            waves = lax.dynamic_update_slice(
                waves, piece[:, None, None], (0, y ^ dy, x ^ dx, 0, 0)
            )
        mine = waves.reshape(blks, m // 2, width)
        other = flip(mine, core_mask)
        first = jnp.where(core == 0, mine, other)
        second = jnp.where(core == 0, other, mine)
        return jnp.concatenate([first, second], axis=1)

    up = [(i, i + 1) for i in range(devices - 1)]
    down = [(j, i) for i, j in up]
    first_index = me * count
    slots = (near_index - first_index + reach).astype(jnp.int32)
    incident_t = jnp.swapaxes(incident, 1, 2)
    other_part = (1 - core).astype(jnp.int32).reshape(1)
    own_part = core.astype(jnp.int32).reshape(1)

    high = solve(incident_t, t_matrices, reach, reach)
    low = solve(incident_t, t_matrices, 0, reach)
    for sweep in range(ITERS):
        send = outward(other_part, low, high, wave_basis, phases, 2, blks)
        keep = outward(own_part, low, high, wave_basis, phases, 2, blks)
        before = lax.ppermute(high, AXES, up)
        after = lax.ppermute(low, AXES, down)
        waves = reduce_reflect_gather(send, keep)
        partial = near(
            slots, near_count, near_type, before, low, high, after, incident_t, translations
        )
        if sweep == ITERS - 1:
            coeffs = back(phases, waves, wave_basis, partial, t_matrices, 0, count)
            return jnp.swapaxes(coeffs, 1, 2)
        high = back(phases, waves, wave_basis, partial, t_matrices, reach, reach)
        low = back(phases, waves, wave_basis, partial, t_matrices, 0, reach)


def solution(mesh):
    placed = (
        P(("dom", "blk"), None, None),
        P(("dom", "blk"), None, None),
        P(),
        P(("dom", "blk"), None),
        P(("dom", "blk")),
        P(("dom", "blk"), None),
        P(("dom", "blk"), None),
        P(),
        P("blk", None, None),
    )
    return jax.shard_map(
        local, mesh=mesh, in_specs=placed, out_specs=P(("dom", "blk"), None, None), check_vma=False
    )
```

time: 341 us -> 175 us (0.51)
  the two profiles are of different devices: /device:TPU:0 before, /device:TPU:3 now
where the time goes in v1:
time: 175 us
  waiting for transfers between devices  66.2 us (38%)
  Pallas kernels  44.7 us (26%)
  starting transfers between devices  42 us (24%)
  local copies, waits for them, and re-layouts  14.5 us (8%)
  other arithmetic  5.96 us (3%)
    ppermute x28, waiting for transfers between devices, flip(): return lax.ppermute(array, AXES, [(i, i ^ mask) for i in range(devices)])  66.1 us
    ppermute x28, starting transfers between devices, flip(): return lax.ppermute(array, AXES, [(i, i ^ mask) for i in range(devices)])  25.2 us
    pallas_call x2, Pallas kernels, near(): pl.pallas_call(near_kernel, grid_spec=pltpu.PrefetchScalarGridSpec(num_sc...  15.5 us
    pallas_call x4, Pallas kernels, outward(): pl.pallas_call(outward_kernel, grid_spec=pltpu.PrefetchScalarGridSpec(num...  15.1 us
    pallas_call x3, Pallas kernels, back(): pl.pallas_call(back_kernel, grid=(count // group,), in_specs=[pl.BlockSpe...  11.4 us
    ppermute x2, starting transfers between devices, local(): after = lax.ppermute(low, AXES, down)  11.1 us
    unnamed x36, local copies, waits for them, and re-layouts  10.9 us
    ppermute x2, starting transfers between devices, local(): before = lax.ppermute(high, AXES, up)  5.62 us
  transfers between devices with their start and end apart: 32, of which 11 were waited for; matrix products, arithmetic and copies ran while one was open for 3% of the time, Pallas kernels for 13%

profile of v1, /device:TPU:3, one launch (start us, length us, event | category | flops | bytes accessed | tf_op | source)
XLA Modules:
  0.0 174.8 jit_solution(7044464655955093158)
XLA Ops:
  0.0 2.2 %copy-done = bf16[8,512,512]{2,1,0:T(8,128)(2,1)S(1)} copy-done((bf16[8,512,512]{2,1,0:T(8,128)(2,1)S(1)}, bf16[8,512,512]{2,1,0:T(8,128)(2,1)}, u32[]{:S(2)}) %copy-start) | copy-done | bytes 4194328
  2.2 1.4 copy-done.3
  3.6 1.3 solve.2.low_ref
  5.0 1.4 solve.3.high_ref
  6.3 0.9 copy-done.6
  7.2 1.1 copy-done.7
  8.4 4.6 %outward.5 = bf16[8,96,256]{2,1,0:T(8,128)(2,1)} custom-call(s32[1]{0:T(128)} %bitcast.4.part_ref, bf16[4,192,512]{2,1,0:T(8,128)(2,1)S(1)} %solve.2.low_ref, bf16[4,192,512]{2,1,0:T(8,128)(2,1)S(1)} %copy-done.7, bf16[2048,512]{1,0:T(8,128)(2,1)S(1)} %copy-done.2, bf16[8,2048]{1,0:T(8,128)(2,1)S(1)} %copy-done.10), custom_call_target="tpu_custom_call" | custom-call | flops 1610612736 | bytes 2883584 | tf_op jit(solution)/shard_map/outward/pallas_call | solution.py:69
  12.9 0.7 collective-permute-start
  13.6 1.1 copy-done.8
  14.8 3.5 %outward.4 = bf16[8,96,256]{2,1,0:T(8,128)(2,1)S(1)} custom-call(s32[1]{0:T(128)} %bitcast.1.part_ref, bf16[4,192,512]{2,1,0:T(8,128)(2,1)S(1)} %solve.2.low_ref, bf16[4,192,512]{2,1,0:T(8,128)(2,1)S(1)} %copy-done.8, bf16[2048,512]{1,0:T(8,128)(2,1)S(1)} %copy-done.2, bf16[8,2048]{1,0:T(8,128)(2,1)S(1)} %copy-done.10), custom_call_target="tpu_custom_call" | custom-call | flops 1610612736 | bytes 2883584 | tf_op jit(solution)/shard_map/outward/pallas_call | solution.py:69
  18.3 1.7 fusion.6
  20.0 1.2 collective-permute-start.1
  21.4 1.6 fusion.8
  22.9 1.3 collective-permute-start.3
  24.3 1.3 collective-permute-done.1
  25.6 2.5 %collective-permute-done.2 = bf16[4,48,256]{2,1,0:T(8,128)(2,1)} collective-permute-done((bf16[4,48,256]{2,1,0:T(8,128)(2,1)}, bf16[4,48,256]{2,1,0:T(8,128)(2,1)}, u32[]{:S(2)}, u32[]{:S(2)}) %collective-permute-start.2) | collective-permute-done | bytes 98336 | tf_op jit(solution)/shard_map/ppermute | solution.py:246
  28.1 1.1 fusion.5
  29.3 2.3 %collective-permute-start.4 = (bf16[48,256]{1,0:T(8,128)(2,1)S(1)}, bf16[48,256]{1,0:T(8,128)(2,1)S(1)}, u32[]{:S(2)}, u32[]{:S(2)}) collective-permute-start(bf16[48,256]{1,0:T(8,128)(2,1)S(1)} %get-tuple-element.16), channel_id=1, source_target_pairs={{0,4},{1,5},{2,6},{3,7},{4,0},{5,1},{6,2},{7,3},{8,12},{9,13},{10,... | collective-permute-start | bytes 73736 | tf_op jit(solution)/shard_map/ppermute | solution.py:246
  31.6 1.1 collective-permute-start.5
  32.9 2.2 %collective-permute-start.14 = (bf16[4,192,512]{2,1,0:T(8,128)(2,1)}, bf16[4,192,512]{2,1,0:T(8,128)(2,1)}, u32[]{:S(2)}, u32[]{:S(2)}) collective-permute-start(bf16[4,192,512]{2,1,0:T(8,128)(2,1)} %copy-done.6), channel_id=1, source_target_pairs={{0,1},{1,2},{2,3},{3,4},{4,5},{5,6},{6,7},{7,8},{8,9},{9,10},{10,1... | collective-permute-start | bytes 2359304 | tf_op jit(solution)/shard_map/ppermute | solution.py:332
  35.1 6.2 %collective-permute-start.15 = (bf16[4,192,512]{2,1,0:T(8,128)(2,1)S(1)}, bf16[4,192,512]{2,1,0:T(8,128)(2,1)}, u32[]{:S(2)}, u32[]{:S(2)}) collective-permute-start(bf16[4,192,512]{2,1,0:T(8,128)(2,1)S(1)} %solve.2.low_ref), channel_id=1, source_target_pairs={{1,0},{2,1},{3,2},{4,3},{5,4},{6,5},{7,6},{8,7},{9,8},{10,9},{11,1... | collective-permute-start | bytes 2359304 | tf_op jit(solution)/shard_map/ppermute | solution.py:333
  41.3 0.2 convolution_convert_fusion.2
  41.6 0.2 convolution_convert_fusion.3
  42.0 1.1 collective-permute-start.8
  43.1 1.4 collective-permute-start.9
  44.5 13.7 %collective-permute-done.7 = bf16[48,256]{1,0:T(8,128)(2,1)S(1)} collective-permute-done((bf16[48,256]{1,0:T(8,128)(2,1)S(1)}, bf16[48,256]{1,0:T(8,128)(2,1)S(1)}, u32[]{:S(2)}, u32[]{:S(2)}) %collective-permute-start.7) | collective-permute-done | bytes 24608 | tf_op jit(solution)/shard_map/ppermute | solution.py:246
  58.3 0.3 collective-permute-done.8
  58.6 2.1 %collective-permute-start.10 = (bf16[4,48,256]{2,1,0:T(8,128)(2,1)S(1)}, bf16[4,48,256]{2,1,0:T(8,128)(2,1)S(1)}, u32[]{:S(2)}, u32[]{:S(2)}) collective-permute-start(bf16[4,48,256]{2,1,0:T(8,128)(2,1)S(1)} %bitcast_dynamic-update-slice_fusion.11), channel_id=1, source_target_pairs={{0,17},{1,16},{2,19},{3,18},{4,21},{5,20},{6,23},{7,22},{8,25},{9,... | collective-permute-start | bytes 294920 | tf_op jit(solution)/shard_map/ppermute | solution.py:246
  60.7 0.6 collective-permute-start.12
  61.3 0.8 broadcast.10.clone
  62.1 0.6 bitcast_dynamic-update-slice_fusion.6
  62.8 0.4 collective-permute-done.10
  63.2 0.7 bitcast_dynamic-update-slice_fusion.5
  63.8 13.7 %collective-permute-done.11 = bf16[4,48,256]{2,1,0:T(8,128)(2,1)S(1)} collective-permute-done((bf16[4,48,256]{2,1,0:T(8,128)(2,1)S(1)}, bf16[4,48,256]{2,1,0:T(8,128)(2,1)S(1)}, u32[]{:S(2)}, u32[]{:S(2)}) %collective-permute-start.11) | collective-permute-done | bytes 98336 | tf_op jit(solution)/shard_map/ppermute | solution.py:246
  77.5 0.7 bitcast_dynamic-update-slice_fusion.4
  78.2 0.6 bitcast_dynamic-update-slice_fusion.3
  78.8 1.2 collective-permute-start.13
  80.1 1.4 copy-done.4
  81.5 1.1 copy-done.9
  82.7 1.6 copy-done.11
  84.3 8.6 %near.2.partial_ref = f32[8,192,512]{2,1,0:T(8,128)S(1)} custom-call(s32[8,6]{1,0:T(8,128)S(1)} %subtract_add_fusion.slot_ref, s32[8]{0:T(128)S(1)} %copy-done.14, s32[8,6]{1,0:T(8,128)S(1)} %copy-done.13, bf16[4,192,512]{2,1,0:T(8,128)(2,1)} %collective-permute-done.14.before_ref, bf16[4,192,512]{2,1,0:T(8,128)(2,1)S(1)} %solve.2.low_ref, ...), custom_call_target="tpu_custom_call" | custom-call | flops 3221225472 | bytes 2097152 | tf_op jit(solution)/shard_map/near/pallas_call | solution.py:143
  92.9 1.2 broadcast_select_fusion.3
  94.1 2.7 %back.4.high_ref = bf16[4,192,512]{2,1,0:T(8,128)(2,1)S(1)} custom-call(bf16[8,1,2048]{2,1,0:T(2,128)(2,1)S(1)} %copy.50.phase_ref, bf16[8,192,256]{2,1,0:T(8,128)(2,1)S(1)} %pad_maximum_fusion.waves_ref, bf16[2048,512]{1,0:T(8,128)(2,1)S(1)} %copy-done.2, f32[8,192,512]{2,1,0:T(8,128)S(1)} %near.2.partial_ref, bf16[8,512,512]{2,1,0:T(8,128)(2,1)S(1)} %copy-done.1), custom_call_target="tpu_custom_call" | custom-call | flops 2013265920 | bytes 4194304 | tf_op jit(solution)/shard_map/back/pallas_call | solution.py:195
  96.8 2.7 %back.3.low_ref = bf16[4,192,512]{2,1,0:T(8,128)(2,1)S(1)} custom-call(bf16[8,1,2048]{2,1,0:T(2,128)(2,1)S(1)} %copy.50.phase_ref, bf16[8,192,256]{2,1,0:T(8,128)(2,1)S(1)} %pad_maximum_fusion.waves_ref, bf16[2048,512]{1,0:T(8,128)(2,1)S(1)} %copy-done.2, f32[8,192,512]{2,1,0:T(8,128)S(1)} %near.2.partial_ref, bf16[8,512,512]{2,1,0:T(8,128)(2,1)S(1)} %copy-done.1), custom_call_target="tpu_custom_call" | custom-call | flops 2013265920 | bytes 4194304 | tf_op jit(solution)/shard_map/back/pallas_call | solution.py:195
  99.5 3.5 %outward.7 = bf16[8,96,256]{2,1,0:T(8,128)(2,1)S(1)} custom-call(s32[1]{0:T(128)} %bitcast.4.part_ref, bf16[4,192,512]{2,1,0:T(8,128)(2,1)S(1)} %back.3.low_ref, bf16[4,192,512]{2,1,0:T(8,128)(2,1)S(1)} %back.4.high_ref, bf16[2048,512]{1,0:T(8,128)(2,1)S(1)} %copy-done.2, bf16[8,2048]{1,0:T(8,128)(2,1)S(1)} %copy-done.10), custom_call_target="tpu_custom_call" | custom-call | flops 1610612736 | bytes 2883584 | tf_op jit(solution)/shard_map/outward/pallas_call | solution.py:69
  103.1 3.5 %outward.6 = bf16[8,96,256]{2,1,0:T(8,128)(2,1)S(1)} custom-call(s32[1]{0:T(128)} %bitcast.1.part_ref, bf16[4,192,512]{2,1,0:T(8,128)(2,1)S(1)} %back.3.low_ref, bf16[4,192,512]{2,1,0:T(8,128)(2,1)S(1)} %back.4.high_ref, bf16[2048,512]{1,0:T(8,128)(2,1)S(1)} %copy-done.2, bf16[8,2048]{1,0:T(8,128)(2,1)S(1)} %copy-done.10), custom_call_target="tpu_custom_call" | custom-call | flops 1610612736 | bytes 2883584 | tf_op jit(solution)/shard_map/outward/pallas_call | solution.py:69
  106.9 2.6 %collective-permute-start.19 = (bf16[4,48,256]{2,1,0:T(8,128)(2,1)S(1)}, bf16[4,48,256]{2,1,0:T(8,128)(2,1)S(1)}, u32[]{:S(2)}, u32[]{:S(2)}) collective-permute-start(bf16[4,48,256]{2,1,0:T(8,128)(2,1)S(1)} %fusion.11), channel_id=1, source_target_pairs={{0,16},{1,17},{2,18},{3,19},{4,20},{5,21},{6,22},{7,23},{8,24},{9,... | collective-permute-start | bytes 294920 | tf_op jit(solution)/shard_map/ppermute | solution.py:246
  109.5 2.2 %collective-permute-done.17 = bf16[4,48,256]{2,1,0:T(8,128)(2,1)S(1)} collective-permute-done((bf16[4,48,256]{2,1,0:T(8,128)(2,1)S(1)}, bf16[4,48,256]{2,1,0:T(8,128)(2,1)S(1)}, u32[]{:S(2)}, u32[]{:S(2)}) %collective-permute-start.17) | collective-permute-done | bytes 98336 | tf_op jit(solution)/shard_map/ppermute | solution.py:246
  111.7 0.7 collective-permute-done.18
  112.5 1.6 collective-permute-start.20
  114.1 1.2 collective-permute-start.21
  115.3 3.5 %collective-permute-start.30 = (bf16[4,192,512]{2,1,0:T(8,128)(2,1)S(1)}, bf16[4,192,512]{2,1,0:T(8,128)(2,1)S(1)}, u32[]{:S(2)}, u32[]{:S(2)}) collective-permute-start(bf16[4,192,512]{2,1,0:T(8,128)(2,1)S(1)} %back.4.high_ref), channel_id=1, source_target_pairs={{0,1},{1,2},{2,3},{3,4},{4,5},{5,6},{6,7},{7,8},{8,9},{9,10},{10,1... | collective-permute-start | bytes 2359304 | tf_op jit(solution)/shard_map/ppermute | solution.py:332
  118.8 5.0 %collective-permute-start.31 = (bf16[4,192,512]{2,1,0:T(8,128)(2,1)S(1)}, bf16[4,192,512]{2,1,0:T(8,128)(2,1)S(1)}, u32[]{:S(2)}, u32[]{:S(2)}) collective-permute-start(bf16[4,192,512]{2,1,0:T(8,128)(2,1)S(1)} %back.3.low_ref), channel_id=1, source_target_pairs={{1,0},{2,1},{3,2},{4,3},{5,4},{6,5},{7,6},{8,7},{9,8},{10,9},{11,1... | collective-permute-start | bytes 2359304 | tf_op jit(solution)/shard_map/ppermute | solution.py:333
  124.3 0.3 collective-permute-start.23
  124.6 1.2 collective-permute-start.24
  125.9 1.2 collective-permute-start.25
  127.1 13.3 %collective-permute-done.23 = bf16[48,256]{1,0:T(8,128)(2,1)S(1)} collective-permute-done((bf16[48,256]{1,0:T(8,128)(2,1)S(1)}, bf16[48,256]{1,0:T(8,128)(2,1)S(1)}, u32[]{:S(2)}, u32[]{:S(2)}) %collective-permute-start.23) | collective-permute-done | bytes 24608 | tf_op jit(solution)/shard_map/ppermute | solution.py:246
  140.4 2.3 %collective-permute-start.26 = (bf16[4,48,256]{2,1,0:T(8,128)(2,1)S(1)}, bf16[4,48,256]{2,1,0:T(8,128)(2,1)S(1)}, u32[]{:S(2)}, u32[]{:S(2)}) collective-permute-start(bf16[4,48,256]{2,1,0:T(8,128)(2,1)S(1)} %bitcast_dynamic-update-slice_fusion.8), channel_id=1, source_target_pairs={{0,17},{1,16},{2,19},{3,18},{4,21},{5,20},{6,23},{7,22},{8,25},{9,... | collective-permute-start | bytes 294920 | tf_op jit(solution)/shard_map/ppermute | solution.py:246
  142.7 0.3 collective-permute-start.27
  143.2 1.8 %collective-permute-done.26 = bf16[4,48,256]{2,1,0:T(8,128)(2,1)S(1)} collective-permute-done((bf16[4,48,256]{2,1,0:T(8,128)(2,1)S(1)}, bf16[4,48,256]{2,1,0:T(8,128)(2,1)S(1)}, u32[]{:S(2)}, u32[]{:S(2)}) %collective-permute-start.26) | collective-permute-done | bytes 98336 | tf_op jit(solution)/shard_map/ppermute | solution.py:246
  145.0 16.0 %collective-permute-done.27 = bf16[4,48,256]{2,1,0:T(8,128)(2,1)S(1)} collective-permute-done((bf16[4,48,256]{2,1,0:T(8,128)(2,1)S(1)}, bf16[4,48,256]{2,1,0:T(8,128)(2,1)S(1)}, u32[]{:S(2)}, u32[]{:S(2)}) %collective-permute-start.27) | collective-permute-done | bytes 98336 | tf_op jit(solution)/shard_map/ppermute | solution.py:246
  161.1 0.6 collective-permute-start.29
  161.7 6.9 %near.3.partial_ref = f32[8,192,512]{2,1,0:T(8,128)S(1)} custom-call(s32[8,6]{1,0:T(8,128)S(1)} %subtract_add_fusion.slot_ref, s32[8]{0:T(128)S(1)} %copy-done.14, s32[8,6]{1,0:T(8,128)S(1)} %copy-done.13, bf16[4,192,512]{2,1,0:T(8,128)(2,1)S(1)} %collective-permute-done.30.before_ref, bf16[4,192,512]{2,1,0:T(8,128)(2,1)S(1)} %back.3.low_ref, ...), custom_call_target="tpu_custom_call" | custom-call | flops 3221225472 | bytes 2097152 | tf_op jit(solution)/shard_map/near/pallas_call | solution.py:143
  168.7 6.0 %back.5 = bf16[8,192,512]{2,1,0:T(8,128)(2,1)} custom-call(bf16[8,1,2048]{2,1,0:T(2,128)(2,1)S(1)} %copy.50.phase_ref, bf16[8,192,256]{2,1,0:T(8,128)(2,1)S(1)} %pad_maximum_fusion.1.waves_ref, bf16[2048,512]{1,0:T(8,128)(2,1)S(1)} %copy-done.2, f32[8,192,512]{2,1,0:T(8,128)S(1)} %near.3.partial_ref, bf16[8,512,512]{2,1,0:T(8,128)(2,1)S(1)} %copy-done.1), custom_call_target="tpu_custom_call" | custom-call | flops 4026531840 | bytes 6291456 | tf_op jit(solution)/shard_map/back/pallas_call | solution.py:195
  (89 shorter events, 2.0 us)
Async XLA Ops:
  0.0 2.2 %copy-start = (bf16[8,512,512]{2,1,0:T(8,128)(2,1)S(1)}, bf16[8,512,512]{2,1,0:T(8,128)(2,1)}, u32[]{:S(2)}) copy-start(bf16[8,512,512]{2,1,0:T(8,128)(2,1)} %t_ref.9) | copy-start | bytes 12582916
  2.2 1.4 copy-start.3
  4.9 2.3 %copy-start.2 = (bf16[2048,512]{1,0:T(8,128)(2,1)S(1)}, bf16[2048,512]{1,0:T(8,128)(2,1)}, u32[]{:S(2)}) copy-start(bf16[2048,512]{1,0:T(8,128)(2,1)} %basis_ref.13) | copy-start | bytes 6291460
  5.0 2.3 %copy-start.10 = (bf16[8,2048]{1,0:T(8,128)(2,1)S(1)}, bf16[8,2048]{1,0:T(8,128)(2,1)}, u32[]{:S(2)}) copy-start(bf16[8,2048]{1,0:T(8,128)(2,1)} %phase_ref.7) | copy-start | bytes 98308
  6.3 0.9 copy-start.6
  7.2 1.1 copy-start.7
  12.9 5.3 %collective-permute-start = (bf16[8,96,256]{2,1,0:T(8,128)(2,1)}, bf16[8,96,256]{2,1,0:T(8,128)(2,1)}, u32[]{:S(2)}, u32[]{:S(2)}) collective-permute-start(bf16[8,96,256]{2,1,0:T(8,128)(2,1)} %outward.5), channel_id=1, source_target_pairs={{0,8},{1,9},{2,10},{3,11},{4,12},{5,13},{6,14},{7,15},{8,0},{9,1},... | collective-permute-start | bytes 1179656 | tf_op jit(solution)/shard_map/ppermute | solution.py:246
  13.6 1.1 copy-start.8
  18.3 23.1 %copy-start.15 = (f32[2,128,128]{2,1,0:T(8,128)S(1)}, f32[2,128,128]{2,1,0:T(8,128)}, u32[]{:S(2)}) copy-start(f32[2,128,128]{2,1,0:T(8,128)} %param.17) | copy-start | bytes 393220
  20.0 60.0 %copy-start.17 = (s32[8,6]{1,0:T(8,128)S(1)}, s32[8,6]{1,0:T(8,128)}, u32[]{:S(2)}) copy-start(s32[8,6]{1,0:T(8,128)} %param.12) | copy-start | bytes 580
  20.0 60.1 %copy-start.13 = (s32[8,6]{1,0:T(8,128)S(1)}, s32[8,6]{1,0:T(8,128)}, u32[]{:S(2)}) copy-start(s32[8,6]{1,0:T(8,128)} %type_ref.3) | copy-start | bytes 580
  20.0 60.1 %copy-start.14 = (s32[8]{0:T(128)S(1)}, s32[8]{0:T(128)}, u32[]{:S(2)}) copy-start(s32[8]{0:T(128)} %count_ref.3) | copy-start | bytes 100
  20.0 5.6 %collective-permute-start.1 = (bf16[4,48,256]{2,1,0:T(8,128)(2,1)}, bf16[4,48,256]{2,1,0:T(8,128)(2,1)S(1)}, u32[]{:S(2)}, u32[]{:S(2)}) collective-permute-start(bf16[4,48,256]{2,1,0:T(8,128)(2,1)} %get-tuple-element.11), channel_id=1, source_target_pairs={{0,17},{1,16},{2,19},{3,18},{4,21},{5,20},{6,23},{7,22},{8,25},{9,... | collective-permute-start | bytes 294920 | tf_op jit(solution)/shard_map/ppermute | solution.py:246
  21.2 6.9 %collective-permute-start.2 = (bf16[4,48,256]{2,1,0:T(8,128)(2,1)}, bf16[4,48,256]{2,1,0:T(8,128)(2,1)}, u32[]{:S(2)}, u32[]{:S(2)}) collective-permute-start(bf16[4,48,256]{2,1,0:T(8,128)(2,1)} %get-tuple-element.12), channel_id=1, source_target_pairs={{0,1},{1,0},{2,3},{3,2},{4,5},{5,4},{6,7},{7,6},{8,9},{9,8},{10,11... | collective-permute-start | bytes 294920 | tf_op jit(solution)/shard_map/ppermute | solution.py:246
  22.9 5.2 %collective-permute-start.3 = (bf16[4,48,256]{2,1,0:T(8,128)(2,1)}, bf16[4,48,256]{2,1,0:T(8,128)(2,1)}, u32[]{:S(2)}, u32[]{:S(2)}) collective-permute-start(bf16[4,48,256]{2,1,0:T(8,128)(2,1)} %fusion.8), channel_id=1, source_target_pairs={{0,16},{1,17},{2,18},{3,19},{4,20},{5,21},{6,22},{7,23},{8,24},{9,... | collective-permute-start | bytes 294920 | tf_op jit(solution)/shard_map/ppermute | solution.py:246
  25.6 2.5 %copy-start.16 = (bf16[4,48,256]{2,1,0:T(8,128)(2,1)}, bf16[4,48,256]{2,1,0:T(8,128)(2,1)S(1)}, u32[]{:S(2)}) copy-start(bf16[4,48,256]{2,1,0:T(8,128)(2,1)S(1)} %collective-permute-done.1) | copy-start | bytes 294916
  29.3 12.0 %collective-permute-start.4 = (bf16[48,256]{1,0:T(8,128)(2,1)S(1)}, bf16[48,256]{1,0:T(8,128)(2,1)S(1)}, u32[]{:S(2)}, u32[]{:S(2)}) collective-permute-start(bf16[48,256]{1,0:T(8,128)(2,1)S(1)} %get-tuple-element.16), channel_id=1, source_target_pairs={{0,4},{1,5},{2,6},{3,7},{4,0},{5,1},{6,2},{7,3},{8,12},{9,13},{10,... | collective-permute-start | bytes 73736 | tf_op jit(solution)/shard_map/ppermute | solution.py:246
  31.6 9.7 %collective-permute-start.5 = (bf16[48,256]{1,0:T(8,128)(2,1)S(1)}, bf16[48,256]{1,0:T(8,128)(2,1)S(1)}, u32[]{:S(2)}, u32[]{:S(2)}) collective-permute-start(bf16[48,256]{1,0:T(8,128)(2,1)S(1)} %get-tuple-element.18), channel_id=1, source_target_pairs={{0,6},{1,7},{2,4},{3,5},{4,2},{5,3},{6,0},{7,1},{8,14},{9,15},{10,... | collective-permute-start | bytes 73736 | tf_op jit(solution)/shard_map/ppermute | solution.py:246
  32.7 8.6 %collective-permute-start.6 = (bf16[48,256]{1,0:T(8,128)(2,1)S(1)}, bf16[48,256]{1,0:T(8,128)(2,1)S(1)}, u32[]{:S(2)}, u32[]{:S(2)}) collective-permute-start(bf16[48,256]{1,0:T(8,128)(2,1)S(1)} %get-tuple-element.17), channel_id=1, source_target_pairs={{0,2},{1,3},{2,0},{3,1},{4,6},{5,7},{6,4},{7,5},{8,10},{9,11},{10,... | collective-permute-start | bytes 73736 | tf_op jit(solution)/shard_map/ppermute | solution.py:246
  32.9 47.2 %collective-permute-start.14 = (bf16[4,192,512]{2,1,0:T(8,128)(2,1)}, bf16[4,192,512]{2,1,0:T(8,128)(2,1)}, u32[]{:S(2)}, u32[]{:S(2)}) collective-permute-start(bf16[4,192,512]{2,1,0:T(8,128)(2,1)} %copy-done.6), channel_id=1, source_target_pairs={{0,1},{1,2},{2,3},{3,4},{4,5},{5,6},{6,7},{7,8},{8,9},{9,10},{10,1... | collective-permute-start | bytes 2359304 | tf_op jit(solution)/shard_map/ppermute | solution.py:332
  35.1 45.0 %collective-permute-start.15 = (bf16[4,192,512]{2,1,0:T(8,128)(2,1)S(1)}, bf16[4,192,512]{2,1,0:T(8,128)(2,1)}, u32[]{:S(2)}, u32[]{:S(2)}) collective-permute-start(bf16[4,192,512]{2,1,0:T(8,128)(2,1)S(1)} %solve.2.low_ref), channel_id=1, source_target_pairs={{1,0},{2,1},{3,2},{4,3},{5,4},{6,5},{7,6},{8,7},{9,8},{10,9},{11,1... | collective-permute-start | bytes 2359304 | tf_op jit(solution)/shard_map/ppermute | solution.py:333
  41.8 16.5 %collective-permute-start.7 = (bf16[48,256]{1,0:T(8,128)(2,1)S(1)}, bf16[48,256]{1,0:T(8,128)(2,1)S(1)}, u32[]{:S(2)}, u32[]{:S(2)}) collective-permute-start(bf16[48,256]{1,0:T(8,128)(2,1)S(1)} %pad_maximum_fusion.2), channel_id=1, source_target_pairs={{0,4},{1,5},{2,6},{3,7},{4,0},{5,1},{6,2},{7,3},{8,12},{9,13},{10,... | collective-permute-start | bytes 73736 | tf_op jit(solution)/shard_map/ppermute | solution.py:246
  42.0 16.6 %collective-permute-start.8 = (bf16[48,256]{1,0:T(8,128)(2,1)S(1)}, bf16[48,256]{1,0:T(8,128)(2,1)S(1)}, u32[]{:S(2)}, u32[]{:S(2)}) collective-permute-start(bf16[48,256]{1,0:T(8,128)(2,1)S(1)} %pad_maximum_fusion.2), channel_id=1, source_target_pairs={{0,6},{1,7},{2,4},{3,5},{4,2},{5,3},{6,0},{7,1},{8,14},{9,15},{10,... | collective-permute-start | bytes 73736 | tf_op jit(solution)/shard_map/ppermute | solution.py:246
  43.1 15.5 %collective-permute-start.9 = (bf16[48,256]{1,0:T(8,128)(2,1)S(1)}, bf16[48,256]{1,0:T(8,128)(2,1)S(1)}, u32[]{:S(2)}, u32[]{:S(2)}) collective-permute-start(bf16[48,256]{1,0:T(8,128)(2,1)S(1)} %pad_maximum_fusion.2), channel_id=1, source_target_pairs={{0,2},{1,3},{2,0},{3,1},{4,6},{5,7},{6,4},{7,5},{8,10},{9,11},{10,... | collective-permute-start | bytes 73736 | tf_op jit(solution)/shard_map/ppermute | solution.py:246
  58.6 4.5 %collective-permute-start.10 = (bf16[4,48,256]{2,1,0:T(8,128)(2,1)S(1)}, bf16[4,48,256]{2,1,0:T(8,128)(2,1)S(1)}, u32[]{:S(2)}, u32[]{:S(2)}) collective-permute-start(bf16[4,48,256]{2,1,0:T(8,128)(2,1)S(1)} %bitcast_dynamic-update-slice_fusion.11), channel_id=1, source_target_pairs={{0,17},{1,16},{2,19},{3,18},{4,21},{5,20},{6,23},{7,22},{8,25},{9,... | collective-permute-start | bytes 294920 | tf_op jit(solution)/shard_map/ppermute | solution.py:246
  60.7 16.8 %collective-permute-start.11 = (bf16[4,48,256]{2,1,0:T(8,128)(2,1)S(1)}, bf16[4,48,256]{2,1,0:T(8,128)(2,1)S(1)}, u32[]{:S(2)}, u32[]{:S(2)}) collective-permute-start(bf16[4,48,256]{2,1,0:T(8,128)(2,1)S(1)} %bitcast_dynamic-update-slice_fusion.11), channel_id=1, source_target_pairs={{0,1},{1,0},{2,3},{3,2},{4,5},{5,4},{6,7},{7,6},{8,9},{9,8},{10,11... | collective-permute-start | bytes 294920 | tf_op jit(solution)/shard_map/ppermute | solution.py:246
  60.7 17.5 %collective-permute-start.12 = (bf16[4,48,256]{2,1,0:T(8,128)(2,1)S(1)}, bf16[4,48,256]{2,1,0:T(8,128)(2,1)S(1)}, u32[]{:S(2)}, u32[]{:S(2)}) collective-permute-start(bf16[4,48,256]{2,1,0:T(8,128)(2,1)S(1)} %bitcast_dynamic-update-slice_fusion.11), channel_id=1, source_target_pairs={{0,16},{1,17},{2,18},{3,19},{4,20},{5,21},{6,22},{7,23},{8,24},{9,... | collective-permute-start | bytes 294920 | tf_op jit(solution)/shard_map/ppermute | solution.py:246
  78.8 14.0 %collective-permute-start.13 = (bf16[8,96,256]{2,1,0:T(8,128)(2,1)}, bf16[8,96,256]{2,1,0:T(8,128)(2,1)}, u32[]{:S(2)}, u32[]{:S(2)}) collective-permute-start(bf16[8,96,256]{2,1,0:T(8,128)(2,1)} %bitcast.29), channel_id=1, source_target_pairs={{0,8},{1,9},{2,10},{3,11},{4,12},{5,13},{6,14},{7,15},{8,0},{9,1},... | collective-permute-start | bytes 1179656 | tf_op jit(solution)/shard_map/ppermute | solution.py:246
  80.1 1.4 copy-start.4
  81.5 1.1 copy-start.9
  82.7 1.6 copy-start.11
  84.3 9.9 %copy-start.1 = (bf16[8,512,512]{2,1,0:T(8,128)(2,1)S(1)}, bf16[8,512,512]{2,1,0:T(8,128)(2,1)}, u32[]{:S(2)}) copy-start(bf16[8,512,512]{2,1,0:T(8,128)(2,1)} %t_ref.9) | copy-start | bytes 12582916
  103.0 3.6 %collective-permute-start.16 = (bf16[8,96,256]{2,1,0:T(8,128)(2,1)S(1)}, bf16[8,96,256]{2,1,0:T(8,128)(2,1)S(1)}, u32[]{:S(2)}, u32[]{:S(2)}) collective-permute-start(bf16[8,96,256]{2,1,0:T(8,128)(2,1)S(1)} %outward.7), channel_id=1, source_target_pairs={{0,8},{1,9},{2,10},{3,11},{4,12},{5,13},{6,14},{7,15},{8,0},{9,1},... | collective-permute-start | bytes 1179656 | tf_op jit(solution)/shard_map/ppermute | solution.py:246
  103.1 58.6 %copy-start.12 = (bf16[4,512,512]{2,1,0:T(8,128)(2,1)S(1)}, bf16[4,512,512]{2,1,0:T(8,128)(2,1)}, u32[]{:S(2)}) copy-start(bf16[4,512,512]{2,1,0:T(8,128)(2,1)} %translations_ref.3) | copy-start | bytes 6291460
  106.7 54.9 %copy-start.5 = (bf16[8,512,192]{1,2,0:T(8,128)(2,1)S(1)}, bf16[8,512,192]{1,2,0:T(8,128)(2,1)}, u32[]{:S(2)}) copy-start(bf16[8,512,192]{1,2,0:T(8,128)(2,1)} %param.9) | copy-start | bytes 4718596
  106.8 4.9 %collective-permute-start.17 = (bf16[4,48,256]{2,1,0:T(8,128)(2,1)S(1)}, bf16[4,48,256]{2,1,0:T(8,128)(2,1)S(1)}, u32[]{:S(2)}, u32[]{:S(2)}) collective-permute-start(bf16[4,48,256]{2,1,0:T(8,128)(2,1)S(1)} %get-tuple-element.7), channel_id=1, source_target_pairs={{0,17},{1,16},{2,19},{3,18},{4,21},{5,20},{6,23},{7,22},{8,25},{9,... | collective-permute-start | bytes 294920 | tf_op jit(solution)/shard_map/ppermute | solution.py:246
  106.8 5.6 %collective-permute-start.18 = (bf16[4,48,256]{2,1,0:T(8,128)(2,1)S(1)}, bf16[4,48,256]{2,1,0:T(8,128)(2,1)S(1)}, u32[]{:S(2)}, u32[]{:S(2)}) collective-permute-start(bf16[4,48,256]{2,1,0:T(8,128)(2,1)S(1)} %get-tuple-element.8), channel_id=1, source_target_pairs={{0,1},{1,0},{2,3},{3,2},{4,5},{5,4},{6,7},{7,6},{8,9},{9,8},{10,11... | collective-permute-start | bytes 294920 | tf_op jit(solution)/shard_map/ppermute | solution.py:246
  106.9 5.5 %collective-permute-start.19 = (bf16[4,48,256]{2,1,0:T(8,128)(2,1)S(1)}, bf16[4,48,256]{2,1,0:T(8,128)(2,1)S(1)}, u32[]{:S(2)}, u32[]{:S(2)}) collective-permute-start(bf16[4,48,256]{2,1,0:T(8,128)(2,1)S(1)} %fusion.11), channel_id=1, source_target_pairs={{0,16},{1,17},{2,18},{3,19},{4,20},{5,21},{6,22},{7,23},{8,24},{9,... | collective-permute-start | bytes 294920 | tf_op jit(solution)/shard_map/ppermute | solution.py:246
  112.5 11.3 %collective-permute-start.20 = (bf16[48,256]{1,0:T(8,128)(2,1)S(1)}, bf16[48,256]{1,0:T(8,128)(2,1)S(1)}, u32[]{:S(2)}, u32[]{:S(2)}) collective-permute-start(bf16[48,256]{1,0:T(8,128)(2,1)S(1)} %get-tuple-element.13), channel_id=1, source_target_pairs={{0,4},{1,5},{2,6},{3,7},{4,0},{5,1},{6,2},{7,3},{8,12},{9,13},{10,... | collective-permute-start | bytes 73736 | tf_op jit(solution)/shard_map/ppermute | solution.py:246
  114.1 9.7 %collective-permute-start.21 = (bf16[48,256]{1,0:T(8,128)(2,1)S(1)}, bf16[48,256]{1,0:T(8,128)(2,1)S(1)}, u32[]{:S(2)}, u32[]{:S(2)}) collective-permute-start(bf16[48,256]{1,0:T(8,128)(2,1)S(1)} %get-tuple-element.15), channel_id=1, source_target_pairs={{0,6},{1,7},{2,4},{3,5},{4,2},{5,3},{6,0},{7,1},{8,14},{9,15},{10,... | collective-permute-start | bytes 73736 | tf_op jit(solution)/shard_map/ppermute | solution.py:246
  115.3 8.5 %collective-permute-start.22 = (bf16[48,256]{1,0:T(8,128)(2,1)S(1)}, bf16[48,256]{1,0:T(8,128)(2,1)S(1)}, u32[]{:S(2)}, u32[]{:S(2)}) collective-permute-start(bf16[48,256]{1,0:T(8,128)(2,1)S(1)} %get-tuple-element.14), channel_id=1, source_target_pairs={{0,2},{1,3},{2,0},{3,1},{4,6},{5,7},{6,4},{7,5},{8,10},{9,11},{10,... | collective-permute-start | bytes 73736 | tf_op jit(solution)/shard_map/ppermute | solution.py:246
  115.3 46.3 %collective-permute-start.30 = (bf16[4,192,512]{2,1,0:T(8,128)(2,1)S(1)}, bf16[4,192,512]{2,1,0:T(8,128)(2,1)S(1)}, u32[]{:S(2)}, u32[]{:S(2)}) collective-permute-start(bf16[4,192,512]{2,1,0:T(8,128)(2,1)S(1)} %back.4.high_ref), channel_id=1, source_target_pairs={{0,1},{1,2},{2,3},{3,4},{4,5},{5,6},{6,7},{7,8},{8,9},{9,10},{10,1... | collective-permute-start | bytes 2359304 | tf_op jit(solution)/shard_map/ppermute | solution.py:332
  118.8 42.8 %collective-permute-start.31 = (bf16[4,192,512]{2,1,0:T(8,128)(2,1)S(1)}, bf16[4,192,512]{2,1,0:T(8,128)(2,1)S(1)}, u32[]{:S(2)}, u32[]{:S(2)}) collective-permute-start(bf16[4,192,512]{2,1,0:T(8,128)(2,1)S(1)} %back.3.low_ref), channel_id=1, source_target_pairs={{1,0},{2,1},{3,2},{4,3},{5,4},{6,5},{7,6},{8,7},{9,8},{10,9},{11,1... | collective-permute-start | bytes 2359304 | tf_op jit(solution)/shard_map/ppermute | solution.py:333
  124.3 16.1 %collective-permute-start.23 = (bf16[48,256]{1,0:T(8,128)(2,1)S(1)}, bf16[48,256]{1,0:T(8,128)(2,1)S(1)}, u32[]{:S(2)}, u32[]{:S(2)}) collective-permute-start(bf16[48,256]{1,0:T(8,128)(2,1)S(1)} %pad_maximum_fusion.3), channel_id=1, source_target_pairs={{0,4},{1,5},{2,6},{3,7},{4,0},{5,1},{6,2},{7,3},{8,12},{9,13},{10,... | collective-permute-start | bytes 73736 | tf_op jit(solution)/shard_map/ppermute | solution.py:246
  124.6 15.8 %collective-permute-start.24 = (bf16[48,256]{1,0:T(8,128)(2,1)S(1)}, bf16[48,256]{1,0:T(8,128)(2,1)S(1)}, u32[]{:S(2)}, u32[]{:S(2)}) collective-permute-start(bf16[48,256]{1,0:T(8,128)(2,1)S(1)} %pad_maximum_fusion.3), channel_id=1, source_target_pairs={{0,6},{1,7},{2,4},{3,5},{4,2},{5,3},{6,0},{7,1},{8,14},{9,15},{10,... | collective-permute-start | bytes 73736 | tf_op jit(solution)/shard_map/ppermute | solution.py:246
  125.9 14.5 %collective-permute-start.25 = (bf16[48,256]{1,0:T(8,128)(2,1)S(1)}, bf16[48,256]{1,0:T(8,128)(2,1)S(1)}, u32[]{:S(2)}, u32[]{:S(2)}) collective-permute-start(bf16[48,256]{1,0:T(8,128)(2,1)S(1)} %pad_maximum_fusion.3), channel_id=1, source_target_pairs={{0,2},{1,3},{2,0},{3,1},{4,6},{5,7},{6,4},{7,5},{8,10},{9,11},{10,... | collective-permute-start | bytes 73736 | tf_op jit(solution)/shard_map/ppermute | solution.py:246
  140.4 4.5 %collective-permute-start.26 = (bf16[4,48,256]{2,1,0:T(8,128)(2,1)S(1)}, bf16[4,48,256]{2,1,0:T(8,128)(2,1)S(1)}, u32[]{:S(2)}, u32[]{:S(2)}) collective-permute-start(bf16[4,48,256]{2,1,0:T(8,128)(2,1)S(1)} %bitcast_dynamic-update-slice_fusion.8), channel_id=1, source_target_pairs={{0,17},{1,16},{2,19},{3,18},{4,21},{5,20},{6,23},{7,22},{8,25},{9,... | collective-permute-start | bytes 294920 | tf_op jit(solution)/shard_map/ppermute | solution.py:246
  142.7 18.3 %collective-permute-start.27 = (bf16[4,48,256]{2,1,0:T(8,128)(2,1)S(1)}, bf16[4,48,256]{2,1,0:T(8,128)(2,1)S(1)}, u32[]{:S(2)}, u32[]{:S(2)}) collective-permute-start(bf16[4,48,256]{2,1,0:T(8,128)(2,1)S(1)} %bitcast_dynamic-update-slice_fusion.8), channel_id=1, source_target_pairs={{0,1},{1,0},{2,3},{3,2},{4,5},{5,4},{6,7},{7,6},{8,9},{9,8},{10,11... | collective-permute-start | bytes 294920 | tf_op jit(solution)/shard_map/ppermute | solution.py:246
  143.0 18.0 %collective-permute-start.28 = (bf16[4,48,256]{2,1,0:T(8,128)(2,1)S(1)}, bf16[4,48,256]{2,1,0:T(8,128)(2,1)S(1)}, u32[]{:S(2)}, u32[]{:S(2)}) collective-permute-start(bf16[4,48,256]{2,1,0:T(8,128)(2,1)S(1)} %bitcast_dynamic-update-slice_fusion.8), channel_id=1, source_target_pairs={{0,16},{1,17},{2,18},{3,19},{4,20},{5,21},{6,22},{7,23},{8,24},{9,... | collective-permute-start | bytes 294920 | tf_op jit(solution)/shard_map/ppermute | solution.py:246
  161.1 7.5 %collective-permute-start.29 = (bf16[8,96,256]{2,1,0:T(8,128)(2,1)S(1)}, bf16[8,96,256]{2,1,0:T(8,128)(2,1)S(1)}, u32[]{:S(2)}, u32[]{:S(2)}) collective-permute-start(bf16[8,96,256]{2,1,0:T(8,128)(2,1)S(1)} %bitcast.148), channel_id=1, source_target_pairs={{0,8},{1,9},{2,10},{3,11},{4,12},{5,13},{6,14},{7,15},{8,0},{9,1},... | collective-permute-start | bytes 1179656 | tf_op jit(solution)/shard_map/ppermute | solution.py:246

commit v2 on v1

v2 whole, which is shorter than its diff:
```python
import jax
import jax.numpy as jnp
from jax import lax
from jax.experimental import pallas as pl
from jax.experimental.pallas import tpu as pltpu
from jax.sharding import PartitionSpec as P

ITERS = 2
AXES = ("dom", "blk")
F32 = jnp.float32
BF16 = jnp.bfloat16
LAST = (((1,), (1,)), ((), ()))
MIB = 1 << 20


def params(mib):
    return pltpu.CompilerParams(vmem_limit_bytes=mib * MIB)


def cost(macs, moved):
    return pl.CostEstimate(flops=1, bytes_accessed=1, transcendentals=0)


def solve_kernel(first_ref, source_ref, t_ref, out_ref, sources, matrices, arrived):
    count = out_ref.shape[0]
    copies = []
    for p in range(count):
        at = first_ref[0] * count + p
        pair = (
            pltpu.make_async_copy(source_ref.at[at], sources.at[p], arrived.at[2 * p]),
            pltpu.make_async_copy(t_ref.at[at], matrices.at[p], arrived.at[2 * p + 1]),
        )
        for copy in pair:
            copy.start()
        copies.append(pair)
    for p in range(count):
        for copy in copies[p]:
            copy.wait()
        out_ref[p] = lax.dot_general(
            sources[p], matrices[p], LAST, preferred_element_type=F32
        ).astype(BF16)


def solve(first, source, t_matrices, count):
    m, size = source.shape[1:]
    return pl.pallas_call(
        solve_kernel,
        grid_spec=pltpu.PrefetchScalarGridSpec(
            num_scalar_prefetch=1,
            grid=(1,),
            in_specs=[pl.BlockSpec(memory_space=pl.ANY)] * 2,
            out_specs=pl.BlockSpec((count, m, size), lambda p, first: (0, 0, 0)),
            scratch_shapes=[
                pltpu.VMEM((count, m, size), BF16),
                pltpu.VMEM((count, size, size), BF16),
                pltpu.SemaphoreType.DMA((2 * count,)),
            ],
        ),
        out_shape=jax.ShapeDtypeStruct((count, m, size), BF16),
        compiler_params=params(16),
        cost_estimate=cost(count * m * size * size, 2 * count * size * (2 * m + size)),
        name="solve",
    )(first, source, t_matrices)


def outward_kernel(part_ref, one_ref, two_ref, basis_ref, phase_ref, out_ref):
    half, rows, size = one_ref.shape
    chunks, _, chunk = out_ref.shape
    width = basis_ref.shape[0]
    total = jnp.zeros((rows, width), F32)
    for index, ref in ((0, one_ref), (half, two_ref)):
        spread = lax.dot_general(
            ref[...].reshape(half * rows, size),
            basis_ref[...],
            LAST,
            preferred_element_type=F32,
        )
        for p in range(half):
            phase = phase_ref[index + p, :].astype(F32)[None, :]
            total = total + phase * spread[p * rows : (p + 1) * rows]
    total = total.astype(BF16)
    for c in range(chunks):
        out_ref[c] = total[:, c * chunk : (c + 1) * chunk]


def outward(part, one, two, basis, phases, parts, chunks):
    half, m, size = one.shape
    total_rows = basis.shape[0]
    chunk = total_rows // chunks
    steps = 2
    width = total_rows // steps
    rows = m // parts
    return pl.pallas_call(
        outward_kernel,
        grid_spec=pltpu.PrefetchScalarGridSpec(
            num_scalar_prefetch=1,
            grid=(steps,),
            in_specs=[
                pl.BlockSpec((half, rows, size), lambda g, part: (0, part[0], 0)),
                pl.BlockSpec((half, rows, size), lambda g, part: (0, part[0], 0)),
                pl.BlockSpec((width, size), lambda g, part: (g, 0)),
                pl.BlockSpec((2 * half, width), lambda g, part: (0, g)),
            ],
            out_specs=pl.BlockSpec((chunks // steps, rows, chunk), lambda g, part: (g, 0, 0)),
        ),
        out_shape=jax.ShapeDtypeStruct((chunks, rows, chunk), BF16),
        compiler_params=params(24),
        cost_estimate=cost(
            2 * half * rows * size * total_rows, 2 * size * (total_rows + 2 * half * rows)
        ),
        name="outward",
    )(part, one, two, basis, phases)


def split_kernel(place_ref, offsets, levels, keep_ref, got_ref, *out_refs):
    across = keep_ref.shape[0] // levels
    for (dx, dy), out_ref in zip(offsets, out_refs):
        x, y = place_ref[0] ^ dx, place_ref[1] ^ dy
        for level in range(levels):
            chunk = level * across + y
            out_ref[level] = (
                keep_ref[chunk, x].astype(F32) + got_ref[chunk, x].astype(F32)
            ).astype(BF16)


def split(place, offsets, levels, keep, got):
    _, _, rows, width = keep.shape

    def body(place_ref, *refs):
        split_kernel(place_ref, offsets, levels, *refs)

    piece = jax.ShapeDtypeStruct((levels, rows, width), BF16)
    return pl.pallas_call(
        body,
        grid_spec=pltpu.PrefetchScalarGridSpec(
            num_scalar_prefetch=1,
            grid=(1,),
            in_specs=[pl.BlockSpec(keep.shape, lambda i, place: (0, 0, 0, 0))] * 2,
            out_specs=[pl.BlockSpec(piece.shape, lambda i, place: (0, 0, 0))] * len(offsets),
        ),
        out_shape=[piece] * len(offsets),
        compiler_params=params(8),
        cost_estimate=cost(keep.size, 6 * keep.size),
        name="split",
    )(place, keep, got)


def add_kernel(*refs):
    total = refs[0][...].astype(F32)
    for ref in refs[1:-1]:
        total = total + ref[...].astype(F32)
    refs[-1][...] = total.astype(BF16)


def add(*terms):
    return pl.pallas_call(
        add_kernel,
        out_shape=jax.ShapeDtypeStruct(terms[0].shape, BF16),
        compiler_params=params(8),
        cost_estimate=cost(len(terms) * terms[0].size, 2 * (len(terms) + 1) * terms[0].size),
        name="add",
    )(*terms)


def reflect_kernel(*refs):
    blocks_ref, out_ref = refs[-2:]
    levels, owned, order = blocks_ref.shape[:3]
    total = refs[0][...].astype(F32)
    for ref in refs[1:-2]:
        total = total + ref[...].astype(F32)
    total = total.astype(BF16)
    for level in range(levels):
        for b in range(owned):
            out_ref[level, :, b * order : (b + 1) * order] = lax.dot_general(
                total[level, :, b * order : (b + 1) * order],
                blocks_ref[level, b],
                LAST,
                preferred_element_type=F32,
            ).astype(BF16)


def reflect(terms, blocks):
    return pl.pallas_call(
        reflect_kernel,
        out_shape=jax.ShapeDtypeStruct(terms[0].shape, BF16),
        compiler_params=params(8),
        cost_estimate=cost(terms[0].size * 128, 2 * (len(terms) + 1) * terms[0].size),
        name="reflect",
    )(*terms, blocks)


def near_kernel(
    first_ref,
    slot_ref,
    count_ref,
    type_ref,
    halo_ref,
    own_ref,
    inner_ref,
    incident_ref,
    translations_ref,
    out_ref,
    extended,
    sums,
):
    group, m, size = incident_ref.shape
    kinds = translations_ref.shape[0]
    most = slot_ref.shape[1]
    for index, ref in enumerate((halo_ref, own_ref, inner_ref)):
        extended[pl.ds(index * group, group)] = ref[...]
    sums[...] = jnp.zeros(sums.shape, F32)
    for p in range(group):
        for k in range(most):

            @pl.when(k < count_ref[p])
            def _():
                place = type_ref[p, k]
                sums[place, p] += extended[slot_ref[p, k]].astype(F32)

    total = incident_ref[...].astype(F32).reshape(group * m, size)
    for t in range(kinds):
        total = total + lax.dot_general(
            sums[t].astype(BF16).reshape(group * m, size),
            translations_ref[t],
            LAST,
            preferred_element_type=F32,
        )
    out_ref[...] = total.reshape(group, m, size)


def near(first, slots, counts, types, halo, own, inner, incident, translations):
    m, size = incident.shape[1:]
    group = own.shape[0]
    kinds = translations.shape[0]
    whole = pl.BlockSpec((group, m, size), lambda p, *_: (0, 0, 0))
    return pl.pallas_call(
        near_kernel,
        grid_spec=pltpu.PrefetchScalarGridSpec(
            num_scalar_prefetch=4,
            grid=(1,),
            in_specs=[
                whole,
                whole,
                whole,
                pl.BlockSpec((group, m, size), lambda p, first, *_: (first[0], 0, 0)),
                pl.BlockSpec((kinds, size, size), lambda p, *_: (0, 0, 0)),
            ],
            out_specs=whole,
            scratch_shapes=[
                pltpu.VMEM((3 * group, m, size), BF16),
                pltpu.VMEM((kinds, group, m, size), F32),
            ],
        ),
        out_shape=jax.ShapeDtypeStruct((group, m, size), F32),
        compiler_params=params(32),
        cost_estimate=cost(kinds * group * m * size * size, 2 * size * size * kinds),
        name="near",
    )(first, slots, counts, types, halo, own, inner, incident, translations)


def back_kernel(first_ref, place_ref, offsets, refs):
    pieces = refs[: len(offsets)]
    phase_ref, basis_ref, partial_ref, t_ref = refs[len(offsets) : len(offsets) + 4]
    out_ref, waves = refs[-2:]
    group, m, size = partial_ref.shape
    chunks, parts, rows, width = waves.shape
    levels = pieces[0].shape[0]
    across = chunks // levels

    @pl.when(pl.program_id(0) == 0)
    def _():
        for (dc, dx, dy), piece in zip(offsets, pieces):
            part = (place_ref[2] ^ dc) * (parts // 2) + (place_ref[0] ^ dx)
            for level in range(levels):
                waves[level * across + (place_ref[1] ^ dy), part] = piece[level]

    total = partial_ref[...].reshape(group * m, size)
    for c in range(chunks):
        waves_here = waves[c].reshape(m, width)
        weighted = [
            phase_ref[i, :, pl.ds(c * width, width)] * waves_here for i in range(group)
        ]
        total = total + jnp.dot(
            jnp.concatenate(weighted, axis=0),
            basis_ref[pl.ds(c * width, width), :],
            preferred_element_type=F32,
        )
    source = total.astype(BF16)
    for i in range(group):
        out_ref[i] = lax.dot_general(
            source[i * m : (i + 1) * m], t_ref[i], LAST, preferred_element_type=F32
        ).astype(BF16)


def back(first, place, offsets, pieces, chunks, parts, phases, basis, partial, t_matrices, whole, onto=None):
    count, m, size = partial.shape
    levels, rows, width = pieces[0].shape
    total_rows = basis.shape[0]
    group = 2
    steps = count // group

    def body(first_ref, place_ref, *refs):
        if onto is not None:
            refs = refs[: len(offsets) + 4] + refs[len(offsets) + 5 :]
        back_kernel(first_ref, place_ref, offsets, refs)

    def here(p, first, place):
        return (first[0] * steps + p, 0, 0)

    def local_here(p, first, place):
        return (p, 0, 0)

    in_specs = [pl.BlockSpec((levels, rows, width), lambda p, *_: (0, 0, 0))] * len(pieces) + [
        pl.BlockSpec((group, 1, total_rows), here),
        pl.BlockSpec((total_rows, size), lambda p, *_: (0, 0)),
        pl.BlockSpec((group, m, size), local_here),
        pl.BlockSpec((group, size, size), here),
    ]
    operands = [first, place, *pieces, phases, basis, partial, t_matrices]
    aliases = {}
    if onto is not None:
        in_specs.append(pl.BlockSpec(memory_space=pl.ANY))
        aliases = {len(operands): 0}
        operands.append(onto)
    return pl.pallas_call(
        body,
        grid_spec=pltpu.PrefetchScalarGridSpec(
            num_scalar_prefetch=2,
            grid=(steps,),
            in_specs=in_specs,
            out_specs=pl.BlockSpec((group, m, size), here if whole else local_here),
            scratch_shapes=[pltpu.VMEM((chunks, parts, rows, width), BF16)],
        ),
        out_shape=jax.ShapeDtypeStruct((2 * count if whole else count, m, size), BF16),
        input_output_aliases=aliases,
        compiler_params=params(32),
        cost_estimate=cost(
            count * m * size * (total_rows + size), 2 * size * (total_rows + count * size)
        ),
        name="back",
    )(*operands)


def local(
    incident,
    t_matrices,
    translations,
    near_index,
    near_count,
    near_type,
    phases,
    wave_basis,
    grating_blocks,
):
    doms, blks = lax.axis_size("dom"), lax.axis_size("blk")
    devices = doms * blks
    levels = min(4, blks)
    y_count = blks // levels
    x_lo = min(2, doms // 2)
    x_hi = doms // 2 // x_lo
    count, size, m = incident.shape
    reach = count // 2
    me = lax.axis_index(AXES)
    dom, blk = lax.axis_index("dom"), lax.axis_index("blk")
    core, x = dom % 2, dom // 2 % x_lo
    z, y = blk // y_count, blk % y_count
    parts = 2 * x_lo
    rows = m // parts

    def flip(array, mask):
        return lax.ppermute(array, AXES, [(i, i ^ mask) for i in range(devices)])

    def scalar(*values):
        return jnp.stack([jnp.asarray(v, jnp.int32) for v in values])

    core_mask = blks
    plane = [(dx, dy) for dx in range(x_lo) for dy in range(y_count) if (dx, dy) != (0, 0)]
    plane.sort(key=lambda pair: -(pair[0] > 0) - (pair[1] > 0))
    plane_masks = [dx * 2 * blks + dy for dx, dy in plane]
    offsets = [(0, 0)] + plane
    all_offsets = [(dc, dx, dy) for dc in (0, 1) for dx, dy in offsets]
    columns = [
        (h, d) for h in range(x_hi) for d in (2, 3, 1, 0) if d < levels and (h, d) != (0, 0)
    ]
    column_masks = [h * x_lo * 2 * blks + d * y_count for h, d in columns]
    place = scalar(x, y, core)

    even = me % 2 == 0
    e_group = jnp.where(even, 1, 0).astype(jnp.int32)
    o_group = 1 - e_group
    e_pairs = [(i, i ^ 1) for i in range(devices)]
    o_pairs = [(i, i - 1 if i % 2 == 0 else i + 1) for i in range(1, devices - 1)]
    side = (near_index - me * count + reach) // reach
    within = (near_index - me * count + reach) % reach

    def lists(group):
        def taken(array):
            return lax.dynamic_slice_in_dim(array, group * reach, reach, axis=0)

        position = jnp.where(group == 0, side, 3 - side)
        slots = jnp.clip(position * reach + within, 0, 3 * reach - 1)
        return taken(slots).astype(jnp.int32), taken(near_count), taken(near_type)

    e_lists, o_lists = lists(e_group), lists(o_group)
    e_first, o_first = scalar(e_group), scalar(o_group)
    incident_t = jnp.swapaxes(incident, 1, 2)
    phase_rows = phases[:, None, :]
    grouped_phases = jnp.concatenate(
        [lax.dynamic_slice_in_dim(phases, g * reach, reach, axis=0) for g in (o_group, e_group)],
        axis=0,
    )

    held = [pltpu.with_memory_space_constraint(a, pltpu.HBM) for a in (incident_t, t_matrices)]
    o_coeffs = solve(o_first, *held, reach)
    e_coeffs = solve(e_first, *held, reach)
    for sweep in range(ITERS):
        o_halo = lax.ppermute(o_coeffs, AXES, o_pairs)
        send = outward(
            scalar(1 - core), o_coeffs, e_coeffs, wave_basis, grouped_phases, 2, blks
        )
        got = flip(send, core_mask)
        keep = outward(scalar(core), o_coeffs, e_coeffs, wave_basis, grouped_phases, 2, blks)
        shape = (blks, x_lo, rows, keep.shape[2])
        pieces = split(place, offsets, levels, keep.reshape(shape), got.reshape(shape))
        arrived = [flip(piece, mask) for piece, mask in zip(pieces[1:], plane_masks)]
        if sweep == 0:
            own_blocks, _ = lax.optimization_barrier((grating_blocks.astype(BF16), pieces[0]))
            gathered = jnp.zeros((levels,) + own_blocks.shape, BF16)
            gathered = lax.dynamic_update_slice(gathered, own_blocks[None], (z, 0, 0, 0))
            for d in range(1, levels):
                gathered = lax.dynamic_update_slice(
                    gathered, flip(own_blocks, d * y_count)[None], (z ^ d, 0, 0, 0)
                )
        arrived, o_halo = lax.optimization_barrier((arrived, o_halo))
        plane_sum = add(pieces[0], *arrived)
        e_sent, _ = lax.optimization_barrier((e_coeffs, plane_sum))
        e_halo = lax.ppermute(e_sent, AXES, e_pairs)
        o_near = near(
            o_first, *o_lists, o_halo, o_coeffs, e_coeffs, incident_t, translations
        )
        arrived = [flip(plane_sum, mask) for mask in column_masks]
        arrived, o_near = lax.optimization_barrier((arrived, o_near))
        stack = reflect([plane_sum, *arrived], gathered)
        e_near = near(
            e_first, *e_lists, e_halo, e_coeffs, o_coeffs, incident_t, translations
        )
        stacks = [stack] + [flip(stack, mask) for mask in plane_masks]
        late = [n for n, (dx, dy) in enumerate(offsets) if dy]
        held, e_near = lax.optimization_barrier(([stacks[n] for n in late], e_near))
        for n, piece in zip(late, held):
            stacks[n] = piece
        stacks = stacks + [flip(piece, core_mask) for piece in stacks]
        last = sweep == ITERS - 1
        common = (place, all_offsets, stacks, blks, parts, phase_rows, wave_basis)
        o_coeffs = back(o_first, *common, o_near, t_matrices, last)
        if not last:
            e_near, _ = lax.optimization_barrier((e_near, o_coeffs))
        e_coeffs = back(
            e_first, *common, e_near, t_matrices, last, o_coeffs if last else None
        )
    return jnp.swapaxes(e_coeffs, 1, 2)


def solution(mesh):
    placed = (
        P(("dom", "blk"), None, None),
        P(("dom", "blk"), None, None),
        P(),
        P(("dom", "blk"), None),
        P(("dom", "blk")),
        P(("dom", "blk"), None),
        P(("dom", "blk"), None),
        P(),
        P("blk", None, None),
    )
    return jax.shard_map(
        local, mesh=mesh, in_specs=placed, out_specs=P(("dom", "blk"), None, None), check_vma=False
    )
```

time: 175 us -> 130 us (0.74)
  the two profiles are of different devices: /device:TPU:3 before, /device:TPU:0 now
where the time goes in v2:
time: 130 us
  Pallas kernels  48.1 us (37%)
  starting transfers between devices  43.3 us (33%)
  waiting for transfers between devices  31.6 us (24%)
  local copies, waits for them, and re-layouts  6.17 us (5%)
    ppermute x31, starting transfers between devices, flip(): return lax.ppermute(array, AXES, [(i, i ^ mask) for i in range(devices)])  35.9 us
    ppermute x31, waiting for transfers between devices, flip(): return lax.ppermute(array, AXES, [(i, i ^ mask) for i in range(devices)])  26.1 us
    pallas_call x4, Pallas kernels, near(): pl.pallas_call(near_kernel, grid_spec=pltpu.PrefetchScalarGridSpec(num_sc...  16.1 us
    pallas_call x4, Pallas kernels, back(): pl.pallas_call(body, grid_spec=pltpu.PrefetchScalarGridSpec(num_scalar_pr...  14.7 us
    pallas_call x4, Pallas kernels, outward(): pl.pallas_call(outward_kernel, grid_spec=pltpu.PrefetchScalarGridSpec(num...  9.2 us
    unnamed x30, local copies, waits for them, and re-layouts  5.89 us
    ppermute x2, waiting for transfers between devices, local(): e_halo = lax.ppermute(e_sent, AXES, e_pairs)  5.46 us
    pallas_call x2, Pallas kernels, solve(): pl.pallas_call(solve_kernel, grid_spec=pltpu.PrefetchScalarGridSpec(num_s...  5.2 us
  transfers between devices with their start and end apart: 35, of which 14 were waited for; matrix products, arithmetic and copies ran while one was open for 0% of the time, Pallas kernels for 26%

profile of v2, /device:TPU:0, one launch (start us, length us, event | category | flops | bytes accessed | tf_op | source)
XLA Modules:
  0.0 129.8 jit_solution(17173964786324802767)
XLA Ops:
  0.0 2.5 %solve.2.one_ref.own_ref.inner_ref = bf16[4,192,512]{2,1,0:T(8,128)(2,1)S(1)} custom-call(s32[1]{0:T(128)} %bitcast.4.first_ref, bf16[8,192,512]{2,1,0:T(8,128)(2,1)} %bitcast.21, bf16[8,512,512]{2,1,0:T(8,128)(2,1)} %refs_11_.7), custom_call_target="tpu_custom_call" | custom-call | flops 1 | bytes 1 | tf_op jit(solution)/shard_map/solve/pallas_call | solution.py:46
  2.5 1.6 %collective-permute-start.4 = (bf16[4,192,512]{2,1,0:T(8,128)(2,1)S(1)}, bf16[4,192,512]{2,1,0:T(8,128)(2,1)}, u32[]{:S(2)}, u32[]{:S(2)}) collective-permute-start(bf16[4,192,512]{2,1,0:T(8,128)(2,1)S(1)} %solve.2.one_ref.own_ref.inner_ref), channel_id=1, source_target_pairs={{1,2},{2,1},{3,4},{4,3},{5,6},{6,5},{7,8},{8,7},{9,10},{10,9},{11,... | collective-permute-start | bytes 2359304 | tf_op jit(solution)/shard_map/ppermute | solution.py:417
  4.1 2.7 %solve.3.two_ref.inner_ref.own_ref = bf16[4,192,512]{2,1,0:T(8,128)(2,1)S(1)} custom-call(s32[1]{0:T(128)} %bitcast.first_ref, bf16[8,192,512]{2,1,0:T(8,128)(2,1)} %bitcast.22, bf16[8,512,512]{2,1,0:T(8,128)(2,1)} %refs_11_.7), custom_call_target="tpu_custom_call" | custom-call | flops 1 | bytes 1 | tf_op jit(solution)/shard_map/solve/pallas_call | solution.py:46
  6.8 0.9 copy-done.5
  7.8 1.1 copy-done.6
  8.9 2.8 %outward.5 = bf16[8,96,256]{2,1,0:T(8,128)(2,1)} custom-call(s32[1]{0:T(128)} %bitcast.7.part_ref, bf16[4,192,512]{2,1,0:T(8,128)(2,1)S(1)} %solve.2.one_ref.own_ref.inner_ref, bf16[4,192,512]{2,1,0:T(8,128)(2,1)S(1)} %copy-done.6, bf16[2048,512]{1,0:T(8,128)(2,1)S(1)} %copy-done.1, bf16[8,2048]{1,0:T(8,128)(2,1)S(1)} %pad_maximum_fusion.phase_ref), custom_call_target="tpu_custom_call" | custom-call | flops 1 | bytes 1 | tf_op jit(solution)/shard_map/outward/pallas_call | solution.py:93
  11.7 6.5 %collective-permute-start = (bf16[8,96,256]{2,1,0:T(8,128)(2,1)}, bf16[8,96,256]{2,1,0:T(8,128)(2,1)}, u32[]{:S(2)}, u32[]{:S(2)}) collective-permute-start(bf16[8,96,256]{2,1,0:T(8,128)(2,1)} %outward.5), channel_id=1, source_target_pairs={{0,8},{1,9},{2,10},{3,11},{4,12},{5,13},{6,14},{7,15},{8,0},{9,1},... | collective-permute-start | bytes 1179656 | tf_op jit(solution)/shard_map/ppermute | solution.py:371
  18.2 1.1 copy-done.7
  19.3 2.1 %outward.4 = bf16[8,96,256]{2,1,0:T(8,128)(2,1)S(1)} custom-call(s32[1]{0:T(128)} %bitcast.3.part_ref, bf16[4,192,512]{2,1,0:T(8,128)(2,1)S(1)} %solve.2.one_ref.own_ref.inner_ref, bf16[4,192,512]{2,1,0:T(8,128)(2,1)S(1)} %copy-done.7, bf16[2048,512]{1,0:T(8,128)(2,1)S(1)} %copy-done.1, bf16[8,2048]{1,0:T(8,128)(2,1)S(1)} %pad_maximum_fusion.phase_ref), custom_call_target="tpu_custom_call" | custom-call | flops 1 | bytes 1 | tf_op jit(solution)/shard_map/outward/pallas_call | solution.py:93
  21.5 0.1 fusion.8
  21.6 0.1 pad_add_fusion.place_ref
  21.8 1.6 %split.2 = (bf16[4,48,256]{2,1,0:T(8,128)(2,1)S(1)}, bf16[4,48,256]{2,1,0:T(8,128)(2,1)S(1)}, bf16[4,48,256]{2,1,0:T(8,128)(2,1)S(1)}, bf16[4,48,256]{2,1,0:T(8,128)(2,1)S(1)}) custom-call(s32[3]{0:T(128)S(1)} %pad_add_fusion.place_ref, bf16[8,2,48,256]{3,2,1,0:T(8,128)(2,1)S(1)} %bitcast.27, bf16[8,2,48,256]{3,2,1,0:T(8,128)(2,1)} %bitcast.8.refs_1_), custom_call_target="tpu_custom_call" | custom-call | flops 1 | bytes 1 | tf_op jit(solution)/shard_map/split/pallas_call | solution.py:133
  23.5 2.9 %collective-permute-start.2 = (bf16[4,48,256]{2,1,0:T(8,128)(2,1)S(1)}, bf16[4,48,256]{2,1,0:T(8,128)(2,1)S(1)}, u32[]{:S(2)}, u32[]{:S(2)}) collective-permute-start(bf16[4,48,256]{2,1,0:T(8,128)(2,1)S(1)} %get-tuple-element.41), channel_id=1, source_target_pairs={{0,1},{1,0},{2,3},{3,2},{4,5},{5,4},{6,7},{7,6},{8,9},{9,8},{10,11... | collective-permute-start | bytes 294920 | tf_op jit(solution)/shard_map/ppermute | solution.py:371
  26.4 0.5 collective-permute-start.3
  27.1 3.1 %collective-permute-done.1.refs_1_ = bf16[4,48,256]{2,1,0:T(8,128)(2,1)S(1)} collective-permute-done((bf16[4,48,256]{2,1,0:T(8,128)(2,1)S(1)}, bf16[4,48,256]{2,1,0:T(8,128)(2,1)S(1)}, u32[]{:S(2)}, u32[]{:S(2)}) %collective-permute-start.1) | collective-permute-done | bytes 98336 | tf_op jit(solution)/shard_map/ppermute | solution.py:371
  30.2 0.7 collective-permute-start.9
  30.9 1.1 collective-permute-done.2.refs_2_
  32.0 3.3 %collective-permute-start.10 = (bf16[2,128,128]{2,1,0:T(8,128)(2,1)S(1)}, bf16[2,128,128]{2,1,0:T(8,128)(2,1)S(1)}, u32[]{:S(2)}, u32[]{:S(2)}) collective-permute-start(bf16[2,128,128]{2,1,0:T(8,128)(2,1)S(1)} %convert_element_type.3), channel_id=1, source_target_pairs={{0,6},{1,7},{2,4},{3,5},{4,2},{5,3},{6,0},{7,1},{8,14},{9,15},{10,... | collective-permute-start | bytes 196616 | tf_op jit(solution)/shard_map/ppermute | solution.py:371
  35.3 2.5 %collective-permute-start.13 = (bf16[4,192,512]{2,1,0:T(8,128)(2,1)}, bf16[4,192,512]{2,1,0:T(8,128)(2,1)S(1)}, u32[]{:S(2)}, u32[]{:S(2)}) collective-permute-start(bf16[4,192,512]{2,1,0:T(8,128)(2,1)} %copy-done.5), channel_id=1, source_target_pairs={{0,1},{1,0},{2,3},{3,2},{4,5},{5,4},{6,7},{7,6},{8,9},{9,8},{10,11... | collective-permute-start | bytes 2359304 | tf_op jit(solution)/shard_map/ppermute | solution.py:437
  37.9 0.1 collective-permute-start.5
  38.0 0.9 collective-permute-start.6
  38.9 2.5 %collective-permute-start.7 = (bf16[4,48,256]{2,1,0:T(8,128)(2,1)S(1)}, bf16[4,48,256]{2,1,0:T(8,128)(2,1)S(1)}, u32[]{:S(2)}, u32[]{:S(2)}) collective-permute-start(bf16[4,48,256]{2,1,0:T(8,128)(2,1)S(1)} %add.114.refs_0_), channel_id=1, source_target_pairs={{0,2},{1,3},{2,0},{3,1},{4,6},{5,7},{6,4},{7,5},{8,10},{9,11},{10,... | collective-permute-start | bytes 294920 | tf_op jit(solution)/shard_map/ppermute | solution.py:371
  41.5 1.6 %copy-done.3 = bf16[4,512,512]{2,1,0:T(8,128)(2,1)S(1)} copy-done((bf16[4,512,512]{2,1,0:T(8,128)(2,1)S(1)}, bf16[4,512,512]{2,1,0:T(8,128)(2,1)}, u32[]{:S(2)}) %copy-start.3) | copy-done | bytes 2097176
  43.1 1.1 copy-done.8
  44.2 5.0 %near.4.refs_10_ = f32[4,192,512]{2,1,0:T(8,128)S(1)} custom-call(s32[1]{0:T(128)} %bitcast.4.first_ref, s32[4,6]{1,0:T(4,128)S(1)} %constant_dynamic-slice_fusion.3.slot_ref, s32[4]{0:T(128)S(1)} %get-tuple-element.80.count_ref, s32[4,6]{1,0:T(4,128)S(1)} %get-tuple-element.76.type_ref, bf16[4,192,512]{2,1,0:T(8,128)(2,1)} %collective-permute-done.4.halo_ref, ...), custom_call_target="tpu_custom_call" | custom-call | flops 1 | bytes 1 | tf_op jit(solution)/shard_map/near/pallas_call | solution.py:236
  49.3 0.3 reflect.2.refs_0_
  49.6 3.1 %collective-permute-start.12 = (bf16[4,48,256]{2,1,0:T(8,128)(2,1)S(1)}, bf16[4,48,256]{2,1,0:T(8,128)(2,1)S(1)}, u32[]{:S(2)}, u32[]{:S(2)}) collective-permute-start(bf16[4,48,256]{2,1,0:T(8,128)(2,1)S(1)} %reflect.2.refs_0_), channel_id=1, source_target_pairs={{0,1},{1,0},{2,3},{3,2},{4,5},{5,4},{6,7},{7,6},{8,9},{9,8},{10,11... | collective-permute-start | bytes 294920 | tf_op jit(solution)/shard_map/ppermute | solution.py:371
  52.8 0.4 collective-permute-start.14
  53.1 4.2 %collective-permute-done.14.refs_3_ = bf16[4,48,256]{2,1,0:T(8,128)(2,1)S(1)} collective-permute-done((bf16[4,48,256]{2,1,0:T(8,128)(2,1)S(1)}, bf16[4,48,256]{2,1,0:T(8,128)(2,1)S(1)}, u32[]{:S(2)}, u32[]{:S(2)}) %collective-permute-start.14) | collective-permute-done | bytes 98336 | tf_op jit(solution)/shard_map/ppermute | solution.py:371
  57.4 1.2 collective-permute-done.13.halo_ref
  58.6 3.8 %near.5.refs_10_ = f32[4,192,512]{2,1,0:T(8,128)S(1)} custom-call(s32[1]{0:T(128)} %bitcast.first_ref, s32[4,6]{1,0:T(4,128)S(1)} %constant_dynamic-slice_fusion.1.slot_ref, s32[4]{0:T(128)S(1)} %get-tuple-element.79.count_ref, s32[4,6]{1,0:T(4,128)S(1)} %get-tuple-element.75.type_ref, bf16[4,192,512]{2,1,0:T(8,128)(2,1)S(1)} %collective-permute-done.13.halo_ref, ...), custom_call_target="tpu_custom_call" | custom-call | flops 1 | bytes 1 | tf_op jit(solution)/shard_map/near/pallas_call | solution.py:236
  62.4 0.5 collective-permute-start.17
  63.0 0.7 collective-permute-done.16.refs_5_
  63.7 0.2 collective-permute-done.17.refs_6_
  63.9 3.3 %back.4.one_ref.own_ref.inner_ref = bf16[4,192,512]{2,1,0:T(8,128)(2,1)S(1)} custom-call(s32[1]{0:T(128)} %bitcast.4.first_ref, s32[3]{0:T(128)S(1)} %pad_add_fusion.place_ref, bf16[4,48,256]{2,1,0:T(8,128)(2,1)S(1)} %reflect.2.refs_0_, bf16[4,48,256]{2,1,0:T(8,128)(2,1)S(1)} %collective-permute-done.11.refs_1_, ...), custom_call_target="tpu_custom_call" | custom-call | flops 1 | bytes 1 | tf_op jit(solution)/shard_map/back/pallas_call | solution.py:325
  67.2 0.7 collective-permute-start.23
  67.9 3.3 %back.5.two_ref.inner_ref.own_ref = bf16[4,192,512]{2,1,0:T(8,128)(2,1)S(1)} custom-call(s32[1]{0:T(128)} %bitcast.first_ref, s32[3]{0:T(128)S(1)} %pad_add_fusion.place_ref, bf16[4,48,256]{2,1,0:T(8,128)(2,1)S(1)} %reflect.2.refs_0_, bf16[4,48,256]{2,1,0:T(8,128)(2,1)S(1)} %collective-permute-done.11.refs_1_, ...), custom_call_target="tpu_custom_call" | custom-call | flops 1 | bytes 1 | tf_op jit(solution)/shard_map/back/pallas_call | solution.py:325
  71.2 2.2 %outward.7 = bf16[8,96,256]{2,1,0:T(8,128)(2,1)S(1)} custom-call(s32[1]{0:T(128)} %bitcast.7.part_ref, bf16[4,192,512]{2,1,0:T(8,128)(2,1)S(1)} %back.4.one_ref.own_ref.inner_ref, bf16[4,192,512]{2,1,0:T(8,128)(2,1)S(1)} %back.5.two_ref.inner_ref.own_ref, bf16[2048,512]{1,0:T(8,128)(2,1)S(1)} %copy-done.1, bf16[8,2048]{1,0:T(8,128)(2,1)S(1)} %pad_maximum_fusion.phase_ref), custom_call_target="tpu_custom_call" | custom-call | flops 1 | bytes 1 | tf_op jit(solution)/shard_map/outward/pallas_call | solution.py:93
  73.4 3.0 %collective-permute-start.19 = (bf16[8,96,256]{2,1,0:T(8,128)(2,1)S(1)}, bf16[8,96,256]{2,1,0:T(8,128)(2,1)S(1)}, u32[]{:S(2)}, u32[]{:S(2)}) collective-permute-start(bf16[8,96,256]{2,1,0:T(8,128)(2,1)S(1)} %outward.7), channel_id=1, source_target_pairs={{0,8},{1,9},{2,10},{3,11},{4,12},{5,13},{6,14},{7,15},{8,0},{9,1},... | collective-permute-start | bytes 1179656 | tf_op jit(solution)/shard_map/ppermute | solution.py:371
  76.4 2.1 %outward.6 = bf16[8,96,256]{2,1,0:T(8,128)(2,1)S(1)} custom-call(s32[1]{0:T(128)} %bitcast.3.part_ref, bf16[4,192,512]{2,1,0:T(8,128)(2,1)S(1)} %back.4.one_ref.own_ref.inner_ref, bf16[4,192,512]{2,1,0:T(8,128)(2,1)S(1)} %back.5.two_ref.inner_ref.own_ref, bf16[2048,512]{1,0:T(8,128)(2,1)S(1)} %copy-done.1, bf16[8,2048]{1,0:T(8,128)(2,1)S(1)} %pad_maximum_fusion.phase_ref), custom_call_target="tpu_custom_call" | custom-call | flops 1 | bytes 1 | tf_op jit(solution)/shard_map/outward/pallas_call | solution.py:93
  78.5 0.6 split.3
  79.1 0.3 collective-permute-start.20
  79.4 2.6 %collective-permute-start.21 = (bf16[4,48,256]{2,1,0:T(8,128)(2,1)S(1)}, bf16[4,48,256]{2,1,0:T(8,128)(2,1)S(1)}, u32[]{:S(2)}, u32[]{:S(2)}) collective-permute-start(bf16[4,48,256]{2,1,0:T(8,128)(2,1)S(1)} %get-tuple-element.59), channel_id=1, source_target_pairs={{0,1},{1,0},{2,3},{3,2},{4,5},{5,4},{6,7},{7,6},{8,9},{9,8},{10,11... | collective-permute-start | bytes 294920 | tf_op jit(solution)/shard_map/ppermute | solution.py:371
  82.0 0.7 collective-permute-start.22
  82.7 3.7 %collective-permute-done.20.refs_1_ = bf16[4,48,256]{2,1,0:T(8,128)(2,1)S(1)} collective-permute-done((bf16[4,48,256]{2,1,0:T(8,128)(2,1)S(1)}, bf16[4,48,256]{2,1,0:T(8,128)(2,1)S(1)}, u32[]{:S(2)}, u32[]{:S(2)}) %collective-permute-start.20) | collective-permute-done | bytes 98336 | tf_op jit(solution)/shard_map/ppermute | solution.py:371
  86.4 6.9 %collective-permute-done.21.refs_2_ = bf16[4,48,256]{2,1,0:T(8,128)(2,1)S(1)} collective-permute-done((bf16[4,48,256]{2,1,0:T(8,128)(2,1)S(1)}, bf16[4,48,256]{2,1,0:T(8,128)(2,1)S(1)}, u32[]{:S(2)}, u32[]{:S(2)}) %collective-permute-start.21) | collective-permute-done | bytes 98336 | tf_op jit(solution)/shard_map/ppermute | solution.py:371
  93.3 2.5 %collective-permute-start.29 = (bf16[4,192,512]{2,1,0:T(8,128)(2,1)S(1)}, bf16[4,192,512]{2,1,0:T(8,128)(2,1)S(1)}, u32[]{:S(2)}, u32[]{:S(2)}) collective-permute-start(bf16[4,192,512]{2,1,0:T(8,128)(2,1)S(1)} %back.5.two_ref.inner_ref.own_ref), channel_id=1, source_target_pairs={{0,1},{1,0},{2,3},{3,2},{4,5},{5,4},{6,7},{7,6},{8,9},{9,8},{10,11... | collective-permute-start | bytes 2359304 | tf_op jit(solution)/shard_map/ppermute | solution.py:437
  95.9 2.3 %collective-permute-start.25 = (bf16[4,48,256]{2,1,0:T(8,128)(2,1)S(1)}, bf16[4,48,256]{2,1,0:T(8,128)(2,1)S(1)}, u32[]{:S(2)}, u32[]{:S(2)}) collective-permute-start(bf16[4,48,256]{2,1,0:T(8,128)(2,1)S(1)} %add.115.refs_0_), channel_id=1, source_target_pairs={{0,6},{1,7},{2,4},{3,5},{4,2},{5,3},{6,0},{7,1},{8,14},{9,15},{10,... | collective-permute-start | bytes 294920 | tf_op jit(solution)/shard_map/ppermute | solution.py:371
  98.2 1.2 collective-permute-start.26
  99.4 3.6 %near.6.refs_10_ = f32[4,192,512]{2,1,0:T(8,128)S(1)} custom-call(s32[1]{0:T(128)} %bitcast.4.first_ref, s32[4,6]{1,0:T(4,128)S(1)} %constant_dynamic-slice_fusion.3.slot_ref, s32[4]{0:T(128)S(1)} %get-tuple-element.80.count_ref, s32[4,6]{1,0:T(4,128)S(1)} %get-tuple-element.76.type_ref, bf16[4,192,512]{2,1,0:T(8,128)(2,1)S(1)} %collective-permute-done.23.halo_ref, ...), custom_call_target="tpu_custom_call" | custom-call | flops 1 | bytes 1 | tf_op jit(solution)/shard_map/near/pallas_call | solution.py:236
  103.0 2.3 %collective-permute-done.24.refs_1_ = bf16[4,48,256]{2,1,0:T(8,128)(2,1)S(1)} collective-permute-done((bf16[4,48,256]{2,1,0:T(8,128)(2,1)S(1)}, bf16[4,48,256]{2,1,0:T(8,128)(2,1)S(1)}, u32[]{:S(2)}, u32[]{:S(2)}) %collective-permute-start.24) | collective-permute-done | bytes 98336 | tf_op jit(solution)/shard_map/ppermute | solution.py:371
  105.3 1.2 collective-permute-done.26.refs_3_
  106.4 0.3 reflect.3.refs_0_
  106.7 0.3 collective-permute-start.30
  107.1 1.7 %collective-permute-start.27 = (bf16[4,48,256]{2,1,0:T(8,128)(2,1)S(1)}, bf16[4,48,256]{2,1,0:T(8,128)(2,1)S(1)}, u32[]{:S(2)}, u32[]{:S(2)}) collective-permute-start(bf16[4,48,256]{2,1,0:T(8,128)(2,1)S(1)} %reflect.3.refs_0_), channel_id=1, source_target_pairs={{0,17},{1,16},{2,19},{3,18},{4,21},{5,20},{6,23},{7,22},{8,25},{9,... | collective-permute-start | bytes 294920 | tf_op jit(solution)/shard_map/ppermute | solution.py:371
  108.8 1.5 %collective-permute-start.28 = (bf16[4,48,256]{2,1,0:T(8,128)(2,1)S(1)}, bf16[4,48,256]{2,1,0:T(8,128)(2,1)S(1)}, u32[]{:S(2)}, u32[]{:S(2)}) collective-permute-start(bf16[4,48,256]{2,1,0:T(8,128)(2,1)S(1)} %reflect.3.refs_0_), channel_id=1, source_target_pairs={{0,1},{1,0},{2,3},{3,2},{4,5},{5,4},{6,7},{7,6},{8,9},{9,8},{10,11... | collective-permute-start | bytes 294920 | tf_op jit(solution)/shard_map/ppermute | solution.py:371
  110.3 1.8 %collective-permute-done.30.refs_3_ = bf16[4,48,256]{2,1,0:T(8,128)(2,1)S(1)} collective-permute-done((bf16[4,48,256]{2,1,0:T(8,128)(2,1)S(1)}, bf16[4,48,256]{2,1,0:T(8,128)(2,1)S(1)}, u32[]{:S(2)}, u32[]{:S(2)}) %collective-permute-start.30) | collective-permute-done | bytes 98336 | tf_op jit(solution)/shard_map/ppermute | solution.py:371
  112.1 4.3 %collective-permute-done.29.halo_ref = bf16[4,192,512]{2,1,0:T(8,128)(2,1)S(1)} collective-permute-done((bf16[4,192,512]{2,1,0:T(8,128)(2,1)S(1)}, bf16[4,192,512]{2,1,0:T(8,128)(2,1)S(1)}, u32[]{:S(2)}, u32[]{:S(2)}) %collective-permute-start.29) | collective-permute-done | bytes 786464 | tf_op jit(solution)/shard_map/ppermute | solution.py:437
  116.3 3.8 %near.7.refs_10_ = f32[4,192,512]{2,1,0:T(8,128)S(1)} custom-call(s32[1]{0:T(128)} %bitcast.first_ref, s32[4,6]{1,0:T(4,128)S(1)} %constant_dynamic-slice_fusion.1.slot_ref, s32[4]{0:T(128)S(1)} %get-tuple-element.79.count_ref, s32[4,6]{1,0:T(4,128)S(1)} %get-tuple-element.75.type_ref, bf16[4,192,512]{2,1,0:T(8,128)(2,1)S(1)} %collective-permute-done.29.halo_ref, ...), custom_call_target="tpu_custom_call" | custom-call | flops 1 | bytes 1 | tf_op jit(solution)/shard_map/near/pallas_call | solution.py:236
  120.2 0.5 collective-permute-start.33
  120.7 0.8 collective-permute-done.32.refs_5_
  121.5 0.2 collective-permute-done.33.refs_6_
  121.7 4.0 %back.6.refs_12_ = bf16[8,192,512]{2,1,0:T(8,128)(2,1)} custom-call(s32[1]{0:T(128)} %bitcast.4.first_ref, s32[3]{0:T(128)S(1)} %pad_add_fusion.place_ref, bf16[4,48,256]{2,1,0:T(8,128)(2,1)S(1)} %reflect.3.refs_0_, bf16[4,48,256]{2,1,0:T(8,128)(2,1)S(1)} %collective-permute-done.27.refs_1_, bf16[4,48,256]{2,1,0:T(8,128)(2,1)S(1)} %collective-permute-done.28.refs_2_, ...), custom_call_target="tpu_custom_call" | custom-call | flops 1 | bytes 1 | tf_op jit(solution)/shard_map/back/pallas_call | solution.py:325
  125.7 4.0 %back.7 = bf16[8,192,512]{2,1,0:T(8,128)(2,1)} custom-call(s32[1]{0:T(128)} %bitcast.first_ref, s32[3]{0:T(128)S(1)} %pad_add_fusion.place_ref, bf16[4,48,256]{2,1,0:T(8,128)(2,1)S(1)} %reflect.3.refs_0_, bf16[4,48,256]{2,1,0:T(8,128)(2,1)S(1)} %collective-permute-done.27.refs_1_, ...), custom_call_target="tpu_custom_call", output_to_operand_aliasing={{}: (14, {})} | custom-call | flops 1 | bytes 1 | tf_op jit(solution)/shard_map/back/pallas_call | solution.py:325
  (71 shorter events, 0.8 us)
Async XLA Ops:
  2.5 32.7 %collective-permute-start.4 = (bf16[4,192,512]{2,1,0:T(8,128)(2,1)S(1)}, bf16[4,192,512]{2,1,0:T(8,128)(2,1)}, u32[]{:S(2)}, u32[]{:S(2)}) collective-permute-start(bf16[4,192,512]{2,1,0:T(8,128)(2,1)S(1)} %solve.2.one_ref.own_ref.inner_ref), channel_id=1, source_target_pairs={{1,2},{2,1},{3,4},{4,3},{5,6},{6,5},{7,8},{8,7},{9,10},{10,9},{11,... | collective-permute-start | bytes 2359304 | tf_op jit(solution)/shard_map/ppermute | solution.py:417
  4.1 3.6 %copy-start.10 = (bf16[8,2048]{1,0:T(8,128)(2,1)S(1)}, bf16[8,2048]{1,0:T(8,128)(2,1)}, u32[]{:S(2)}) copy-start(bf16[8,2048]{1,0:T(8,128)(2,1)} %param.15) | copy-start | bytes 98308
  4.1 3.6 %copy-start.1 = (bf16[2048,512]{1,0:T(8,128)(2,1)S(1)}, bf16[2048,512]{1,0:T(8,128)(2,1)}, u32[]{:S(2)}) copy-start(bf16[2048,512]{1,0:T(8,128)(2,1)} %refs_9_.7) | copy-start | bytes 6291460
  6.8 0.9 copy-start.5
  7.7 1.1 copy-start.6
  11.7 10.1 %collective-permute-start = (bf16[8,96,256]{2,1,0:T(8,128)(2,1)}, bf16[8,96,256]{2,1,0:T(8,128)(2,1)}, u32[]{:S(2)}, u32[]{:S(2)}) collective-permute-start(bf16[8,96,256]{2,1,0:T(8,128)(2,1)} %outward.5), channel_id=1, source_target_pairs={{0,8},{1,9},{2,10},{3,11},{4,12},{5,13},{6,14},{7,15},{8,0},{9,1},... | collective-permute-start | bytes 1179656 | tf_op jit(solution)/shard_map/ppermute | solution.py:371
  18.2 1.1 copy-start.7
  19.3 2.2 %copy-start.14 = (s32[8]{0:T(128)S(1)}, s32[8]{0:T(128)}, u32[]{:S(2)}) copy-start(s32[8]{0:T(128)} %param.13) | copy-start | bytes 100
  19.3 2.3 %copy-start.11 = (f32[2,128,128]{2,1,0:T(8,128)S(1)}, f32[2,128,128]{2,1,0:T(8,128)}, u32[]{:S(2)}) copy-start(f32[2,128,128]{2,1,0:T(8,128)} %param.17) | copy-start | bytes 393220
  19.3 2.4 %copy-start.12 = (s32[8,6]{1,0:T(8,128)S(1)}, s32[8,6]{1,0:T(8,128)}, u32[]{:S(2)}) copy-start(s32[8,6]{1,0:T(8,128)} %param.12) | copy-start | bytes 580
  19.3 2.4 %copy-start.13 = (s32[8,6]{1,0:T(8,128)S(1)}, s32[8,6]{1,0:T(8,128)}, u32[]{:S(2)}) copy-start(s32[8,6]{1,0:T(8,128)} %param.14) | copy-start | bytes 580
  21.6 19.9 %copy-start.2 = (bf16[8,512,192]{1,2,0:T(8,128)(2,1)S(1)}, bf16[8,512,192]{1,2,0:T(8,128)(2,1)}, u32[]{:S(2)}) copy-start(bf16[8,512,192]{1,2,0:T(8,128)(2,1)} %param.9) | copy-start | bytes 4718596
  23.4 6.7 %collective-permute-start.1 = (bf16[4,48,256]{2,1,0:T(8,128)(2,1)S(1)}, bf16[4,48,256]{2,1,0:T(8,128)(2,1)S(1)}, u32[]{:S(2)}, u32[]{:S(2)}) collective-permute-start(bf16[4,48,256]{2,1,0:T(8,128)(2,1)S(1)} %get-tuple-element.40), channel_id=1, source_target_pairs={{0,17},{1,16},{2,19},{3,18},{4,21},{5,20},{6,23},{7,22},{8,25},{9,... | collective-permute-start | bytes 294920 | tf_op jit(solution)/shard_map/ppermute | solution.py:371
  23.5 8.5 %collective-permute-start.2 = (bf16[4,48,256]{2,1,0:T(8,128)(2,1)S(1)}, bf16[4,48,256]{2,1,0:T(8,128)(2,1)S(1)}, u32[]{:S(2)}, u32[]{:S(2)}) collective-permute-start(bf16[4,48,256]{2,1,0:T(8,128)(2,1)S(1)} %get-tuple-element.41), channel_id=1, source_target_pairs={{0,1},{1,0},{2,3},{3,2},{4,5},{5,4},{6,7},{7,6},{8,9},{9,8},{10,11... | collective-permute-start | bytes 294920 | tf_op jit(solution)/shard_map/ppermute | solution.py:371
  26.4 8.8 %collective-permute-start.3 = (bf16[4,48,256]{2,1,0:T(8,128)(2,1)S(1)}, bf16[4,48,256]{2,1,0:T(8,128)(2,1)S(1)}, u32[]{:S(2)}, u32[]{:S(2)}) collective-permute-start(bf16[4,48,256]{2,1,0:T(8,128)(2,1)S(1)} %get-tuple-element.42), channel_id=1, source_target_pairs={{0,16},{1,17},{2,18},{3,19},{4,20},{5,21},{6,22},{7,23},{8,24},{9,... | collective-permute-start | bytes 294920 | tf_op jit(solution)/shard_map/ppermute | solution.py:371
  27.0 10.9 %collective-permute-start.8 = (bf16[2,128,128]{2,1,0:T(8,128)(2,1)S(1)}, bf16[2,128,128]{2,1,0:T(8,128)(2,1)S(1)}, u32[]{:S(2)}, u32[]{:S(2)}) collective-permute-start(bf16[2,128,128]{2,1,0:T(8,128)(2,1)S(1)} %convert_element_type.3), channel_id=1, source_target_pairs={{0,2},{1,3},{2,0},{3,1},{4,6},{5,7},{6,4},{7,5},{8,10},{9,11},{10,... | collective-permute-start | bytes 196616 | tf_op jit(solution)/shard_map/ppermute | solution.py:371
  30.2 7.7 %collective-permute-start.9 = (bf16[2,128,128]{2,1,0:T(8,128)(2,1)S(1)}, bf16[2,128,128]{2,1,0:T(8,128)(2,1)S(1)}, u32[]{:S(2)}, u32[]{:S(2)}) collective-permute-start(bf16[2,128,128]{2,1,0:T(8,128)(2,1)S(1)} %convert_element_type.3), channel_id=1, source_target_pairs={{0,4},{1,5},{2,6},{3,7},{4,0},{5,1},{6,2},{7,3},{8,12},{9,13},{10,... | collective-permute-start | bytes 196616 | tf_op jit(solution)/shard_map/ppermute | solution.py:371
  32.0 9.5 %collective-permute-start.10 = (bf16[2,128,128]{2,1,0:T(8,128)(2,1)S(1)}, bf16[2,128,128]{2,1,0:T(8,128)(2,1)S(1)}, u32[]{:S(2)}, u32[]{:S(2)}) collective-permute-start(bf16[2,128,128]{2,1,0:T(8,128)(2,1)S(1)} %convert_element_type.3), channel_id=1, source_target_pairs={{0,6},{1,7},{2,4},{3,5},{4,2},{5,3},{6,0},{7,1},{8,14},{9,15},{10,... | collective-permute-start | bytes 196616 | tf_op jit(solution)/shard_map/ppermute | solution.py:371
  35.3 23.2 %collective-permute-start.13 = (bf16[4,192,512]{2,1,0:T(8,128)(2,1)}, bf16[4,192,512]{2,1,0:T(8,128)(2,1)S(1)}, u32[]{:S(2)}, u32[]{:S(2)}) collective-permute-start(bf16[4,192,512]{2,1,0:T(8,128)(2,1)} %copy-done.5), channel_id=1, source_target_pairs={{0,1},{1,0},{2,3},{3,2},{4,5},{5,4},{6,7},{7,6},{8,9},{9,8},{10,11... | collective-permute-start | bytes 2359304 | tf_op jit(solution)/shard_map/ppermute | solution.py:437
  37.9 11.3 %collective-permute-start.5 = (bf16[4,48,256]{2,1,0:T(8,128)(2,1)S(1)}, bf16[4,48,256]{2,1,0:T(8,128)(2,1)S(1)}, u32[]{:S(2)}, u32[]{:S(2)}) collective-permute-start(bf16[4,48,256]{2,1,0:T(8,128)(2,1)S(1)} %add.114.refs_0_), channel_id=1, source_target_pairs={{0,4},{1,5},{2,6},{3,7},{4,0},{5,1},{6,2},{7,3},{8,12},{9,13},{10,... | collective-permute-start | bytes 294920 | tf_op jit(solution)/shard_map/ppermute | solution.py:371
  38.0 11.2 %collective-permute-start.6 = (bf16[4,48,256]{2,1,0:T(8,128)(2,1)S(1)}, bf16[4,48,256]{2,1,0:T(8,128)(2,1)S(1)}, u32[]{:S(2)}, u32[]{:S(2)}) collective-permute-start(bf16[4,48,256]{2,1,0:T(8,128)(2,1)S(1)} %add.114.refs_0_), channel_id=1, source_target_pairs={{0,6},{1,7},{2,4},{3,5},{4,2},{5,3},{6,0},{7,1},{8,14},{9,15},{10,... | collective-permute-start | bytes 294920 | tf_op jit(solution)/shard_map/ppermute | solution.py:371
  38.9 10.3 %collective-permute-start.7 = (bf16[4,48,256]{2,1,0:T(8,128)(2,1)S(1)}, bf16[4,48,256]{2,1,0:T(8,128)(2,1)S(1)}, u32[]{:S(2)}, u32[]{:S(2)}) collective-permute-start(bf16[4,48,256]{2,1,0:T(8,128)(2,1)S(1)} %add.114.refs_0_), channel_id=1, source_target_pairs={{0,2},{1,3},{2,0},{3,1},{4,6},{5,7},{6,4},{7,5},{8,10},{9,11},{10,... | collective-permute-start | bytes 294920 | tf_op jit(solution)/shard_map/ppermute | solution.py:371
  41.5 1.6 %copy-start.3 = (bf16[4,512,512]{2,1,0:T(8,128)(2,1)S(1)}, bf16[4,512,512]{2,1,0:T(8,128)(2,1)}, u32[]{:S(2)}) copy-start(bf16[4,512,512]{2,1,0:T(8,128)(2,1)} %translations_ref.7) | copy-start | bytes 6291460
  43.1 1.1 copy-start.8
  44.2 14.3 %copy-start.4 = (bf16[4,512,512]{2,1,0:T(8,128)(2,1)S(1)}, bf16[4,512,512]{2,1,0:T(8,128)(2,1)}, u32[]{:S(2)}) copy-start(bf16[4,512,512]{2,1,0:T(8,128)(2,1)} %translations_ref.7) | copy-start | bytes 6291460
  44.2 14.3 %copy-start.9 = (bf16[4,192,512]{2,1,0:T(8,128)(2,1)S(1)}, bf16[4,192,512]{2,1,0:T(8,128)(2,1)}, u32[]{:S(2)}) copy-start(bf16[4,192,512]{2,1,0:T(8,128)(2,1)} %copy-done.5) | copy-start | bytes 2359300
  49.6 12.8 %collective-permute-start.11 = (bf16[4,48,256]{2,1,0:T(8,128)(2,1)S(1)}, bf16[4,48,256]{2,1,0:T(8,128)(2,1)S(1)}, u32[]{:S(2)}, u32[]{:S(2)}) collective-permute-start(bf16[4,48,256]{2,1,0:T(8,128)(2,1)S(1)} %reflect.2.refs_0_), channel_id=1, source_target_pairs={{0,17},{1,16},{2,19},{3,18},{4,21},{5,20},{6,23},{7,22},{8,25},{9,... | collective-permute-start | bytes 294920 | tf_op jit(solution)/shard_map/ppermute | solution.py:371
  49.6 12.7 %collective-permute-start.12 = (bf16[4,48,256]{2,1,0:T(8,128)(2,1)S(1)}, bf16[4,48,256]{2,1,0:T(8,128)(2,1)S(1)}, u32[]{:S(2)}, u32[]{:S(2)}) collective-permute-start(bf16[4,48,256]{2,1,0:T(8,128)(2,1)S(1)} %reflect.2.refs_0_), channel_id=1, source_target_pairs={{0,1},{1,0},{2,3},{3,2},{4,5},{5,4},{6,7},{7,6},{8,9},{9,8},{10,11... | collective-permute-start | bytes 294920 | tf_op jit(solution)/shard_map/ppermute | solution.py:371
  52.8 4.6 %collective-permute-start.14 = (bf16[4,48,256]{2,1,0:T(8,128)(2,1)S(1)}, bf16[4,48,256]{2,1,0:T(8,128)(2,1)S(1)}, u32[]{:S(2)}, u32[]{:S(2)}) collective-permute-start(bf16[4,48,256]{2,1,0:T(8,128)(2,1)S(1)} %reflect.2.refs_0_), channel_id=1, source_target_pairs={{0,16},{1,17},{2,18},{3,19},{4,20},{5,21},{6,22},{7,23},{8,24},{9,... | collective-permute-start | bytes 294920 | tf_op jit(solution)/shard_map/ppermute | solution.py:371
  53.1 9.9 %collective-permute-start.15 = (bf16[4,48,256]{2,1,0:T(8,128)(2,1)S(1)}, bf16[4,48,256]{2,1,0:T(8,128)(2,1)S(1)}, u32[]{:S(2)}, u32[]{:S(2)}) collective-permute-start(bf16[4,48,256]{2,1,0:T(8,128)(2,1)S(1)} %reflect.2.refs_0_), channel_id=1, source_target_pairs={{0,8},{1,9},{2,10},{3,11},{4,12},{5,13},{6,14},{7,15},{8,0},{9,1},... | collective-permute-start | bytes 294920 | tf_op jit(solution)/shard_map/ppermute | solution.py:371
  57.4 5.6 %collective-permute-start.18 = (bf16[4,48,256]{2,1,0:T(8,128)(2,1)S(1)}, bf16[4,48,256]{2,1,0:T(8,128)(2,1)S(1)}, u32[]{:S(2)}, u32[]{:S(2)}) collective-permute-start(bf16[4,48,256]{2,1,0:T(8,128)(2,1)S(1)} %collective-permute-done.14.refs_3_), channel_id=1, source_target_pairs={{0,8},{1,9},{2,10},{3,11},{4,12},{5,13},{6,14},{7,15},{8,0},{9,1},... | collective-permute-start | bytes 294920 | tf_op jit(solution)/shard_map/ppermute | solution.py:371
  58.6 5.3 %copy-start = (bf16[8,512,512]{2,1,0:T(8,128)(2,1)S(1)}, bf16[8,512,512]{2,1,0:T(8,128)(2,1)}, u32[]{:S(2)}) copy-start(bf16[8,512,512]{2,1,0:T(8,128)(2,1)} %refs_11_.7) | copy-start | bytes 12582916
  62.4 1.4 %collective-permute-start.16 = (bf16[4,48,256]{2,1,0:T(8,128)(2,1)S(1)}, bf16[4,48,256]{2,1,0:T(8,128)(2,1)S(1)}, u32[]{:S(2)}, u32[]{:S(2)}) collective-permute-start(bf16[4,48,256]{2,1,0:T(8,128)(2,1)S(1)} %collective-permute-done.11.refs_1_), channel_id=1, source_target_pairs={{0,8},{1,9},{2,10},{3,11},{4,12},{5,13},{6,14},{7,15},{8,0},{9,1},... | collective-permute-start | bytes 294920 | tf_op jit(solution)/shard_map/ppermute | solution.py:371
  62.4 1.4 %collective-permute-start.17 = (bf16[4,48,256]{2,1,0:T(8,128)(2,1)S(1)}, bf16[4,48,256]{2,1,0:T(8,128)(2,1)S(1)}, u32[]{:S(2)}, u32[]{:S(2)}) collective-permute-start(bf16[4,48,256]{2,1,0:T(8,128)(2,1)S(1)} %collective-permute-done.12.refs_2_), channel_id=1, source_target_pairs={{0,8},{1,9},{2,10},{3,11},{4,12},{5,13},{6,14},{7,15},{8,0},{9,1},... | collective-permute-start | bytes 294920 | tf_op jit(solution)/shard_map/ppermute | solution.py:371
  67.2 26.1 %collective-permute-start.23 = (bf16[4,192,512]{2,1,0:T(8,128)(2,1)S(1)}, bf16[4,192,512]{2,1,0:T(8,128)(2,1)S(1)}, u32[]{:S(2)}, u32[]{:S(2)}) collective-permute-start(bf16[4,192,512]{2,1,0:T(8,128)(2,1)S(1)} %back.4.one_ref.own_ref.inner_ref), channel_id=1, source_target_pairs={{1,2},{2,1},{3,4},{4,3},{5,6},{6,5},{7,8},{8,7},{9,10},{10,9},{11,... | collective-permute-start | bytes 2359304 | tf_op jit(solution)/shard_map/ppermute | solution.py:417
  73.4 5.1 %collective-permute-start.19 = (bf16[8,96,256]{2,1,0:T(8,128)(2,1)S(1)}, bf16[8,96,256]{2,1,0:T(8,128)(2,1)S(1)}, u32[]{:S(2)}, u32[]{:S(2)}) collective-permute-start(bf16[8,96,256]{2,1,0:T(8,128)(2,1)S(1)} %outward.7), channel_id=1, source_target_pairs={{0,8},{1,9},{2,10},{3,11},{4,12},{5,13},{6,14},{7,15},{8,0},{9,1},... | collective-permute-start | bytes 1179656 | tf_op jit(solution)/shard_map/ppermute | solution.py:371
  79.1 7.2 %collective-permute-start.20 = (bf16[4,48,256]{2,1,0:T(8,128)(2,1)S(1)}, bf16[4,48,256]{2,1,0:T(8,128)(2,1)S(1)}, u32[]{:S(2)}, u32[]{:S(2)}) collective-permute-start(bf16[4,48,256]{2,1,0:T(8,128)(2,1)S(1)} %get-tuple-element.58), channel_id=1, source_target_pairs={{0,17},{1,16},{2,19},{3,18},{4,21},{5,20},{6,23},{7,22},{8,25},{9,... | collective-permute-start | bytes 294920 | tf_op jit(solution)/shard_map/ppermute | solution.py:371
  79.4 13.8 %collective-permute-start.21 = (bf16[4,48,256]{2,1,0:T(8,128)(2,1)S(1)}, bf16[4,48,256]{2,1,0:T(8,128)(2,1)S(1)}, u32[]{:S(2)}, u32[]{:S(2)}) collective-permute-start(bf16[4,48,256]{2,1,0:T(8,128)(2,1)S(1)} %get-tuple-element.59), channel_id=1, source_target_pairs={{0,1},{1,0},{2,3},{3,2},{4,5},{5,4},{6,7},{7,6},{8,9},{9,8},{10,11... | collective-permute-start | bytes 294920 | tf_op jit(solution)/shard_map/ppermute | solution.py:371
  82.0 11.3 %collective-permute-start.22 = (bf16[4,48,256]{2,1,0:T(8,128)(2,1)S(1)}, bf16[4,48,256]{2,1,0:T(8,128)(2,1)S(1)}, u32[]{:S(2)}, u32[]{:S(2)}) collective-permute-start(bf16[4,48,256]{2,1,0:T(8,128)(2,1)S(1)} %get-tuple-element.60), channel_id=1, source_target_pairs={{0,16},{1,17},{2,18},{3,19},{4,20},{5,21},{6,22},{7,23},{8,24},{9,... | collective-permute-start | bytes 294920 | tf_op jit(solution)/shard_map/ppermute | solution.py:371
  93.3 23.0 %collective-permute-start.29 = (bf16[4,192,512]{2,1,0:T(8,128)(2,1)S(1)}, bf16[4,192,512]{2,1,0:T(8,128)(2,1)S(1)}, u32[]{:S(2)}, u32[]{:S(2)}) collective-permute-start(bf16[4,192,512]{2,1,0:T(8,128)(2,1)S(1)} %back.5.two_ref.inner_ref.own_ref), channel_id=1, source_target_pairs={{0,1},{1,0},{2,3},{3,2},{4,5},{5,4},{6,7},{7,6},{8,9},{9,8},{10,11... | collective-permute-start | bytes 2359304 | tf_op jit(solution)/shard_map/ppermute | solution.py:437
  95.9 9.4 %collective-permute-start.24 = (bf16[4,48,256]{2,1,0:T(8,128)(2,1)S(1)}, bf16[4,48,256]{2,1,0:T(8,128)(2,1)S(1)}, u32[]{:S(2)}, u32[]{:S(2)}) collective-permute-start(bf16[4,48,256]{2,1,0:T(8,128)(2,1)S(1)} %add.115.refs_0_), channel_id=1, source_target_pairs={{0,4},{1,5},{2,6},{3,7},{4,0},{5,1},{6,2},{7,3},{8,12},{9,13},{10,... | collective-permute-start | bytes 294920 | tf_op jit(solution)/shard_map/ppermute | solution.py:371
  95.9 9.4 %collective-permute-start.25 = (bf16[4,48,256]{2,1,0:T(8,128)(2,1)S(1)}, bf16[4,48,256]{2,1,0:T(8,128)(2,1)S(1)}, u32[]{:S(2)}, u32[]{:S(2)}) collective-permute-start(bf16[4,48,256]{2,1,0:T(8,128)(2,1)S(1)} %add.115.refs_0_), channel_id=1, source_target_pairs={{0,6},{1,7},{2,4},{3,5},{4,2},{5,3},{6,0},{7,1},{8,14},{9,15},{10,... | collective-permute-start | bytes 294920 | tf_op jit(solution)/shard_map/ppermute | solution.py:371
  98.2 8.2 %collective-permute-start.26 = (bf16[4,48,256]{2,1,0:T(8,128)(2,1)S(1)}, bf16[4,48,256]{2,1,0:T(8,128)(2,1)S(1)}, u32[]{:S(2)}, u32[]{:S(2)}) collective-permute-start(bf16[4,48,256]{2,1,0:T(8,128)(2,1)S(1)} %add.115.refs_0_), channel_id=1, source_target_pairs={{0,2},{1,3},{2,0},{3,1},{4,6},{5,7},{6,4},{7,5},{8,10},{9,11},{10,... | collective-permute-start | bytes 294920 | tf_op jit(solution)/shard_map/ppermute | solution.py:371
  106.7 5.4 %collective-permute-start.30 = (bf16[4,48,256]{2,1,0:T(8,128)(2,1)S(1)}, bf16[4,48,256]{2,1,0:T(8,128)(2,1)S(1)}, u32[]{:S(2)}, u32[]{:S(2)}) collective-permute-start(bf16[4,48,256]{2,1,0:T(8,128)(2,1)S(1)} %reflect.3.refs_0_), channel_id=1, source_target_pairs={{0,16},{1,17},{2,18},{3,19},{4,20},{5,21},{6,22},{7,23},{8,24},{9,... | collective-permute-start | bytes 294920 | tf_op jit(solution)/shard_map/ppermute | solution.py:371
  107.1 13.1 %collective-permute-start.27 = (bf16[4,48,256]{2,1,0:T(8,128)(2,1)S(1)}, bf16[4,48,256]{2,1,0:T(8,128)(2,1)S(1)}, u32[]{:S(2)}, u32[]{:S(2)}) collective-permute-start(bf16[4,48,256]{2,1,0:T(8,128)(2,1)S(1)} %reflect.3.refs_0_), channel_id=1, source_target_pairs={{0,17},{1,16},{2,19},{3,18},{4,21},{5,20},{6,23},{7,22},{8,25},{9,... | collective-permute-start | bytes 294920 | tf_op jit(solution)/shard_map/ppermute | solution.py:371
  108.8 11.4 %collective-permute-start.28 = (bf16[4,48,256]{2,1,0:T(8,128)(2,1)S(1)}, bf16[4,48,256]{2,1,0:T(8,128)(2,1)S(1)}, u32[]{:S(2)}, u32[]{:S(2)}) collective-permute-start(bf16[4,48,256]{2,1,0:T(8,128)(2,1)S(1)} %reflect.3.refs_0_), channel_id=1, source_target_pairs={{0,1},{1,0},{2,3},{3,2},{4,5},{5,4},{6,7},{7,6},{8,9},{9,8},{10,11... | collective-permute-start | bytes 294920 | tf_op jit(solution)/shard_map/ppermute | solution.py:371
  110.3 10.5 %collective-permute-start.31 = (bf16[4,48,256]{2,1,0:T(8,128)(2,1)S(1)}, bf16[4,48,256]{2,1,0:T(8,128)(2,1)S(1)}, u32[]{:S(2)}, u32[]{:S(2)}) collective-permute-start(bf16[4,48,256]{2,1,0:T(8,128)(2,1)S(1)} %reflect.3.refs_0_), channel_id=1, source_target_pairs={{0,8},{1,9},{2,10},{3,11},{4,12},{5,13},{6,14},{7,15},{8,0},{9,1},... | collective-permute-start | bytes 294920 | tf_op jit(solution)/shard_map/ppermute | solution.py:371
  112.1 8.7 %collective-permute-start.34 = (bf16[4,48,256]{2,1,0:T(8,128)(2,1)S(1)}, bf16[4,48,256]{2,1,0:T(8,128)(2,1)S(1)}, u32[]{:S(2)}, u32[]{:S(2)}) collective-permute-start(bf16[4,48,256]{2,1,0:T(8,128)(2,1)S(1)} %collective-permute-done.30.refs_3_), channel_id=1, source_target_pairs={{0,8},{1,9},{2,10},{3,11},{4,12},{5,13},{6,14},{7,15},{8,0},{9,1},... | collective-permute-start | bytes 294920 | tf_op jit(solution)/shard_map/ppermute | solution.py:371
  120.2 1.4 %collective-permute-start.32 = (bf16[4,48,256]{2,1,0:T(8,128)(2,1)S(1)}, bf16[4,48,256]{2,1,0:T(8,128)(2,1)S(1)}, u32[]{:S(2)}, u32[]{:S(2)}) collective-permute-start(bf16[4,48,256]{2,1,0:T(8,128)(2,1)S(1)} %collective-permute-done.27.refs_1_), channel_id=1, source_target_pairs={{0,8},{1,9},{2,10},{3,11},{4,12},{5,13},{6,14},{7,15},{8,0},{9,1},... | collective-permute-start | bytes 294920 | tf_op jit(solution)/shard_map/ppermute | solution.py:371
  120.2 1.4 %collective-permute-start.33 = (bf16[4,48,256]{2,1,0:T(8,128)(2,1)S(1)}, bf16[4,48,256]{2,1,0:T(8,128)(2,1)S(1)}, u32[]{:S(2)}, u32[]{:S(2)}) collective-permute-start(bf16[4,48,256]{2,1,0:T(8,128)(2,1)S(1)} %collective-permute-done.28.refs_2_), channel_id=1, source_target_pairs={{0,8},{1,9},{2,10},{3,11},{4,12},{5,13},{6,14},{7,15},{8,0},{9,1},... | collective-permute-start | bytes 294920 | tf_op jit(solution)/shard_map/ppermute | solution.py:371

commit v3 on v2

--- a/solution.py
+++ b/solution.py
@@ -11,6 +11,10 @@
 BF16 = jnp.bfloat16
 LAST = (((1,), (1,)), ((), ()))
 MIB = 1 << 20
+
+
+SCALARS = pl.BlockSpec(memory_space=pltpu.SMEM)
+VECTORS = pl.BlockSpec(memory_space=pltpu.VMEM)
 
 
 def params(mib):
@@ -112,37 +116,51 @@
     )(part, one, two, basis, phases)
 
 
-def split_kernel(place_ref, offsets, levels, keep_ref, got_ref, *out_refs):
-    across = keep_ref.shape[0] // levels
-    for (dx, dy), out_ref in zip(offsets, out_refs):
-        x, y = place_ref[0] ^ dx, place_ref[1] ^ dy
-        for level in range(levels):
-            chunk = level * across + y
-            out_ref[level] = (
+def split_kernel(place_ref, keep_ref, got_ref, here_ref, there_ref):
+    for dx, out_ref in ((0, here_ref), (1, there_ref)):
+        x = place_ref[0] ^ dx
+        for chunk in range(keep_ref.shape[0]):
+            out_ref[chunk] = (
                 keep_ref[chunk, x].astype(F32) + got_ref[chunk, x].astype(F32)
             ).astype(BF16)
 
 
-def split(place, offsets, levels, keep, got):
-    _, _, rows, width = keep.shape
-
-    def body(place_ref, *refs):
-        split_kernel(place_ref, offsets, levels, *refs)
-
-    piece = jax.ShapeDtypeStruct((levels, rows, width), BF16)
-    return pl.pallas_call(
-        body,
-        grid_spec=pltpu.PrefetchScalarGridSpec(
-            num_scalar_prefetch=1,
-            grid=(1,),
-            in_specs=[pl.BlockSpec(keep.shape, lambda i, place: (0, 0, 0, 0))] * 2,
-            out_specs=[pl.BlockSpec(piece.shape, lambda i, place: (0, 0, 0))] * len(offsets),
-        ),
-        out_shape=[piece] * len(offsets),
-        compiler_params=params(8),
+def split(place, keep, got):
+    chunks, _, rows, width = keep.shape
+    return pl.pallas_call(
+        split_kernel,
+        in_specs=[SCALARS, VECTORS, VECTORS],
+        out_specs=[VECTORS] * 2,
+        out_shape=[jax.ShapeDtypeStruct((chunks, rows, width), BF16)] * 2,
+        compiler_params=params(4),
         cost_estimate=cost(keep.size, 6 * keep.size),
         name="split",
     )(place, keep, got)
+
+
+def deal_kernel(place_ref, mine_ref, got_ref, *out_refs):
+    levels = out_refs[0].shape[0]
+    across = mine_ref.shape[0] // levels
+    for dy, out_ref in enumerate(out_refs):
+        for level in range(levels):
+            chunk = level * across + (place_ref[1] ^ dy)
+            out_ref[level] = (
+                mine_ref[chunk].astype(F32) + got_ref[chunk].astype(F32)
+            ).astype(BF16)
+
+
+def deal(place, levels, mine, got):
+    chunks, rows, width = mine.shape
+    across = chunks // levels
+    return pl.pallas_call(
+        deal_kernel,
+        in_specs=[SCALARS, VECTORS, VECTORS],
+        out_specs=[VECTORS] * across,
+        out_shape=[jax.ShapeDtypeStruct((levels, rows, width), BF16)] * across,
+        compiler_params=params(4),
+        cost_estimate=cost(mine.size, 6 * mine.size),
+        name="deal",
+    )(place, mine, got)
 
 
 def add_kernel(*refs):
@@ -373,17 +391,17 @@
     def scalar(*values):
         return jnp.stack([jnp.asarray(v, jnp.int32) for v in values])
 
-    core_mask = blks
-    plane = [(dx, dy) for dx in range(x_lo) for dy in range(y_count) if (dx, dy) != (0, 0)]
-    plane.sort(key=lambda pair: -(pair[0] > 0) - (pair[1] > 0))
-    plane_masks = [dx * 2 * blks + dy for dx, dy in plane]
-    offsets = [(0, 0)] + plane
-    all_offsets = [(dc, dx, dy) for dc in (0, 1) for dx, dy in offsets]
+    core_mask, x_mask = blks, 2 * blks
+    turns = [bin(dy).count("1") % 2 for dy in range(y_count)]
+    y_masks = [turn * x_mask + dy for dy, turn in enumerate(turns)]
+    twist = sum(jnp.where(y == dy, turn, 0) for dy, turn in enumerate(turns))
+    offsets = [(dh, dy) for dh in (0, 1) for dy in range(y_count)]
+    all_offsets = [(dc, dh, dy) for dc in (0, 1) for dh, dy in offsets]
     columns = [
         (h, d) for h in range(x_hi) for d in (2, 3, 1, 0) if d < levels and (h, d) != (0, 0)
     ]
     column_masks = [h * x_lo * 2 * blks + d * y_count for h, d in columns]
-    place = scalar(x, y, core)
+    place = scalar(x ^ twist, y, core)
 
     even = me % 2 == 0
     e_group = jnp.where(even, 1, 0).astype(jnp.int32)
@@ -421,10 +439,11 @@
         got = flip(send, core_mask)
         keep = outward(scalar(core), o_coeffs, e_coeffs, wave_basis, grouped_phases, 2, blks)
         shape = (blks, x_lo, rows, keep.shape[2])
-        pieces = split(place, offsets, levels, keep.reshape(shape), got.reshape(shape))
-        arrived = [flip(piece, mask) for piece, mask in zip(pieces[1:], plane_masks)]
+        mine, theirs = split(place, keep.reshape(shape), got.reshape(shape))
+        pieces = deal(place, levels, mine, flip(theirs, x_mask))
+        arrived = [flip(pieces[dy], y_masks[dy]) for dy in range(1, y_count)]
         if sweep == 0:
-            own_blocks, _ = lax.optimization_barrier((grating_blocks.astype(BF16), pieces[0]))
+            own_blocks, _ = lax.optimization_barrier((grating_blocks.astype(BF16), mine))
             gathered = jnp.zeros((levels,) + own_blocks.shape, BF16)
             gathered = lax.dynamic_update_slice(gathered, own_blocks[None], (z, 0, 0, 0))
             for d in range(1, levels):
@@ -444,8 +463,9 @@
         e_near = near(
             e_first, *e_lists, e_halo, e_coeffs, o_coeffs, incident_t, translations
         )
-        stacks = [stack] + [flip(stack, mask) for mask in plane_masks]
-        late = [n for n, (dx, dy) in enumerate(offsets) if dy]
+        stacks = [stack] + [flip(stack, mask) for mask in y_masks[1:]]
+        stacks = stacks + [flip(piece, x_mask) for piece in stacks]
+        late = [n for n, (dh, dy) in enumerate(offsets) if dh and dy]
         held, e_near = lax.optimization_barrier(([stacks[n] for n in late], e_near))
         for n, piece in zip(late, held):
             stacks[n] = piece

time: 130 us -> 128 us (0.985)
  waiting for transfers between devices: 31.6 us -> 21.8 us
  starting transfers between devices: 43.3 us -> 49.9 us
    ppermute x31 -> x29, starting transfers between devices: 35.9 us -> 45.8 us  [flip(): return lax.ppermute(array, AXES, [(i, i ^ mask) for i in range(devices)])]
    ppermute x31 -> x29, waiting for transfers between devices: 26.1 us -> 20 us  [flip(): return lax.ppermute(array, AXES, [(i, i ^ mask) for i in range(devices)])]
    ppermute x2, waiting for transfers between devices: 5.46 us -> 1.86 us  [local(): e_halo = lax.ppermute(e_sent, AXES, e_pairs)]
    ppermute x2, starting transfers between devices: 5.09 us -> 1.78 us  [local(): e_halo = lax.ppermute(e_sent, AXES, e_pairs)]
    pallas_call x2 -> x4, Pallas kernels: 2.27 us -> 3.02 us  [the longest x2 1.83 us: split(): pl.pallas_call(split_kernel, in_specs=[SCALARS, VECTORS, VECTORS], out_sp...]
  transfers between devices with their start and end apart: 35 -> 33, of which waited for: 14 -> 11; matrix products, arithmetic and copies ran while one was open for 0% -> 0% of each run, Pallas kernels for 26% -> 27%
where the time goes in v3:
time: 128 us; the launch traced here: 127 us
  starting transfers between devices  49.9 us (39%)
  Pallas kernels  48.9 us (38%)
  waiting for transfers between devices  21.8 us (17%)
  local copies, waits for them, and re-layouts  6.17 us (5%)
    ppermute x29, starting transfers between devices, flip(): return lax.ppermute(array, AXES, [(i, i ^ mask) for i in range(devices)])  45.8 us
    ppermute x29, waiting for transfers between devices, flip(): return lax.ppermute(array, AXES, [(i, i ^ mask) for i in range(devices)])  20 us
    pallas_call x4, Pallas kernels, near(): pl.pallas_call(near_kernel, grid_spec=pltpu.PrefetchScalarGridSpec(num_sc...  16.2 us
    pallas_call x4, Pallas kernels, back(): pl.pallas_call(body, grid_spec=pltpu.PrefetchScalarGridSpec(num_scalar_pr...  14.7 us
    pallas_call x4, Pallas kernels, outward(): pl.pallas_call(outward_kernel, grid_spec=pltpu.PrefetchScalarGridSpec(num...  9.2 us
    unnamed x30, local copies, waits for them, and re-layouts  5.9 us
    pallas_call x2, Pallas kernels, solve(): pl.pallas_call(solve_kernel, grid_spec=pltpu.PrefetchScalarGridSpec(num_s...  5.2 us
  transfers between devices with their start and end apart: 33, of which 11 were waited for; matrix products, arithmetic and copies ran while one was open for 0% of the time, Pallas kernels for 27%

profile of v3, /device:TPU:0, one launch (start us, length us, event | category | flops | bytes accessed | tf_op | source)
XLA Modules:
  0.0 127.4 jit_solution(4116058003624117641)
XLA Ops:
  0.0 2.5 %solve.2.one_ref.own_ref.inner_ref = bf16[4,192,512]{2,1,0:T(8,128)(2,1)S(1)} custom-call(s32[1]{0:T(128)} %bitcast.4.first_ref, bf16[8,192,512]{2,1,0:T(8,128)(2,1)} %bitcast.21, bf16[8,512,512]{2,1,0:T(8,128)(2,1)} %refs_11_.7), custom_call_target="tpu_custom_call" | custom-call | flops 1 | bytes 1 | tf_op jit(solution)/shard_map/solve/pallas_call | solution.py:50
  2.5 1.6 %collective-permute-start.3 = (bf16[4,192,512]{2,1,0:T(8,128)(2,1)S(1)}, bf16[4,192,512]{2,1,0:T(8,128)(2,1)}, u32[]{:S(2)}, u32[]{:S(2)}) collective-permute-start(bf16[4,192,512]{2,1,0:T(8,128)(2,1)S(1)} %solve.2.one_ref.own_ref.inner_ref), channel_id=1, source_target_pairs={{1,2},{2,1},{3,4},{4,3},{5,6},{6,5},{7,8},{8,7},{9,10},{10,9},{11,... | collective-permute-start | bytes 2359304 | tf_op jit(solution)/shard_map/ppermute | solution.py:435
  4.1 2.7 %solve.3.two_ref.inner_ref.own_ref = bf16[4,192,512]{2,1,0:T(8,128)(2,1)S(1)} custom-call(s32[1]{0:T(128)} %bitcast.first_ref, bf16[8,192,512]{2,1,0:T(8,128)(2,1)} %bitcast.22, bf16[8,512,512]{2,1,0:T(8,128)(2,1)} %refs_11_.7), custom_call_target="tpu_custom_call" | custom-call | flops 1 | bytes 1 | tf_op jit(solution)/shard_map/solve/pallas_call | solution.py:50
  6.8 0.9 copy-done.5
  7.8 1.1 copy-done.6
  8.9 2.8 %outward.5 = bf16[8,96,256]{2,1,0:T(8,128)(2,1)} custom-call(s32[1]{0:T(128)} %bitcast.7.part_ref, bf16[4,192,512]{2,1,0:T(8,128)(2,1)S(1)} %solve.2.one_ref.own_ref.inner_ref, bf16[4,192,512]{2,1,0:T(8,128)(2,1)S(1)} %copy-done.6, bf16[2048,512]{1,0:T(8,128)(2,1)S(1)} %copy-done.1, bf16[8,2048]{1,0:T(8,128)(2,1)S(1)} %pad_maximum_fusion.phase_ref), custom_call_target="tpu_custom_call" | custom-call | flops 1 | bytes 1 | tf_op jit(solution)/shard_map/outward/pallas_call | solution.py:97
  11.7 6.5 %collective-permute-start = (bf16[8,96,256]{2,1,0:T(8,128)(2,1)}, bf16[8,96,256]{2,1,0:T(8,128)(2,1)}, u32[]{:S(2)}, u32[]{:S(2)}) collective-permute-start(bf16[8,96,256]{2,1,0:T(8,128)(2,1)} %outward.5), channel_id=1, source_target_pairs={{0,8},{1,9},{2,10},{3,11},{4,12},{5,13},{6,14},{7,15},{8,0},{9,1},... | collective-permute-start | bytes 1179656 | tf_op jit(solution)/shard_map/ppermute | solution.py:389
  18.2 1.1 copy-done.7
  19.3 2.1 %outward.4 = bf16[8,96,256]{2,1,0:T(8,128)(2,1)S(1)} custom-call(s32[1]{0:T(128)} %bitcast.3.part_ref, bf16[4,192,512]{2,1,0:T(8,128)(2,1)S(1)} %solve.2.one_ref.own_ref.inner_ref, bf16[4,192,512]{2,1,0:T(8,128)(2,1)S(1)} %copy-done.7, bf16[2048,512]{1,0:T(8,128)(2,1)S(1)} %copy-done.1, bf16[8,2048]{1,0:T(8,128)(2,1)S(1)} %pad_maximum_fusion.phase_ref), custom_call_target="tpu_custom_call" | custom-call | flops 1 | bytes 1 | tf_op jit(solution)/shard_map/outward/pallas_call | solution.py:97
  21.6 0.1 pad_add_fusion.place_ref
  21.7 1.2 split.2
  22.9 1.6 %collective-permute-start.1 = (bf16[8,48,256]{2,1,0:T(8,128)(2,1)S(1)}, bf16[8,48,256]{2,1,0:T(8,128)(2,1)S(1)}, u32[]{:S(2)}, u32[]{:S(2)}) collective-permute-start(bf16[8,48,256]{2,1,0:T(8,128)(2,1)S(1)} %get-tuple-element.34), channel_id=1, source_target_pairs={{0,16},{1,17},{2,18},{3,19},{4,20},{5,21},{6,22},{7,23},{8,24},{9,... | collective-permute-start | bytes 589832 | tf_op jit(solution)/shard_map/ppermute | solution.py:389
  24.6 0.9 collective-permute-start.8
  25.5 3.5 %collective-permute-start.9 = (bf16[2,128,128]{2,1,0:T(8,128)(2,1)S(1)}, bf16[2,128,128]{2,1,0:T(8,128)(2,1)S(1)}, u32[]{:S(2)}, u32[]{:S(2)}) collective-permute-start(bf16[2,128,128]{2,1,0:T(8,128)(2,1)S(1)} %convert_element_type.3), channel_id=1, source_target_pairs={{0,6},{1,7},{2,4},{3,5},{4,2},{5,3},{6,0},{7,1},{8,14},{9,15},{10,... | collective-permute-start | bytes 196616 | tf_op jit(solution)/shard_map/ppermute | solution.py:389
  29.0 0.8 collective-permute-done.1.got_ref
  29.8 0.6 deal.2
  30.4 3.0 %collective-permute-start.2 = (bf16[4,48,256]{2,1,0:T(8,128)(2,1)S(1)}, bf16[4,48,256]{2,1,0:T(8,128)(2,1)S(1)}, u32[]{:S(2)}, u32[]{:S(2)}) collective-permute-start(bf16[4,48,256]{2,1,0:T(8,128)(2,1)S(1)} %get-tuple-element.36), channel_id=1, source_target_pairs={{0,17},{1,16},{2,19},{3,18},{4,21},{5,20},{6,23},{7,22},{8,25},{9,... | collective-permute-start | bytes 294920 | tf_op jit(solution)/shard_map/ppermute | solution.py:389
  33.5 2.8 %collective-permute-done.2.refs_1_ = bf16[4,48,256]{2,1,0:T(8,128)(2,1)S(1)} collective-permute-done((bf16[4,48,256]{2,1,0:T(8,128)(2,1)S(1)}, bf16[4,48,256]{2,1,0:T(8,128)(2,1)S(1)}, u32[]{:S(2)}, u32[]{:S(2)}) %collective-permute-start.2) | collective-permute-done | bytes 98336 | tf_op jit(solution)/shard_map/ppermute | solution.py:389
  36.3 0.8 collective-permute-start.13
  37.2 0.5 collective-permute-start.4
  37.6 3.2 %collective-permute-start.5 = (bf16[4,48,256]{2,1,0:T(8,128)(2,1)S(1)}, bf16[4,48,256]{2,1,0:T(8,128)(2,1)S(1)}, u32[]{:S(2)}, u32[]{:S(2)}) collective-permute-start(bf16[4,48,256]{2,1,0:T(8,128)(2,1)S(1)} %add.115.refs_0_), channel_id=1, source_target_pairs={{0,6},{1,7},{2,4},{3,5},{4,2},{5,3},{6,0},{7,1},{8,14},{9,15},{10,... | collective-permute-start | bytes 294920 | tf_op jit(solution)/shard_map/ppermute | solution.py:389
  40.8 0.5 collective-permute-start.6
  41.4 1.6 %copy-done.3 = bf16[4,512,512]{2,1,0:T(8,128)(2,1)S(1)} copy-done((bf16[4,512,512]{2,1,0:T(8,128)(2,1)S(1)}, bf16[4,512,512]{2,1,0:T(8,128)(2,1)}, u32[]{:S(2)}) %copy-start.3) | copy-done | bytes 2097176
  42.9 1.1 copy-done.8
  44.1 5.1 %near.4.refs_10_ = f32[4,192,512]{2,1,0:T(8,128)S(1)} custom-call(s32[1]{0:T(128)} %bitcast.4.first_ref, s32[4,6]{1,0:T(4,128)S(1)} %constant_dynamic-slice_fusion.3.slot_ref, s32[4]{0:T(128)S(1)} %get-tuple-element.68.count_ref, s32[4,6]{1,0:T(4,128)S(1)} %get-tuple-element.64.type_ref, bf16[4,192,512]{2,1,0:T(8,128)(2,1)} %collective-permute-done.3.halo_ref, ...), custom_call_target="tpu_custom_call" | custom-call | flops 1 | bytes 1 | tf_op jit(solution)/shard_map/near/pallas_call | solution.py:254
  49.2 0.3 reflect.2.refs_0_
  49.5 1.1 collective-permute-start.10
  50.6 2.4 %collective-permute-start.11 = (bf16[4,48,256]{2,1,0:T(8,128)(2,1)S(1)}, bf16[4,48,256]{2,1,0:T(8,128)(2,1)S(1)}, u32[]{:S(2)}, u32[]{:S(2)}) collective-permute-start(bf16[4,48,256]{2,1,0:T(8,128)(2,1)S(1)} %reflect.2.refs_0_), channel_id=1, source_target_pairs={{0,16},{1,17},{2,18},{3,19},{4,20},{5,21},{6,22},{7,23},{8,24},{9,... | collective-permute-start | bytes 294920 | tf_op jit(solution)/shard_map/ppermute | solution.py:389
  53.0 2.2 %collective-permute-done.10.refs_1_ = bf16[4,48,256]{2,1,0:T(8,128)(2,1)S(1)} collective-permute-done((bf16[4,48,256]{2,1,0:T(8,128)(2,1)S(1)}, bf16[4,48,256]{2,1,0:T(8,128)(2,1)S(1)}, u32[]{:S(2)}, u32[]{:S(2)}) %collective-permute-start.10) | collective-permute-done | bytes 98336 | tf_op jit(solution)/shard_map/ppermute | solution.py:389
  55.2 3.0 %collective-permute-start.12 = (bf16[4,48,256]{2,1,0:T(8,128)(2,1)S(1)}, bf16[4,48,256]{2,1,0:T(8,128)(2,1)S(1)}, u32[]{:S(2)}, u32[]{:S(2)}) collective-permute-start(bf16[4,48,256]{2,1,0:T(8,128)(2,1)S(1)} %collective-permute-done.10.refs_1_), channel_id=1, source_target_pairs={{0,16},{1,17},{2,18},{3,19},{4,20},{5,21},{6,22},{7,23},{8,24},{9,... | collective-permute-start | bytes 294920 | tf_op jit(solution)/shard_map/ppermute | solution.py:389
  58.1 0.5 collective-permute-start.15
  58.7 3.7 %near.5.refs_10_ = f32[4,192,512]{2,1,0:T(8,128)S(1)} custom-call(s32[1]{0:T(128)} %bitcast.first_ref, s32[4,6]{1,0:T(4,128)S(1)} %constant_dynamic-slice_fusion.1.slot_ref, s32[4]{0:T(128)S(1)} %get-tuple-element.67.count_ref, s32[4,6]{1,0:T(4,128)S(1)} %get-tuple-element.63.type_ref, bf16[4,192,512]{2,1,0:T(8,128)(2,1)S(1)} %collective-permute-done.13.halo_ref, ...), custom_call_target="tpu_custom_call" | custom-call | flops 1 | bytes 1 | tf_op jit(solution)/shard_map/near/pallas_call | solution.py:254
  62.5 0.6 collective-permute-start.17
  63.1 0.9 collective-permute-done.17.refs_7_
  64.0 3.3 %back.4.one_ref.own_ref.inner_ref = bf16[4,192,512]{2,1,0:T(8,128)(2,1)S(1)} custom-call(s32[1]{0:T(128)} %bitcast.4.first_ref, s32[3]{0:T(128)S(1)} %pad_add_fusion.place_ref, bf16[4,48,256]{2,1,0:T(8,128)(2,1)S(1)} %reflect.2.refs_0_, bf16[4,48,256]{2,1,0:T(8,128)(2,1)S(1)} %collective-permute-done.10.refs_1_, ...), custom_call_target="tpu_custom_call" | custom-call | flops 1 | bytes 1 | tf_op jit(solution)/shard_map/back/pallas_call | solution.py:343
  67.3 0.7 collective-permute-start.21
  68.0 3.3 %back.5.two_ref.inner_ref.own_ref = bf16[4,192,512]{2,1,0:T(8,128)(2,1)S(1)} custom-call(s32[1]{0:T(128)} %bitcast.first_ref, s32[3]{0:T(128)S(1)} %pad_add_fusion.place_ref, bf16[4,48,256]{2,1,0:T(8,128)(2,1)S(1)} %reflect.2.refs_0_, bf16[4,48,256]{2,1,0:T(8,128)(2,1)S(1)} %collective-permute-done.10.refs_1_, ...), custom_call_target="tpu_custom_call" | custom-call | flops 1 | bytes 1 | tf_op jit(solution)/shard_map/back/pallas_call | solution.py:343
  71.3 2.2 %outward.7 = bf16[8,96,256]{2,1,0:T(8,128)(2,1)S(1)} custom-call(s32[1]{0:T(128)} %bitcast.7.part_ref, bf16[4,192,512]{2,1,0:T(8,128)(2,1)S(1)} %back.4.one_ref.own_ref.inner_ref, bf16[4,192,512]{2,1,0:T(8,128)(2,1)S(1)} %back.5.two_ref.inner_ref.own_ref, bf16[2048,512]{1,0:T(8,128)(2,1)S(1)} %copy-done.1, bf16[8,2048]{1,0:T(8,128)(2,1)S(1)} %pad_maximum_fusion.phase_ref), custom_call_target="tpu_custom_call" | custom-call | flops 1 | bytes 1 | tf_op jit(solution)/shard_map/outward/pallas_call | solution.py:97
  73.5 3.7 %collective-permute-start.18 = (bf16[8,96,256]{2,1,0:T(8,128)(2,1)S(1)}, bf16[8,96,256]{2,1,0:T(8,128)(2,1)S(1)}, u32[]{:S(2)}, u32[]{:S(2)}) collective-permute-start(bf16[8,96,256]{2,1,0:T(8,128)(2,1)S(1)} %outward.7), channel_id=1, source_target_pairs={{0,8},{1,9},{2,10},{3,11},{4,12},{5,13},{6,14},{7,15},{8,0},{9,1},... | collective-permute-start | bytes 1179656 | tf_op jit(solution)/shard_map/ppermute | solution.py:389
  77.2 2.1 %outward.6 = bf16[8,96,256]{2,1,0:T(8,128)(2,1)S(1)} custom-call(s32[1]{0:T(128)} %bitcast.3.part_ref, bf16[4,192,512]{2,1,0:T(8,128)(2,1)S(1)} %back.4.one_ref.own_ref.inner_ref, bf16[4,192,512]{2,1,0:T(8,128)(2,1)S(1)} %back.5.two_ref.inner_ref.own_ref, bf16[2048,512]{1,0:T(8,128)(2,1)S(1)} %copy-done.1, bf16[8,2048]{1,0:T(8,128)(2,1)S(1)} %pad_maximum_fusion.phase_ref), custom_call_target="tpu_custom_call" | custom-call | flops 1 | bytes 1 | tf_op jit(solution)/shard_map/outward/pallas_call | solution.py:97
  79.3 0.6 split.3
  79.9 2.3 %collective-permute-start.19 = (bf16[8,48,256]{2,1,0:T(8,128)(2,1)S(1)}, bf16[8,48,256]{2,1,0:T(8,128)(2,1)S(1)}, u32[]{:S(2)}, u32[]{:S(2)}) collective-permute-start(bf16[8,48,256]{2,1,0:T(8,128)(2,1)S(1)} %get-tuple-element.49), channel_id=1, source_target_pairs={{0,16},{1,17},{2,18},{3,19},{4,20},{5,21},{6,22},{7,23},{8,24},{9,... | collective-permute-start | bytes 589832 | tf_op jit(solution)/shard_map/ppermute | solution.py:389
  82.2 5.1 %collective-permute-done.19.got_ref = bf16[8,48,256]{2,1,0:T(8,128)(2,1)S(1)} collective-permute-done((bf16[8,48,256]{2,1,0:T(8,128)(2,1)S(1)}, bf16[8,48,256]{2,1,0:T(8,128)(2,1)S(1)}, u32[]{:S(2)}, u32[]{:S(2)}) %collective-permute-start.19) | collective-permute-done | bytes 196640 | tf_op jit(solution)/shard_map/ppermute | solution.py:389
  87.3 0.6 deal.3
  87.9 3.3 %collective-permute-start.20 = (bf16[4,48,256]{2,1,0:T(8,128)(2,1)S(1)}, bf16[4,48,256]{2,1,0:T(8,128)(2,1)S(1)}, u32[]{:S(2)}, u32[]{:S(2)}) collective-permute-start(bf16[4,48,256]{2,1,0:T(8,128)(2,1)S(1)} %get-tuple-element.51), channel_id=1, source_target_pairs={{0,17},{1,16},{2,19},{3,18},{4,21},{5,20},{6,23},{7,22},{8,25},{9,... | collective-permute-start | bytes 294920 | tf_op jit(solution)/shard_map/ppermute | solution.py:389
  91.3 2.6 %collective-permute-done.20.refs_1_ = bf16[4,48,256]{2,1,0:T(8,128)(2,1)S(1)} collective-permute-done((bf16[4,48,256]{2,1,0:T(8,128)(2,1)S(1)}, bf16[4,48,256]{2,1,0:T(8,128)(2,1)S(1)}, u32[]{:S(2)}, u32[]{:S(2)}) %collective-permute-start.20) | collective-permute-done | bytes 98336 | tf_op jit(solution)/shard_map/ppermute | solution.py:389
  93.9 0.9 collective-permute-start.28
  94.8 0.6 collective-permute-start.22
  95.4 1.6 %collective-permute-start.23 = (bf16[4,48,256]{2,1,0:T(8,128)(2,1)S(1)}, bf16[4,48,256]{2,1,0:T(8,128)(2,1)S(1)}, u32[]{:S(2)}, u32[]{:S(2)}) collective-permute-start(bf16[4,48,256]{2,1,0:T(8,128)(2,1)S(1)} %add.116.refs_0_), channel_id=1, source_target_pairs={{0,6},{1,7},{2,4},{3,5},{4,2},{5,3},{6,0},{7,1},{8,14},{9,15},{10,... | collective-permute-start | bytes 294920 | tf_op jit(solution)/shard_map/ppermute | solution.py:389
  97.1 1.2 collective-permute-start.24
  98.3 3.7 %near.6.refs_10_ = f32[4,192,512]{2,1,0:T(8,128)S(1)} custom-call(s32[1]{0:T(128)} %bitcast.4.first_ref, s32[4,6]{1,0:T(4,128)S(1)} %constant_dynamic-slice_fusion.3.slot_ref, s32[4]{0:T(128)S(1)} %get-tuple-element.68.count_ref, s32[4,6]{1,0:T(4,128)S(1)} %get-tuple-element.64.type_ref, bf16[4,192,512]{2,1,0:T(8,128)(2,1)S(1)} %collective-permute-done.21.halo_ref, ...), custom_call_target="tpu_custom_call" | custom-call | flops 1 | bytes 1 | tf_op jit(solution)/shard_map/near/pallas_call | solution.py:254
  102.0 1.5 %collective-permute-done.22.refs_1_ = bf16[4,48,256]{2,1,0:T(8,128)(2,1)S(1)} collective-permute-done((bf16[4,48,256]{2,1,0:T(8,128)(2,1)S(1)}, bf16[4,48,256]{2,1,0:T(8,128)(2,1)S(1)}, u32[]{:S(2)}, u32[]{:S(2)}) %collective-permute-start.22) | collective-permute-done | bytes 98336 | tf_op jit(solution)/shard_map/ppermute | solution.py:389
  103.5 0.1 collective-permute-done.24.refs_3_
  103.6 0.3 reflect.3.refs_0_
  103.9 1.6 %collective-permute-start.25 = (bf16[4,48,256]{2,1,0:T(8,128)(2,1)S(1)}, bf16[4,48,256]{2,1,0:T(8,128)(2,1)S(1)}, u32[]{:S(2)}, u32[]{:S(2)}) collective-permute-start(bf16[4,48,256]{2,1,0:T(8,128)(2,1)S(1)} %reflect.3.refs_0_), channel_id=1, source_target_pairs={{0,17},{1,16},{2,19},{3,18},{4,21},{5,20},{6,23},{7,22},{8,25},{9,... | collective-permute-start | bytes 294920 | tf_op jit(solution)/shard_map/ppermute | solution.py:389
  105.6 1.3 %collective-permute-start.26 = (bf16[4,48,256]{2,1,0:T(8,128)(2,1)S(1)}, bf16[4,48,256]{2,1,0:T(8,128)(2,1)S(1)}, u32[]{:S(2)}, u32[]{:S(2)}) collective-permute-start(bf16[4,48,256]{2,1,0:T(8,128)(2,1)S(1)} %reflect.3.refs_0_), channel_id=1, source_target_pairs={{0,16},{1,17},{2,18},{3,19},{4,20},{5,21},{6,22},{7,23},{8,24},{9,... | collective-permute-start | bytes 294920 | tf_op jit(solution)/shard_map/ppermute | solution.py:389
  106.9 2.7 %collective-permute-done.25.refs_1_ = bf16[4,48,256]{2,1,0:T(8,128)(2,1)S(1)} collective-permute-done((bf16[4,48,256]{2,1,0:T(8,128)(2,1)S(1)}, bf16[4,48,256]{2,1,0:T(8,128)(2,1)S(1)}, u32[]{:S(2)}, u32[]{:S(2)}) %collective-permute-start.25) | collective-permute-done | bytes 98336 | tf_op jit(solution)/shard_map/ppermute | solution.py:389
  109.6 2.2 %collective-permute-start.27 = (bf16[4,48,256]{2,1,0:T(8,128)(2,1)S(1)}, bf16[4,48,256]{2,1,0:T(8,128)(2,1)S(1)}, u32[]{:S(2)}, u32[]{:S(2)}) collective-permute-start(bf16[4,48,256]{2,1,0:T(8,128)(2,1)S(1)} %collective-permute-done.25.refs_1_), channel_id=1, source_target_pairs={{0,16},{1,17},{2,18},{3,19},{4,20},{5,21},{6,22},{7,23},{8,24},{9,... | collective-permute-start | bytes 294920 | tf_op jit(solution)/shard_map/ppermute | solution.py:389
  111.8 0.5 collective-permute-start.30
  112.4 1.9 %collective-permute-done.28.halo_ref = bf16[4,192,512]{2,1,0:T(8,128)(2,1)S(1)} collective-permute-done((bf16[4,192,512]{2,1,0:T(8,128)(2,1)S(1)}, bf16[4,192,512]{2,1,0:T(8,128)(2,1)S(1)}, u32[]{:S(2)}, u32[]{:S(2)}) %collective-permute-start.28) | collective-permute-done | bytes 786464 | tf_op jit(solution)/shard_map/ppermute | solution.py:456
  114.2 3.7 %near.7.refs_10_ = f32[4,192,512]{2,1,0:T(8,128)S(1)} custom-call(s32[1]{0:T(128)} %bitcast.first_ref, s32[4,6]{1,0:T(4,128)S(1)} %constant_dynamic-slice_fusion.1.slot_ref, s32[4]{0:T(128)S(1)} %get-tuple-element.67.count_ref, s32[4,6]{1,0:T(4,128)S(1)} %get-tuple-element.63.type_ref, bf16[4,192,512]{2,1,0:T(8,128)(2,1)S(1)} %collective-permute-done.28.halo_ref, ...), custom_call_target="tpu_custom_call" | custom-call | flops 1 | bytes 1 | tf_op jit(solution)/shard_map/near/pallas_call | solution.py:254
  118.1 1.3 collective-permute-done.32.refs_7_
  119.3 4.0 %back.6.refs_12_ = bf16[8,192,512]{2,1,0:T(8,128)(2,1)} custom-call(s32[1]{0:T(128)} %bitcast.4.first_ref, s32[3]{0:T(128)S(1)} %pad_add_fusion.place_ref, bf16[4,48,256]{2,1,0:T(8,128)(2,1)S(1)} %reflect.3.refs_0_, bf16[4,48,256]{2,1,0:T(8,128)(2,1)S(1)} %collective-permute-done.25.refs_1_, bf16[4,48,256]{2,1,0:T(8,128)(2,1)S(1)} %collective-permute-done.26.refs_2_, ...), custom_call_target="tpu_custom_call" | custom-call | flops 1 | bytes 1 | tf_op jit(solution)/shard_map/back/pallas_call | solution.py:343
  123.4 4.0 %back.7 = bf16[8,192,512]{2,1,0:T(8,128)(2,1)} custom-call(s32[1]{0:T(128)} %bitcast.first_ref, s32[3]{0:T(128)S(1)} %pad_add_fusion.place_ref, bf16[4,48,256]{2,1,0:T(8,128)(2,1)S(1)} %reflect.3.refs_0_, bf16[4,48,256]{2,1,0:T(8,128)(2,1)S(1)} %collective-permute-done.25.refs_1_, ...), custom_call_target="tpu_custom_call", output_to_operand_aliasing={{}: (14, {})} | custom-call | flops 1 | bytes 1 | tf_op jit(solution)/shard_map/back/pallas_call | solution.py:343
  (69 shorter events, 0.7 us)
Async XLA Ops:
  2.5 33.7 %collective-permute-start.3 = (bf16[4,192,512]{2,1,0:T(8,128)(2,1)S(1)}, bf16[4,192,512]{2,1,0:T(8,128)(2,1)}, u32[]{:S(2)}, u32[]{:S(2)}) collective-permute-start(bf16[4,192,512]{2,1,0:T(8,128)(2,1)S(1)} %solve.2.one_ref.own_ref.inner_ref), channel_id=1, source_target_pairs={{1,2},{2,1},{3,4},{4,3},{5,6},{6,5},{7,8},{8,7},{9,10},{10,9},{11,... | collective-permute-start | bytes 2359304 | tf_op jit(solution)/shard_map/ppermute | solution.py:435
  4.1 3.6 %copy-start.10 = (bf16[8,2048]{1,0:T(8,128)(2,1)S(1)}, bf16[8,2048]{1,0:T(8,128)(2,1)}, u32[]{:S(2)}) copy-start(bf16[8,2048]{1,0:T(8,128)(2,1)} %param.15) | copy-start | bytes 98308
  4.1 3.6 %copy-start.1 = (bf16[2048,512]{1,0:T(8,128)(2,1)S(1)}, bf16[2048,512]{1,0:T(8,128)(2,1)}, u32[]{:S(2)}) copy-start(bf16[2048,512]{1,0:T(8,128)(2,1)} %refs_9_.7) | copy-start | bytes 6291460
  6.8 0.9 copy-start.5
  7.7 1.1 copy-start.6
  11.7 10.0 %collective-permute-start = (bf16[8,96,256]{2,1,0:T(8,128)(2,1)}, bf16[8,96,256]{2,1,0:T(8,128)(2,1)}, u32[]{:S(2)}, u32[]{:S(2)}) collective-permute-start(bf16[8,96,256]{2,1,0:T(8,128)(2,1)} %outward.5), channel_id=1, source_target_pairs={{0,8},{1,9},{2,10},{3,11},{4,12},{5,13},{6,14},{7,15},{8,0},{9,1},... | collective-permute-start | bytes 1179656 | tf_op jit(solution)/shard_map/ppermute | solution.py:389
  18.2 1.1 copy-start.7
  19.3 2.2 %copy-start.11 = (f32[2,128,128]{2,1,0:T(8,128)S(1)}, f32[2,128,128]{2,1,0:T(8,128)}, u32[]{:S(2)}) copy-start(f32[2,128,128]{2,1,0:T(8,128)} %param.17) | copy-start | bytes 393220
  19.3 2.3 %copy-start.12 = (s32[8,6]{1,0:T(8,128)S(1)}, s32[8,6]{1,0:T(8,128)}, u32[]{:S(2)}) copy-start(s32[8,6]{1,0:T(8,128)} %param.12) | copy-start | bytes 580
  19.3 5.1 %copy-start.14 = (s32[8]{0:T(128)S(1)}, s32[8]{0:T(128)}, u32[]{:S(2)}) copy-start(s32[8]{0:T(128)} %param.13) | copy-start | bytes 100
  19.3 5.2 %copy-start.13 = (s32[8,6]{1,0:T(8,128)S(1)}, s32[8,6]{1,0:T(8,128)}, u32[]{:S(2)}) copy-start(s32[8,6]{1,0:T(8,128)} %param.14) | copy-start | bytes 580
  21.6 19.8 %copy-start.2 = (bf16[8,512,192]{1,2,0:T(8,128)(2,1)S(1)}, bf16[8,512,192]{1,2,0:T(8,128)(2,1)}, u32[]{:S(2)}) copy-start(bf16[8,512,192]{1,2,0:T(8,128)(2,1)} %param.9) | copy-start | bytes 4718596
  22.9 6.9 %collective-permute-start.1 = (bf16[8,48,256]{2,1,0:T(8,128)(2,1)S(1)}, bf16[8,48,256]{2,1,0:T(8,128)(2,1)S(1)}, u32[]{:S(2)}, u32[]{:S(2)}) collective-permute-start(bf16[8,48,256]{2,1,0:T(8,128)(2,1)S(1)} %get-tuple-element.34), channel_id=1, source_target_pairs={{0,16},{1,17},{2,18},{3,19},{4,20},{5,21},{6,22},{7,23},{8,24},{9,... | collective-permute-start | bytes 589832 | tf_op jit(solution)/shard_map/ppermute | solution.py:389
  24.5 12.6 %collective-permute-start.7 = (bf16[2,128,128]{2,1,0:T(8,128)(2,1)S(1)}, bf16[2,128,128]{2,1,0:T(8,128)(2,1)S(1)}, u32[]{:S(2)}, u32[]{:S(2)}) collective-permute-start(bf16[2,128,128]{2,1,0:T(8,128)(2,1)S(1)} %convert_element_type.3), channel_id=1, source_target_pairs={{0,2},{1,3},{2,0},{3,1},{4,6},{5,7},{6,4},{7,5},{8,10},{9,11},{10,... | collective-permute-start | bytes 196616 | tf_op jit(solution)/shard_map/ppermute | solution.py:389
  24.6 12.5 %collective-permute-start.8 = (bf16[2,128,128]{2,1,0:T(8,128)(2,1)S(1)}, bf16[2,128,128]{2,1,0:T(8,128)(2,1)S(1)}, u32[]{:S(2)}, u32[]{:S(2)}) collective-permute-start(bf16[2,128,128]{2,1,0:T(8,128)(2,1)S(1)} %convert_element_type.3), channel_id=1, source_target_pairs={{0,4},{1,5},{2,6},{3,7},{4,0},{5,1},{6,2},{7,3},{8,12},{9,13},{10,... | collective-permute-start | bytes 196616 | tf_op jit(solution)/shard_map/ppermute | solution.py:389
  25.5 15.8 %collective-permute-start.9 = (bf16[2,128,128]{2,1,0:T(8,128)(2,1)S(1)}, bf16[2,128,128]{2,1,0:T(8,128)(2,1)S(1)}, u32[]{:S(2)}, u32[]{:S(2)}) collective-permute-start(bf16[2,128,128]{2,1,0:T(8,128)(2,1)S(1)} %convert_element_type.3), channel_id=1, source_target_pairs={{0,6},{1,7},{2,4},{3,5},{4,2},{5,3},{6,0},{7,1},{8,14},{9,15},{10,... | collective-permute-start | bytes 196616 | tf_op jit(solution)/shard_map/ppermute | solution.py:389
  30.4 5.9 %collective-permute-start.2 = (bf16[4,48,256]{2,1,0:T(8,128)(2,1)S(1)}, bf16[4,48,256]{2,1,0:T(8,128)(2,1)S(1)}, u32[]{:S(2)}, u32[]{:S(2)}) collective-permute-start(bf16[4,48,256]{2,1,0:T(8,128)(2,1)S(1)} %get-tuple-element.36), channel_id=1, source_target_pairs={{0,17},{1,16},{2,19},{3,18},{4,21},{5,20},{6,23},{7,22},{8,25},{9,... | collective-permute-start | bytes 294920 | tf_op jit(solution)/shard_map/ppermute | solution.py:389
  36.3 22.5 %collective-permute-start.13 = (bf16[4,192,512]{2,1,0:T(8,128)(2,1)}, bf16[4,192,512]{2,1,0:T(8,128)(2,1)S(1)}, u32[]{:S(2)}, u32[]{:S(2)}) collective-permute-start(bf16[4,192,512]{2,1,0:T(8,128)(2,1)} %copy-done.5), channel_id=1, source_target_pairs={{0,1},{1,0},{2,3},{3,2},{4,5},{5,4},{6,7},{7,6},{8,9},{9,8},{10,11... | collective-permute-start | bytes 2359304 | tf_op jit(solution)/shard_map/ppermute | solution.py:456
  37.2 12.0 %collective-permute-start.4 = (bf16[4,48,256]{2,1,0:T(8,128)(2,1)S(1)}, bf16[4,48,256]{2,1,0:T(8,128)(2,1)S(1)}, u32[]{:S(2)}, u32[]{:S(2)}) collective-permute-start(bf16[4,48,256]{2,1,0:T(8,128)(2,1)S(1)} %add.115.refs_0_), channel_id=1, source_target_pairs={{0,4},{1,5},{2,6},{3,7},{4,0},{5,1},{6,2},{7,3},{8,12},{9,13},{10,... | collective-permute-start | bytes 294920 | tf_op jit(solution)/shard_map/ppermute | solution.py:389
  37.6 11.5 %collective-permute-start.5 = (bf16[4,48,256]{2,1,0:T(8,128)(2,1)S(1)}, bf16[4,48,256]{2,1,0:T(8,128)(2,1)S(1)}, u32[]{:S(2)}, u32[]{:S(2)}) collective-permute-start(bf16[4,48,256]{2,1,0:T(8,128)(2,1)S(1)} %add.115.refs_0_), channel_id=1, source_target_pairs={{0,6},{1,7},{2,4},{3,5},{4,2},{5,3},{6,0},{7,1},{8,14},{9,15},{10,... | collective-permute-start | bytes 294920 | tf_op jit(solution)/shard_map/ppermute | solution.py:389
  40.8 8.4 %collective-permute-start.6 = (bf16[4,48,256]{2,1,0:T(8,128)(2,1)S(1)}, bf16[4,48,256]{2,1,0:T(8,128)(2,1)S(1)}, u32[]{:S(2)}, u32[]{:S(2)}) collective-permute-start(bf16[4,48,256]{2,1,0:T(8,128)(2,1)S(1)} %add.115.refs_0_), channel_id=1, source_target_pairs={{0,2},{1,3},{2,0},{3,1},{4,6},{5,7},{6,4},{7,5},{8,10},{9,11},{10,... | collective-permute-start | bytes 294920 | tf_op jit(solution)/shard_map/ppermute | solution.py:389
  41.3 1.6 %copy-start.3 = (bf16[4,512,512]{2,1,0:T(8,128)(2,1)S(1)}, bf16[4,512,512]{2,1,0:T(8,128)(2,1)}, u32[]{:S(2)}) copy-start(bf16[4,512,512]{2,1,0:T(8,128)(2,1)} %translations_ref.7) | copy-start | bytes 6291460
  42.9 1.1 copy-start.8
  44.1 14.7 %copy-start.4 = (bf16[4,512,512]{2,1,0:T(8,128)(2,1)S(1)}, bf16[4,512,512]{2,1,0:T(8,128)(2,1)}, u32[]{:S(2)}) copy-start(bf16[4,512,512]{2,1,0:T(8,128)(2,1)} %translations_ref.7) | copy-start | bytes 6291460
  44.1 14.7 %copy-start.9 = (bf16[4,192,512]{2,1,0:T(8,128)(2,1)S(1)}, bf16[4,192,512]{2,1,0:T(8,128)(2,1)}, u32[]{:S(2)}) copy-start(bf16[4,192,512]{2,1,0:T(8,128)(2,1)} %copy-done.5) | copy-start | bytes 2359300
  49.5 5.7 %collective-permute-start.10 = (bf16[4,48,256]{2,1,0:T(8,128)(2,1)S(1)}, bf16[4,48,256]{2,1,0:T(8,128)(2,1)S(1)}, u32[]{:S(2)}, u32[]{:S(2)}) collective-permute-start(bf16[4,48,256]{2,1,0:T(8,128)(2,1)S(1)} %reflect.2.refs_0_), channel_id=1, source_target_pairs={{0,17},{1,16},{2,19},{3,18},{4,21},{5,20},{6,23},{7,22},{8,25},{9,... | collective-permute-start | bytes 294920 | tf_op jit(solution)/shard_map/ppermute | solution.py:389
  50.6 8.1 %collective-permute-start.11 = (bf16[4,48,256]{2,1,0:T(8,128)(2,1)S(1)}, bf16[4,48,256]{2,1,0:T(8,128)(2,1)S(1)}, u32[]{:S(2)}, u32[]{:S(2)}) collective-permute-start(bf16[4,48,256]{2,1,0:T(8,128)(2,1)S(1)} %reflect.2.refs_0_), channel_id=1, source_target_pairs={{0,16},{1,17},{2,18},{3,19},{4,20},{5,21},{6,22},{7,23},{8,24},{9,... | collective-permute-start | bytes 294920 | tf_op jit(solution)/shard_map/ppermute | solution.py:389
  55.2 7.3 %collective-permute-start.12 = (bf16[4,48,256]{2,1,0:T(8,128)(2,1)S(1)}, bf16[4,48,256]{2,1,0:T(8,128)(2,1)S(1)}, u32[]{:S(2)}, u32[]{:S(2)}) collective-permute-start(bf16[4,48,256]{2,1,0:T(8,128)(2,1)S(1)} %collective-permute-done.10.refs_1_), channel_id=1, source_target_pairs={{0,16},{1,17},{2,18},{3,19},{4,20},{5,21},{6,22},{7,23},{8,24},{9,... | collective-permute-start | bytes 294920 | tf_op jit(solution)/shard_map/ppermute | solution.py:389
  58.1 5.0 %collective-permute-start.14 = (bf16[4,48,256]{2,1,0:T(8,128)(2,1)S(1)}, bf16[4,48,256]{2,1,0:T(8,128)(2,1)S(1)}, u32[]{:S(2)}, u32[]{:S(2)}) collective-permute-start(bf16[4,48,256]{2,1,0:T(8,128)(2,1)S(1)} %reflect.2.refs_0_), channel_id=1, source_target_pairs={{0,8},{1,9},{2,10},{3,11},{4,12},{5,13},{6,14},{7,15},{8,0},{9,1},... | collective-permute-start | bytes 294920 | tf_op jit(solution)/shard_map/ppermute | solution.py:389
  58.1 5.0 %collective-permute-start.15 = (bf16[4,48,256]{2,1,0:T(8,128)(2,1)S(1)}, bf16[4,48,256]{2,1,0:T(8,128)(2,1)S(1)}, u32[]{:S(2)}, u32[]{:S(2)}) collective-permute-start(bf16[4,48,256]{2,1,0:T(8,128)(2,1)S(1)} %collective-permute-done.10.refs_1_), channel_id=1, source_target_pairs={{0,8},{1,9},{2,10},{3,11},{4,12},{5,13},{6,14},{7,15},{8,0},{9,1},... | collective-permute-start | bytes 294920 | tf_op jit(solution)/shard_map/ppermute | solution.py:389
  58.7 4.5 %collective-permute-start.16 = (bf16[4,48,256]{2,1,0:T(8,128)(2,1)S(1)}, bf16[4,48,256]{2,1,0:T(8,128)(2,1)S(1)}, u32[]{:S(2)}, u32[]{:S(2)}) collective-permute-start(bf16[4,48,256]{2,1,0:T(8,128)(2,1)S(1)} %collective-permute-done.11.refs_2_), channel_id=1, source_target_pairs={{0,8},{1,9},{2,10},{3,11},{4,12},{5,13},{6,14},{7,15},{8,0},{9,1},... | collective-permute-start | bytes 294920 | tf_op jit(solution)/shard_map/ppermute | solution.py:389
  58.7 5.2 %copy-start = (bf16[8,512,512]{2,1,0:T(8,128)(2,1)S(1)}, bf16[8,512,512]{2,1,0:T(8,128)(2,1)}, u32[]{:S(2)}) copy-start(bf16[8,512,512]{2,1,0:T(8,128)(2,1)} %refs_11_.7) | copy-start | bytes 12582916
  62.5 1.5 %collective-permute-start.17 = (bf16[4,48,256]{2,1,0:T(8,128)(2,1)S(1)}, bf16[4,48,256]{2,1,0:T(8,128)(2,1)S(1)}, u32[]{:S(2)}, u32[]{:S(2)}) collective-permute-start(bf16[4,48,256]{2,1,0:T(8,128)(2,1)S(1)} %collective-permute-done.12.refs_3_), channel_id=1, source_target_pairs={{0,8},{1,9},{2,10},{3,11},{4,12},{5,13},{6,14},{7,15},{8,0},{9,1},... | collective-permute-start | bytes 294920 | tf_op jit(solution)/shard_map/ppermute | solution.py:389
  67.3 26.6 %collective-permute-start.21 = (bf16[4,192,512]{2,1,0:T(8,128)(2,1)S(1)}, bf16[4,192,512]{2,1,0:T(8,128)(2,1)S(1)}, u32[]{:S(2)}, u32[]{:S(2)}) collective-permute-start(bf16[4,192,512]{2,1,0:T(8,128)(2,1)S(1)} %back.4.one_ref.own_ref.inner_ref), channel_id=1, source_target_pairs={{1,2},{2,1},{3,4},{4,3},{5,6},{6,5},{7,8},{8,7},{9,10},{10,9},{11,... | collective-permute-start | bytes 2359304 | tf_op jit(solution)/shard_map/ppermute | solution.py:435
  73.5 5.8 %collective-permute-start.18 = (bf16[8,96,256]{2,1,0:T(8,128)(2,1)S(1)}, bf16[8,96,256]{2,1,0:T(8,128)(2,1)S(1)}, u32[]{:S(2)}, u32[]{:S(2)}) collective-permute-start(bf16[8,96,256]{2,1,0:T(8,128)(2,1)S(1)} %outward.7), channel_id=1, source_target_pairs={{0,8},{1,9},{2,10},{3,11},{4,12},{5,13},{6,14},{7,15},{8,0},{9,1},... | collective-permute-start | bytes 1179656 | tf_op jit(solution)/shard_map/ppermute | solution.py:389
  79.9 7.4 %collective-permute-start.19 = (bf16[8,48,256]{2,1,0:T(8,128)(2,1)S(1)}, bf16[8,48,256]{2,1,0:T(8,128)(2,1)S(1)}, u32[]{:S(2)}, u32[]{:S(2)}) collective-permute-start(bf16[8,48,256]{2,1,0:T(8,128)(2,1)S(1)} %get-tuple-element.49), channel_id=1, source_target_pairs={{0,16},{1,17},{2,18},{3,19},{4,20},{5,21},{6,22},{7,23},{8,24},{9,... | collective-permute-start | bytes 589832 | tf_op jit(solution)/shard_map/ppermute | solution.py:389
  87.9 5.9 %collective-permute-start.20 = (bf16[4,48,256]{2,1,0:T(8,128)(2,1)S(1)}, bf16[4,48,256]{2,1,0:T(8,128)(2,1)S(1)}, u32[]{:S(2)}, u32[]{:S(2)}) collective-permute-start(bf16[4,48,256]{2,1,0:T(8,128)(2,1)S(1)} %get-tuple-element.51), channel_id=1, source_target_pairs={{0,17},{1,16},{2,19},{3,18},{4,21},{5,20},{6,23},{7,22},{8,25},{9,... | collective-permute-start | bytes 294920 | tf_op jit(solution)/shard_map/ppermute | solution.py:389
  93.9 20.3 %collective-permute-start.28 = (bf16[4,192,512]{2,1,0:T(8,128)(2,1)S(1)}, bf16[4,192,512]{2,1,0:T(8,128)(2,1)S(1)}, u32[]{:S(2)}, u32[]{:S(2)}) collective-permute-start(bf16[4,192,512]{2,1,0:T(8,128)(2,1)S(1)} %back.5.two_ref.inner_ref.own_ref), channel_id=1, source_target_pairs={{0,1},{1,0},{2,3},{3,2},{4,5},{5,4},{6,7},{7,6},{8,9},{9,8},{10,11... | collective-permute-start | bytes 2359304 | tf_op jit(solution)/shard_map/ppermute | solution.py:456
  94.8 8.7 %collective-permute-start.22 = (bf16[4,48,256]{2,1,0:T(8,128)(2,1)S(1)}, bf16[4,48,256]{2,1,0:T(8,128)(2,1)S(1)}, u32[]{:S(2)}, u32[]{:S(2)}) collective-permute-start(bf16[4,48,256]{2,1,0:T(8,128)(2,1)S(1)} %add.116.refs_0_), channel_id=1, source_target_pairs={{0,4},{1,5},{2,6},{3,7},{4,0},{5,1},{6,2},{7,3},{8,12},{9,13},{10,... | collective-permute-start | bytes 294920 | tf_op jit(solution)/shard_map/ppermute | solution.py:389
  95.4 8.1 %collective-permute-start.23 = (bf16[4,48,256]{2,1,0:T(8,128)(2,1)S(1)}, bf16[4,48,256]{2,1,0:T(8,128)(2,1)S(1)}, u32[]{:S(2)}, u32[]{:S(2)}) collective-permute-start(bf16[4,48,256]{2,1,0:T(8,128)(2,1)S(1)} %add.116.refs_0_), channel_id=1, source_target_pairs={{0,6},{1,7},{2,4},{3,5},{4,2},{5,3},{6,0},{7,1},{8,14},{9,15},{10,... | collective-permute-start | bytes 294920 | tf_op jit(solution)/shard_map/ppermute | solution.py:389
  97.1 6.6 %collective-permute-start.24 = (bf16[4,48,256]{2,1,0:T(8,128)(2,1)S(1)}, bf16[4,48,256]{2,1,0:T(8,128)(2,1)S(1)}, u32[]{:S(2)}, u32[]{:S(2)}) collective-permute-start(bf16[4,48,256]{2,1,0:T(8,128)(2,1)S(1)} %add.116.refs_0_), channel_id=1, source_target_pairs={{0,2},{1,3},{2,0},{3,1},{4,6},{5,7},{6,4},{7,5},{8,10},{9,11},{10,... | collective-permute-start | bytes 294920 | tf_op jit(solution)/shard_map/ppermute | solution.py:389
  103.9 5.7 %collective-permute-start.25 = (bf16[4,48,256]{2,1,0:T(8,128)(2,1)S(1)}, bf16[4,48,256]{2,1,0:T(8,128)(2,1)S(1)}, u32[]{:S(2)}, u32[]{:S(2)}) collective-permute-start(bf16[4,48,256]{2,1,0:T(8,128)(2,1)S(1)} %reflect.3.refs_0_), channel_id=1, source_target_pairs={{0,17},{1,16},{2,19},{3,18},{4,21},{5,20},{6,23},{7,22},{8,25},{9,... | collective-permute-start | bytes 294920 | tf_op jit(solution)/shard_map/ppermute | solution.py:389
  105.6 6.8 %collective-permute-start.26 = (bf16[4,48,256]{2,1,0:T(8,128)(2,1)S(1)}, bf16[4,48,256]{2,1,0:T(8,128)(2,1)S(1)}, u32[]{:S(2)}, u32[]{:S(2)}) collective-permute-start(bf16[4,48,256]{2,1,0:T(8,128)(2,1)S(1)} %reflect.3.refs_0_), channel_id=1, source_target_pairs={{0,16},{1,17},{2,18},{3,19},{4,20},{5,21},{6,22},{7,23},{8,24},{9,... | collective-permute-start | bytes 294920 | tf_op jit(solution)/shard_map/ppermute | solution.py:389
  109.6 8.3 %collective-permute-start.27 = (bf16[4,48,256]{2,1,0:T(8,128)(2,1)S(1)}, bf16[4,48,256]{2,1,0:T(8,128)(2,1)S(1)}, u32[]{:S(2)}, u32[]{:S(2)}) collective-permute-start(bf16[4,48,256]{2,1,0:T(8,128)(2,1)S(1)} %collective-permute-done.25.refs_1_), channel_id=1, source_target_pairs={{0,16},{1,17},{2,18},{3,19},{4,20},{5,21},{6,22},{7,23},{8,24},{9,... | collective-permute-start | bytes 294920 | tf_op jit(solution)/shard_map/ppermute | solution.py:389
  111.8 6.2 %collective-permute-start.29 = (bf16[4,48,256]{2,1,0:T(8,128)(2,1)S(1)}, bf16[4,48,256]{2,1,0:T(8,128)(2,1)S(1)}, u32[]{:S(2)}, u32[]{:S(2)}) collective-permute-start(bf16[4,48,256]{2,1,0:T(8,128)(2,1)S(1)} %reflect.3.refs_0_), channel_id=1, source_target_pairs={{0,8},{1,9},{2,10},{3,11},{4,12},{5,13},{6,14},{7,15},{8,0},{9,1},... | collective-permute-start | bytes 294920 | tf_op jit(solution)/shard_map/ppermute | solution.py:389
  111.8 6.2 %collective-permute-start.30 = (bf16[4,48,256]{2,1,0:T(8,128)(2,1)S(1)}, bf16[4,48,256]{2,1,0:T(8,128)(2,1)S(1)}, u32[]{:S(2)}, u32[]{:S(2)}) collective-permute-start(bf16[4,48,256]{2,1,0:T(8,128)(2,1)S(1)} %collective-permute-done.25.refs_1_), channel_id=1, source_target_pairs={{0,8},{1,9},{2,10},{3,11},{4,12},{5,13},{6,14},{7,15},{8,0},{9,1},... | collective-permute-start | bytes 294920 | tf_op jit(solution)/shard_map/ppermute | solution.py:389
  112.4 5.7 %collective-permute-start.31 = (bf16[4,48,256]{2,1,0:T(8,128)(2,1)S(1)}, bf16[4,48,256]{2,1,0:T(8,128)(2,1)S(1)}, u32[]{:S(2)}, u32[]{:S(2)}) collective-permute-start(bf16[4,48,256]{2,1,0:T(8,128)(2,1)S(1)} %collective-permute-done.26.refs_2_), channel_id=1, source_target_pairs={{0,8},{1,9},{2,10},{3,11},{4,12},{5,13},{6,14},{7,15},{8,0},{9,1},... | collective-permute-start | bytes 294920 | tf_op jit(solution)/shard_map/ppermute | solution.py:389
  118.0 1.4 %collective-permute-start.32 = (bf16[4,48,256]{2,1,0:T(8,128)(2,1)S(1)}, bf16[4,48,256]{2,1,0:T(8,128)(2,1)S(1)}, u32[]{:S(2)}, u32[]{:S(2)}) collective-permute-start(bf16[4,48,256]{2,1,0:T(8,128)(2,1)S(1)} %collective-permute-done.27.refs_3_), channel_id=1, source_target_pairs={{0,8},{1,9},{2,10},{3,11},{4,12},{5,13},{6,14},{7,15},{8,0},{9,1},... | collective-permute-start | bytes 294920 | tf_op jit(solution)/shard_map/ppermute | solution.py:389

commit v4 on v3

--- a/solution.py
+++ b/solution.py
@@ -15,13 +15,16 @@
 
 SCALARS = pl.BlockSpec(memory_space=pltpu.SMEM)
 VECTORS = pl.BlockSpec(memory_space=pltpu.VMEM)
+ANYWHERE = pl.BlockSpec(memory_space=pl.ANY)
 
 
 def params(mib):
     return pltpu.CompilerParams(vmem_limit_bytes=mib * MIB)
 
 
-def cost(macs, moved):
+def cost(macs, moved, real=False):
+    if real:
+        return pl.CostEstimate(flops=2 * macs, bytes_accessed=moved, transcendentals=0)
     return pl.CostEstimate(flops=1, bytes_accessed=1, transcendentals=0)
 
 
@@ -67,53 +70,41 @@
     )(first, source, t_matrices)
 
 
-def outward_kernel(part_ref, one_ref, two_ref, basis_ref, phase_ref, out_ref):
-    half, rows, size = one_ref.shape
-    chunks, _, chunk = out_ref.shape
-    width = basis_ref.shape[0]
-    total = jnp.zeros((rows, width), F32)
-    for index, ref in ((0, one_ref), (half, two_ref)):
+def outward_kernel(part_ref, *refs):
+    pieces, (basis_ref, phase_ref, out_ref) = refs[:-3], refs[-3:]
+    chunks, rows, chunk = out_ref.shape
+    total_rows, size = basis_ref.shape
+    width = min(1024, total_rows)
+    start = pl.multiple_of(part_ref[0] * rows, 16)
+    source = jnp.concatenate(
+        [ref[:, pl.ds(start, rows), :].reshape(-1, size) for ref in pieces], axis=0
+    )
+    for g in range(0, total_rows, width):
         spread = lax.dot_general(
-            ref[...].reshape(half * rows, size),
-            basis_ref[...],
-            LAST,
-            preferred_element_type=F32,
-        )
-        for p in range(half):
-            phase = phase_ref[index + p, :].astype(F32)[None, :]
-            total = total + phase * spread[p * rows : (p + 1) * rows]
-    total = total.astype(BF16)
-    for c in range(chunks):
-        out_ref[c] = total[:, c * chunk : (c + 1) * chunk]
-
-
-def outward(part, one, two, basis, phases, parts, chunks):
-    half, m, size = one.shape
-    total_rows = basis.shape[0]
+            source, basis_ref[g : g + width, :], LAST, preferred_element_type=F32
+        )
+        total = phase_ref[0:1, g : g + width] * spread[:rows]
+        for p in range(1, phase_ref.shape[0]):
+            total = total + phase_ref[p : p + 1, g : g + width] * spread[p * rows : (p + 1) * rows]
+        total = total.astype(BF16)
+        for c in range(0, width, chunk):
+            out_ref[(g + c) // chunk] = total[:, c : c + chunk]
+
+
+def outward(part, pieces, basis, phases, parts, chunks):
+    m, size = pieces[0].shape[1:]
+    count, total_rows = phases.shape
     chunk = total_rows // chunks
-    steps = 2
-    width = total_rows // steps
     rows = m // parts
     return pl.pallas_call(
         outward_kernel,
-        grid_spec=pltpu.PrefetchScalarGridSpec(
-            num_scalar_prefetch=1,
-            grid=(steps,),
-            in_specs=[
-                pl.BlockSpec((half, rows, size), lambda g, part: (0, part[0], 0)),
-                pl.BlockSpec((half, rows, size), lambda g, part: (0, part[0], 0)),
-                pl.BlockSpec((width, size), lambda g, part: (g, 0)),
-                pl.BlockSpec((2 * half, width), lambda g, part: (0, g)),
-            ],
-            out_specs=pl.BlockSpec((chunks // steps, rows, chunk), lambda g, part: (g, 0, 0)),
-        ),
+        in_specs=[SCALARS] + [VECTORS] * (len(pieces) + 2),
+        out_specs=VECTORS,
         out_shape=jax.ShapeDtypeStruct((chunks, rows, chunk), BF16),
-        compiler_params=params(24),
-        cost_estimate=cost(
-            2 * half * rows * size * total_rows, 2 * size * (total_rows + 2 * half * rows)
-        ),
+        compiler_params=params(16),
+        cost_estimate=cost(count * rows * size * total_rows, 2 * size * total_rows),
         name="outward",
-    )(part, one, two, basis, phases)
+    )(part, *pieces, basis, phases)
 
 
 def split_kernel(place_ref, keep_ref, got_ref, here_ref, there_ref):
@@ -278,9 +269,10 @@
 
 def back_kernel(first_ref, place_ref, offsets, refs):
     pieces = refs[: len(offsets)]
-    phase_ref, basis_ref, partial_ref, t_ref = refs[len(offsets) : len(offsets) + 4]
+    phase_ref, basis_ref, t_ref = refs[len(offsets) : len(offsets) + 3]
+    partials = refs[len(offsets) + 3 : -2]
     out_ref, waves = refs[-2:]
-    group, m, size = partial_ref.shape
+    group, m, size = out_ref.shape
     chunks, parts, rows, width = waves.shape
     levels = pieces[0].shape[0]
     across = chunks // levels
@@ -292,7 +284,10 @@
             for level in range(levels):
                 waves[level * across + (place_ref[1] ^ dy), part] = piece[level]
 
-    total = partial_ref[...].reshape(group * m, size)
+    total = partials[0][...]
+    if len(partials) > 1:
+        total = jnp.where(pl.program_id(0) // 2 == first_ref[0], total, partials[1][...])
+    total = total.reshape(group * m, size)
     for c in range(chunks):
         waves_here = waves[c].reshape(m, width)
         weighted = [
@@ -310,53 +305,42 @@
         ).astype(BF16)
 
 
-def back(first, place, offsets, pieces, chunks, parts, phases, basis, partial, t_matrices, whole, onto=None):
-    count, m, size = partial.shape
+def back(first, place, offsets, pieces, chunks, parts, phases, basis, t_matrices, partials):
+    count, m, size = partials[0].shape
     levels, rows, width = pieces[0].shape
     total_rows = basis.shape[0]
     group = 2
-    steps = count // group
+    steps = count // group * len(partials)
 
     def body(first_ref, place_ref, *refs):
-        if onto is not None:
-            refs = refs[: len(offsets) + 4] + refs[len(offsets) + 5 :]
         back_kernel(first_ref, place_ref, offsets, refs)
 
     def here(p, first, place):
-        return (first[0] * steps + p, 0, 0)
-
-    def local_here(p, first, place):
-        return (p, 0, 0)
-
-    in_specs = [pl.BlockSpec((levels, rows, width), lambda p, *_: (0, 0, 0))] * len(pieces) + [
-        pl.BlockSpec((group, 1, total_rows), here),
-        pl.BlockSpec((total_rows, size), lambda p, *_: (0, 0)),
-        pl.BlockSpec((group, m, size), local_here),
-        pl.BlockSpec((group, size, size), here),
-    ]
-    operands = [first, place, *pieces, phases, basis, partial, t_matrices]
-    aliases = {}
-    if onto is not None:
-        in_specs.append(pl.BlockSpec(memory_space=pl.ANY))
-        aliases = {len(operands): 0}
-        operands.append(onto)
+        return (first[0] * steps + p if len(partials) == 1 else p, 0, 0)
+
     return pl.pallas_call(
         body,
         grid_spec=pltpu.PrefetchScalarGridSpec(
             num_scalar_prefetch=2,
             grid=(steps,),
-            in_specs=in_specs,
-            out_specs=pl.BlockSpec((group, m, size), here if whole else local_here),
+            in_specs=[pl.BlockSpec((levels, rows, width), lambda p, *_: (0, 0, 0))] * len(pieces)
+            + [
+                pl.BlockSpec((group, 1, total_rows), here),
+                pl.BlockSpec((total_rows, size), lambda p, *_: (0, 0)),
+                pl.BlockSpec((group, size, size), here),
+            ]
+            + [pl.BlockSpec((group, m, size), lambda p, *_: (p % (count // group), 0, 0))]
+            * len(partials),
+            out_specs=pl.BlockSpec((group, m, size), lambda p, *_: (p, 0, 0)),
             scratch_shapes=[pltpu.VMEM((chunks, parts, rows, width), BF16)],
         ),
-        out_shape=jax.ShapeDtypeStruct((2 * count if whole else count, m, size), BF16),
-        input_output_aliases=aliases,
+        out_shape=jax.ShapeDtypeStruct((steps * group, m, size), BF16),
         compiler_params=params(32),
         cost_estimate=cost(
             count * m * size * (total_rows + size), 2 * size * (total_rows + count * size)
         ),
         name="back",
-    )(*operands)
+    )(first, place, *pieces, phases, basis, t_matrices, *partials)
 
 
 def local(
@@ -426,18 +410,18 @@
     grouped_phases = jnp.concatenate(
         [lax.dynamic_slice_in_dim(phases, g * reach, reach, axis=0) for g in (o_group, e_group)],
         axis=0,
-    )
+    ).astype(F32)
 
     held = [pltpu.with_memory_space_constraint(a, pltpu.HBM) for a in (incident_t, t_matrices)]
     o_coeffs = solve(o_first, *held, reach)
     e_coeffs = solve(e_first, *held, reach)
     for sweep in range(ITERS):
+        last = sweep == ITERS - 1
         o_halo = lax.ppermute(o_coeffs, AXES, o_pairs)
-        send = outward(
-            scalar(1 - core), o_coeffs, e_coeffs, wave_basis, grouped_phases, 2, blks
-        )
+        common = ((o_coeffs, e_coeffs), wave_basis, grouped_phases, 2, blks)
+        send = outward(scalar(1 - core), *common)
         got = flip(send, core_mask)
-        keep = outward(scalar(core), o_coeffs, e_coeffs, wave_basis, grouped_phases, 2, blks)
+        keep = outward(scalar(core), *common)
         shape = (blks, x_lo, rows, keep.shape[2])
         mine, theirs = split(place, keep.reshape(shape), got.reshape(shape))
         pieces = deal(place, levels, mine, flip(theirs, x_mask))
@@ -460,25 +444,27 @@
         arrived = [flip(plane_sum, mask) for mask in column_masks]
         arrived, o_near = lax.optimization_barrier((arrived, o_near))
         stack = reflect([plane_sum, *arrived], gathered)
+        stacks = [stack] + [flip(stack, mask) for mask in y_masks[1:]]
+        stacks = stacks + [flip(piece, x_mask) for piece in stacks]
+        if last:
+            stacks = stacks + [flip(piece, core_mask) for piece in stacks]
         e_near = near(
             e_first, *e_lists, e_halo, e_coeffs, o_coeffs, incident_t, translations
         )
-        stacks = [stack] + [flip(stack, mask) for mask in y_masks[1:]]
-        stacks = stacks + [flip(piece, x_mask) for piece in stacks]
-        late = [n for n, (dh, dy) in enumerate(offsets) if dh and dy]
-        held, e_near = lax.optimization_barrier(([stacks[n] for n in late], e_near))
-        for n, piece in zip(late, held):
-            stacks[n] = piece
-        stacks = stacks + [flip(piece, core_mask) for piece in stacks]
-        last = sweep == ITERS - 1
-        common = (place, all_offsets, stacks, blks, parts, phase_rows, wave_basis)
-        o_coeffs = back(o_first, *common, o_near, t_matrices, last)
         if not last:
+            late = [n for n, (dh, dy) in enumerate(offsets) if dh and dy]
+            held, e_near = lax.optimization_barrier(([stacks[n] for n in late], e_near))
+            for n, piece in zip(late, held):
+                stacks[n] = piece
+            stacks = stacks + [flip(piece, core_mask) for piece in stacks]
+        common = (place, all_offsets, stacks, blks, parts, phase_rows, wave_basis, t_matrices)
+        if last:
+            coeffs = back(o_first, *common, (o_near, e_near))
+        else:
+            o_coeffs = back(o_first, *common, (o_near,))
             e_near, _ = lax.optimization_barrier((e_near, o_coeffs))
-        e_coeffs = back(
-            e_first, *common, e_near, t_matrices, last, o_coeffs if last else None
-        )
-    return jnp.swapaxes(e_coeffs, 1, 2)
+            e_coeffs = back(e_first, *common, (e_near,))
+    return jnp.swapaxes(coeffs, 1, 2)
 
 
 def solution(mesh):

time: 128 us -> 126 us (0.984)
  Pallas kernels: 48.9 us -> 46.6 us
  starting transfers between devices: 49.9 us -> 47.9 us
    ppermute x29, waiting for transfers between devices: 20 us -> 22.8 us  [flip(): return lax.ppermute(array, AXES, [(i, i ^ mask) for i in range(devices)])]
    ppermute x2, waiting for transfers between devices: 1.86 us -> 0.01 us  [local(): e_halo = lax.ppermute(e_sent, AXES, e_pairs)]
    ppermute x29, starting transfers between devices: 45.8 us -> 44.4 us  [flip(): return lax.ppermute(array, AXES, [(i, i ^ mask) for i in range(devices)])]
    pallas_call x4 -> x3, Pallas kernels: 14.7 us -> 13.4 us  [back(): pl.pallas_call(body, grid_spec=pltpu.PrefetchScalarGridSpec(num_scalar_pr...]
    unnamed x30 -> x28, local copies, waits for them, and re-layouts: 5.9 us -> 5.89 us
  transfers between devices with their start and end apart: 33 -> 33, of which waited for: 11 -> 10; matrix products, arithmetic and copies ran while one was open for 0% -> 1% of each run, Pallas kernels for 27% -> 27%
where the time goes in v4:
time: 126 us; the launch traced here: 125 us
  starting transfers between devices  47.9 us (38%)
  Pallas kernels  46.6 us (37%)
  waiting for transfers between devices  22.8 us (18%)
  local copies, waits for them, and re-layouts  6.16 us (5%)
    ppermute x29, starting transfers between devices, flip(): return lax.ppermute(array, AXES, [(i, i ^ mask) for i in range(devices)])  44.4 us
    ppermute x29, waiting for transfers between devices, flip(): return lax.ppermute(array, AXES, [(i, i ^ mask) for i in range(devices)])  22.8 us
    pallas_call x4, Pallas kernels, near(): pl.pallas_call(near_kernel, grid_spec=pltpu.PrefetchScalarGridSpec(num_sc...  16.3 us
    pallas_call x3, Pallas kernels, back(): pl.pallas_call(body, grid_spec=pltpu.PrefetchScalarGridSpec(num_scalar_pr...  13.4 us
    pallas_call x4, Pallas kernels, outward(): pl.pallas_call(outward_kernel, in_specs=[SCALARS] + [VECTORS] * (len(piec...  8.15 us
    unnamed x28, local copies, waits for them, and re-layouts  5.89 us
    pallas_call x2, Pallas kernels, solve(): pl.pallas_call(solve_kernel, grid_spec=pltpu.PrefetchScalarGridSpec(num_s...  5.2 us
  transfers between devices with their start and end apart: 33, of which 10 were waited for; matrix products, arithmetic and copies ran while one was open for 1% of the time, Pallas kernels for 27%

profile of v4, /device:TPU:0, one launch (start us, length us, event | category | flops | bytes accessed | tf_op | source)
XLA Modules:
  0.0 125.0 jit_solution(3401801907107307499)
XLA Ops:
  0.0 2.5 %solve.2.refs_0_.own_ref.inner_ref = bf16[4,192,512]{2,1,0:T(8,128)(2,1)S(1)} custom-call(s32[1]{0:T(128)} %bitcast.first_ref, bf16[8,192,512]{2,1,0:T(8,128)(2,1)} %bitcast.21, bf16[8,512,512]{2,1,0:T(8,128)(2,1)} %refs_10_.5), custom_call_target="tpu_custom_call" | custom-call | flops 1 | bytes 1 | tf_op jit(solution)/shard_map/solve/pallas_call | solution.py:53
  2.5 1.6 %collective-permute-start.3 = (bf16[4,192,512]{2,1,0:T(8,128)(2,1)S(1)}, bf16[4,192,512]{2,1,0:T(8,128)(2,1)}, u32[]{:S(2)}, u32[]{:S(2)}) collective-permute-start(bf16[4,192,512]{2,1,0:T(8,128)(2,1)S(1)} %solve.2.refs_0_.own_ref.inner_ref), channel_id=1, source_target_pairs={{1,2},{2,1},{3,4},{4,3},{5,6},{6,5},{7,8},{8,7},{9,10},{10,9},{11,... | collective-permute-start | bytes 2359304 | tf_op jit(solution)/shard_map/ppermute | solution.py:420
  4.1 2.7 %solve.3.refs_1_.inner_ref.own_ref = bf16[4,192,512]{2,1,0:T(8,128)(2,1)S(1)} custom-call(s32[1]{0:T(128)} %bitcast.5.first_ref, bf16[8,192,512]{2,1,0:T(8,128)(2,1)} %bitcast.22, bf16[8,512,512]{2,1,0:T(8,128)(2,1)} %refs_10_.5), custom_call_target="tpu_custom_call" | custom-call | flops 1 | bytes 1 | tf_op jit(solution)/shard_map/solve/pallas_call | solution.py:53
  6.8 0.9 copy-done.5
  7.7 1.1 copy-done.6
  8.9 2.6 %outward.5 = bf16[8,96,256]{2,1,0:T(8,128)(2,1)} custom-call(s32[1]{0:T(128)} %bitcast.7.part_ref, bf16[4,192,512]{2,1,0:T(8,128)(2,1)S(1)} %solve.2.refs_0_.own_ref.inner_ref, bf16[4,192,512]{2,1,0:T(8,128)(2,1)S(1)} %copy-done.6, bf16[2048,512]{1,0:T(8,128)(2,1)S(1)} %copy-done.1, f32[8,2048]{1,0:T(8,128)S(1)} %maximum_convert_fusion.refs_3_), custom_call_target="tpu_custom_call" | custom-call | flops 1 | bytes 1 | tf_op jit(solution)/shard_map/outward/pallas_call | solution.py:99
  11.5 6.5 %collective-permute-start = (bf16[8,96,256]{2,1,0:T(8,128)(2,1)}, bf16[8,96,256]{2,1,0:T(8,128)(2,1)}, u32[]{:S(2)}, u32[]{:S(2)}) collective-permute-start(bf16[8,96,256]{2,1,0:T(8,128)(2,1)} %outward.5), channel_id=1, source_target_pairs={{0,8},{1,9},{2,10},{3,11},{4,12},{5,13},{6,14},{7,15},{8,0},{9,1},... | collective-permute-start | bytes 1179656 | tf_op jit(solution)/shard_map/ppermute | solution.py:373
  18.0 1.1 copy-done.7
  19.1 1.8 %outward.4 = bf16[8,96,256]{2,1,0:T(8,128)(2,1)S(1)} custom-call(s32[1]{0:T(128)} %bitcast.3.part_ref, bf16[4,192,512]{2,1,0:T(8,128)(2,1)S(1)} %solve.2.refs_0_.own_ref.inner_ref, bf16[4,192,512]{2,1,0:T(8,128)(2,1)S(1)} %copy-done.7, bf16[2048,512]{1,0:T(8,128)(2,1)S(1)} %copy-done.1, f32[8,2048]{1,0:T(8,128)S(1)} %maximum_convert_fusion.refs_3_), custom_call_target="tpu_custom_call" | custom-call | flops 1 | bytes 1 | tf_op jit(solution)/shard_map/outward/pallas_call | solution.py:99
  21.0 0.9 convert_element_type.7
  21.9 0.1 pad_add_fusion.place_ref
  22.1 1.2 split.2
  23.3 1.6 %collective-permute-start.1 = (bf16[8,48,256]{2,1,0:T(8,128)(2,1)S(1)}, bf16[8,48,256]{2,1,0:T(8,128)(2,1)S(1)}, u32[]{:S(2)}, u32[]{:S(2)}) collective-permute-start(bf16[8,48,256]{2,1,0:T(8,128)(2,1)S(1)} %get-tuple-element.32), channel_id=1, source_target_pairs={{0,16},{1,17},{2,18},{3,19},{4,20},{5,21},{6,22},{7,23},{8,24},{9,... | collective-permute-start | bytes 589832 | tf_op jit(solution)/shard_map/ppermute | solution.py:373
  24.8 0.1 fusion.8
  25.0 0.9 collective-permute-start.8
  25.9 3.5 %collective-permute-start.9 = (bf16[2,128,128]{2,1,0:T(8,128)(2,1)S(1)}, bf16[2,128,128]{2,1,0:T(8,128)(2,1)S(1)}, u32[]{:S(2)}, u32[]{:S(2)}) collective-permute-start(bf16[2,128,128]{2,1,0:T(8,128)(2,1)S(1)} %convert_element_type.7), channel_id=1, source_target_pairs={{0,6},{1,7},{2,4},{3,5},{4,2},{5,3},{6,0},{7,1},{8,14},{9,15},{10,... | collective-permute-start | bytes 196616 | tf_op jit(solution)/shard_map/ppermute | solution.py:373
  29.4 0.8 collective-permute-done.1.got_ref
  30.1 0.6 deal.2
  30.7 2.9 %collective-permute-start.2 = (bf16[4,48,256]{2,1,0:T(8,128)(2,1)S(1)}, bf16[4,48,256]{2,1,0:T(8,128)(2,1)S(1)}, u32[]{:S(2)}, u32[]{:S(2)}) collective-permute-start(bf16[4,48,256]{2,1,0:T(8,128)(2,1)S(1)} %get-tuple-element.34), channel_id=1, source_target_pairs={{0,17},{1,16},{2,19},{3,18},{4,21},{5,20},{6,23},{7,22},{8,25},{9,... | collective-permute-start | bytes 294920 | tf_op jit(solution)/shard_map/ppermute | solution.py:373
  33.7 2.8 %collective-permute-done.2.refs_1_ = bf16[4,48,256]{2,1,0:T(8,128)(2,1)S(1)} collective-permute-done((bf16[4,48,256]{2,1,0:T(8,128)(2,1)S(1)}, bf16[4,48,256]{2,1,0:T(8,128)(2,1)S(1)}, u32[]{:S(2)}, u32[]{:S(2)}) %collective-permute-start.2) | collective-permute-done | bytes 98336 | tf_op jit(solution)/shard_map/ppermute | solution.py:373
  36.5 0.8 collective-permute-start.13
  37.4 0.6 collective-permute-start.4
  38.0 3.0 %collective-permute-start.5 = (bf16[4,48,256]{2,1,0:T(8,128)(2,1)S(1)}, bf16[4,48,256]{2,1,0:T(8,128)(2,1)S(1)}, u32[]{:S(2)}, u32[]{:S(2)}) collective-permute-start(bf16[4,48,256]{2,1,0:T(8,128)(2,1)S(1)} %add.115.refs_0_), channel_id=1, source_target_pairs={{0,6},{1,7},{2,4},{3,5},{4,2},{5,3},{6,0},{7,1},{8,14},{9,15},{10,... | collective-permute-start | bytes 294920 | tf_op jit(solution)/shard_map/ppermute | solution.py:373
  41.0 0.5 collective-permute-start.6
  41.6 1.6 %copy-done.3 = bf16[4,512,512]{2,1,0:T(8,128)(2,1)S(1)} copy-done((bf16[4,512,512]{2,1,0:T(8,128)(2,1)S(1)}, bf16[4,512,512]{2,1,0:T(8,128)(2,1)}, u32[]{:S(2)}) %copy-start.3) | copy-done | bytes 2097176
  43.1 1.1 copy-done.8
  44.3 5.2 %near.4.refs_11_ = f32[4,192,512]{2,1,0:T(8,128)S(1)} custom-call(s32[1]{0:T(128)} %bitcast.first_ref, s32[4,6]{1,0:T(4,128)S(1)} %constant_dynamic-slice_fusion.3.slot_ref, s32[4]{0:T(128)S(1)} %get-tuple-element.64.count_ref, s32[4,6]{1,0:T(4,128)S(1)} %get-tuple-element.60.type_ref, bf16[4,192,512]{2,1,0:T(8,128)(2,1)} %collective-permute-done.3.halo_ref, ...), custom_call_target="tpu_custom_call" | custom-call | flops 1 | bytes 1 | tf_op jit(solution)/shard_map/near/pallas_call | solution.py:245
  49.5 0.3 reflect.2.refs_0_
  49.8 1.3 %collective-permute-start.10 = (bf16[4,48,256]{2,1,0:T(8,128)(2,1)S(1)}, bf16[4,48,256]{2,1,0:T(8,128)(2,1)S(1)}, u32[]{:S(2)}, u32[]{:S(2)}) collective-permute-start(bf16[4,48,256]{2,1,0:T(8,128)(2,1)S(1)} %reflect.2.refs_0_), channel_id=1, source_target_pairs={{0,17},{1,16},{2,19},{3,18},{4,21},{5,20},{6,23},{7,22},{8,25},{9,... | collective-permute-start | bytes 294920 | tf_op jit(solution)/shard_map/ppermute | solution.py:373
  51.1 1.9 %collective-permute-start.11 = (bf16[4,48,256]{2,1,0:T(8,128)(2,1)S(1)}, bf16[4,48,256]{2,1,0:T(8,128)(2,1)S(1)}, u32[]{:S(2)}, u32[]{:S(2)}) collective-permute-start(bf16[4,48,256]{2,1,0:T(8,128)(2,1)S(1)} %reflect.2.refs_0_), channel_id=1, source_target_pairs={{0,16},{1,17},{2,18},{3,19},{4,20},{5,21},{6,22},{7,23},{8,24},{9,... | collective-permute-start | bytes 294920 | tf_op jit(solution)/shard_map/ppermute | solution.py:373
  53.0 2.5 %collective-permute-done.10.refs_1_ = bf16[4,48,256]{2,1,0:T(8,128)(2,1)S(1)} collective-permute-done((bf16[4,48,256]{2,1,0:T(8,128)(2,1)S(1)}, bf16[4,48,256]{2,1,0:T(8,128)(2,1)S(1)}, u32[]{:S(2)}, u32[]{:S(2)}) %collective-permute-start.10) | collective-permute-done | bytes 98336 | tf_op jit(solution)/shard_map/ppermute | solution.py:373
  55.5 2.7 %collective-permute-start.12 = (bf16[4,48,256]{2,1,0:T(8,128)(2,1)S(1)}, bf16[4,48,256]{2,1,0:T(8,128)(2,1)S(1)}, u32[]{:S(2)}, u32[]{:S(2)}) collective-permute-start(bf16[4,48,256]{2,1,0:T(8,128)(2,1)S(1)} %collective-permute-done.10.refs_1_), channel_id=1, source_target_pairs={{0,16},{1,17},{2,18},{3,19},{4,20},{5,21},{6,22},{7,23},{8,24},{9,... | collective-permute-start | bytes 294920 | tf_op jit(solution)/shard_map/ppermute | solution.py:373
  58.2 0.5 collective-permute-start.15
  58.8 3.7 %near.5.refs_11_ = f32[4,192,512]{2,1,0:T(8,128)S(1)} custom-call(s32[1]{0:T(128)} %bitcast.5.first_ref, s32[4,6]{1,0:T(4,128)S(1)} %constant_dynamic-slice_fusion.1.slot_ref, s32[4]{0:T(128)S(1)} %get-tuple-element.63.count_ref, s32[4,6]{1,0:T(4,128)S(1)} %get-tuple-element.59.type_ref, bf16[4,192,512]{2,1,0:T(8,128)(2,1)S(1)} %collective-permute-done.13.halo_ref, ...), custom_call_target="tpu_custom_call" | custom-call | flops 1 | bytes 1 | tf_op jit(solution)/shard_map/near/pallas_call | solution.py:245
  62.6 0.6 collective-permute-start.17
  63.3 0.9 collective-permute-done.17.refs_7_
  64.2 3.3 %back.3.refs_0_.own_ref.inner_ref = bf16[4,192,512]{2,1,0:T(8,128)(2,1)S(1)} custom-call(s32[1]{0:T(128)} %bitcast.first_ref, s32[3]{0:T(128)S(1)} %pad_add_fusion.place_ref, bf16[4,48,256]{2,1,0:T(8,128)(2,1)S(1)} %reflect.2.refs_0_, bf16[4,48,256]{2,1,0:T(8,128)(2,1)S(1)} %collective-permute-done.10.refs_1_, ...), custom_call_target="tpu_custom_call" | custom-call | flops 1 | bytes 1 | tf_op jit(solution)/shard_map/back/pallas_call | solution.py:321
  67.5 0.7 collective-permute-start.21
  68.2 3.3 %back.4.refs_1_.inner_ref.own_ref = bf16[4,192,512]{2,1,0:T(8,128)(2,1)S(1)} custom-call(s32[1]{0:T(128)} %bitcast.5.first_ref, s32[3]{0:T(128)S(1)} %pad_add_fusion.place_ref, bf16[4,48,256]{2,1,0:T(8,128)(2,1)S(1)} %reflect.2.refs_0_, bf16[4,48,256]{2,1,0:T(8,128)(2,1)S(1)} %collective-permute-done.10.refs_1_, ...), custom_call_target="tpu_custom_call" | custom-call | flops 1 | bytes 1 | tf_op jit(solution)/shard_map/back/pallas_call | solution.py:321
  71.5 1.9 %outward.7 = bf16[8,96,256]{2,1,0:T(8,128)(2,1)S(1)} custom-call(s32[1]{0:T(128)} %bitcast.7.part_ref, bf16[4,192,512]{2,1,0:T(8,128)(2,1)S(1)} %back.3.refs_0_.own_ref.inner_ref, bf16[4,192,512]{2,1,0:T(8,128)(2,1)S(1)} %back.4.refs_1_.inner_ref.own_ref, bf16[2048,512]{1,0:T(8,128)(2,1)S(1)} %copy-done.1, f32[8,2048]{1,0:T(8,128)S(1)} %maximum_convert_fusion.refs_3_), custom_call_target="tpu_custom_call" | custom-call | flops 1 | bytes 1 | tf_op jit(solution)/shard_map/outward/pallas_call | solution.py:99
  73.4 3.6 %collective-permute-start.18 = (bf16[8,96,256]{2,1,0:T(8,128)(2,1)S(1)}, bf16[8,96,256]{2,1,0:T(8,128)(2,1)S(1)}, u32[]{:S(2)}, u32[]{:S(2)}) collective-permute-start(bf16[8,96,256]{2,1,0:T(8,128)(2,1)S(1)} %outward.7), channel_id=1, source_target_pairs={{0,8},{1,9},{2,10},{3,11},{4,12},{5,13},{6,14},{7,15},{8,0},{9,1},... | collective-permute-start | bytes 1179656 | tf_op jit(solution)/shard_map/ppermute | solution.py:373
  77.0 1.9 %outward.6 = bf16[8,96,256]{2,1,0:T(8,128)(2,1)S(1)} custom-call(s32[1]{0:T(128)} %bitcast.3.part_ref, bf16[4,192,512]{2,1,0:T(8,128)(2,1)S(1)} %back.3.refs_0_.own_ref.inner_ref, bf16[4,192,512]{2,1,0:T(8,128)(2,1)S(1)} %back.4.refs_1_.inner_ref.own_ref, bf16[2048,512]{1,0:T(8,128)(2,1)S(1)} %copy-done.1, f32[8,2048]{1,0:T(8,128)S(1)} %maximum_convert_fusion.refs_3_), custom_call_target="tpu_custom_call" | custom-call | flops 1 | bytes 1 | tf_op jit(solution)/shard_map/outward/pallas_call | solution.py:99
  78.9 0.6 split.3
  79.5 2.0 %collective-permute-start.19 = (bf16[8,48,256]{2,1,0:T(8,128)(2,1)S(1)}, bf16[8,48,256]{2,1,0:T(8,128)(2,1)S(1)}, u32[]{:S(2)}, u32[]{:S(2)}) collective-permute-start(bf16[8,48,256]{2,1,0:T(8,128)(2,1)S(1)} %get-tuple-element.47), channel_id=1, source_target_pairs={{0,16},{1,17},{2,18},{3,19},{4,20},{5,21},{6,22},{7,23},{8,24},{9,... | collective-permute-start | bytes 589832 | tf_op jit(solution)/shard_map/ppermute | solution.py:373
  81.6 5.1 %collective-permute-done.19.got_ref = bf16[8,48,256]{2,1,0:T(8,128)(2,1)S(1)} collective-permute-done((bf16[8,48,256]{2,1,0:T(8,128)(2,1)S(1)}, bf16[8,48,256]{2,1,0:T(8,128)(2,1)S(1)}, u32[]{:S(2)}, u32[]{:S(2)}) %collective-permute-start.19) | collective-permute-done | bytes 196640 | tf_op jit(solution)/shard_map/ppermute | solution.py:373
  86.6 0.6 deal.3
  87.2 3.5 %collective-permute-start.20 = (bf16[4,48,256]{2,1,0:T(8,128)(2,1)S(1)}, bf16[4,48,256]{2,1,0:T(8,128)(2,1)S(1)}, u32[]{:S(2)}, u32[]{:S(2)}) collective-permute-start(bf16[4,48,256]{2,1,0:T(8,128)(2,1)S(1)} %get-tuple-element.49), channel_id=1, source_target_pairs={{0,17},{1,16},{2,19},{3,18},{4,21},{5,20},{6,23},{7,22},{8,25},{9,... | collective-permute-start | bytes 294920 | tf_op jit(solution)/shard_map/ppermute | solution.py:373
  90.8 3.2 %collective-permute-done.20.refs_1_ = bf16[4,48,256]{2,1,0:T(8,128)(2,1)S(1)} collective-permute-done((bf16[4,48,256]{2,1,0:T(8,128)(2,1)S(1)}, bf16[4,48,256]{2,1,0:T(8,128)(2,1)S(1)}, u32[]{:S(2)}, u32[]{:S(2)}) %collective-permute-start.20) | collective-permute-done | bytes 98336 | tf_op jit(solution)/shard_map/ppermute | solution.py:373
  94.0 0.3 collective-permute-start.32
  94.4 0.7 collective-permute-start.22
  95.0 2.1 %collective-permute-start.23 = (bf16[4,48,256]{2,1,0:T(8,128)(2,1)S(1)}, bf16[4,48,256]{2,1,0:T(8,128)(2,1)S(1)}, u32[]{:S(2)}, u32[]{:S(2)}) collective-permute-start(bf16[4,48,256]{2,1,0:T(8,128)(2,1)S(1)} %add.116.refs_0_), channel_id=1, source_target_pairs={{0,6},{1,7},{2,4},{3,5},{4,2},{5,3},{6,0},{7,1},{8,14},{9,15},{10,... | collective-permute-start | bytes 294920 | tf_op jit(solution)/shard_map/ppermute | solution.py:373
  97.1 0.7 collective-permute-start.24
  97.8 3.8 %near.6.refs_11_ = f32[4,192,512]{2,1,0:T(8,128)S(1)} custom-call(s32[1]{0:T(128)} %bitcast.first_ref, s32[4,6]{1,0:T(4,128)S(1)} %constant_dynamic-slice_fusion.3.slot_ref, s32[4]{0:T(128)S(1)} %get-tuple-element.64.count_ref, s32[4,6]{1,0:T(4,128)S(1)} %get-tuple-element.60.type_ref, bf16[4,192,512]{2,1,0:T(8,128)(2,1)S(1)} %collective-permute-done.21.halo_ref, ...), custom_call_target="tpu_custom_call" | custom-call | flops 1 | bytes 1 | tf_op jit(solution)/shard_map/near/pallas_call | solution.py:245
  101.7 2.0 %collective-permute-done.22.refs_1_ = bf16[4,48,256]{2,1,0:T(8,128)(2,1)S(1)} collective-permute-done((bf16[4,48,256]{2,1,0:T(8,128)(2,1)S(1)}, bf16[4,48,256]{2,1,0:T(8,128)(2,1)S(1)}, u32[]{:S(2)}, u32[]{:S(2)}) %collective-permute-start.22) | collective-permute-done | bytes 98336 | tf_op jit(solution)/shard_map/ppermute | solution.py:373
  103.6 0.2 collective-permute-done.24.refs_3_
  103.8 0.3 reflect.3.refs_0_
  104.1 1.1 collective-permute-start.25
  105.2 1.5 %collective-permute-start.26 = (bf16[4,48,256]{2,1,0:T(8,128)(2,1)S(1)}, bf16[4,48,256]{2,1,0:T(8,128)(2,1)S(1)}, u32[]{:S(2)}, u32[]{:S(2)}) collective-permute-start(bf16[4,48,256]{2,1,0:T(8,128)(2,1)S(1)} %reflect.3.refs_0_), channel_id=1, source_target_pairs={{0,16},{1,17},{2,18},{3,19},{4,20},{5,21},{6,22},{7,23},{8,24},{9,... | collective-permute-start | bytes 294920 | tf_op jit(solution)/shard_map/ppermute | solution.py:373
  106.7 3.3 %collective-permute-done.25.refs_1_ = bf16[4,48,256]{2,1,0:T(8,128)(2,1)S(1)} collective-permute-done((bf16[4,48,256]{2,1,0:T(8,128)(2,1)S(1)}, bf16[4,48,256]{2,1,0:T(8,128)(2,1)S(1)}, u32[]{:S(2)}, u32[]{:S(2)}) %collective-permute-start.25) | collective-permute-done | bytes 98336 | tf_op jit(solution)/shard_map/ppermute | solution.py:373
  110.0 2.0 %collective-permute-start.27 = (bf16[4,48,256]{2,1,0:T(8,128)(2,1)S(1)}, bf16[4,48,256]{2,1,0:T(8,128)(2,1)S(1)}, u32[]{:S(2)}, u32[]{:S(2)}) collective-permute-start(bf16[4,48,256]{2,1,0:T(8,128)(2,1)S(1)} %collective-permute-done.25.refs_1_), channel_id=1, source_target_pairs={{0,16},{1,17},{2,18},{3,19},{4,20},{5,21},{6,22},{7,23},{8,24},{9,... | collective-permute-start | bytes 294920 | tf_op jit(solution)/shard_map/ppermute | solution.py:373
  112.0 0.5 collective-permute-start.29
  112.5 2.1 %collective-permute-done.27.refs_3_ = bf16[4,48,256]{2,1,0:T(8,128)(2,1)S(1)} collective-permute-done((bf16[4,48,256]{2,1,0:T(8,128)(2,1)S(1)}, bf16[4,48,256]{2,1,0:T(8,128)(2,1)S(1)}, u32[]{:S(2)}, u32[]{:S(2)}) %collective-permute-start.27) | collective-permute-done | bytes 98336 | tf_op jit(solution)/shard_map/ppermute | solution.py:373
  114.6 3.5 %near.7.refs_12_ = f32[4,192,512]{2,1,0:T(8,128)S(1)} custom-call(s32[1]{0:T(128)} %bitcast.5.first_ref, s32[4,6]{1,0:T(4,128)S(1)} %constant_dynamic-slice_fusion.1.slot_ref, s32[4]{0:T(128)S(1)} %get-tuple-element.63.count_ref, s32[4,6]{1,0:T(4,128)S(1)} %get-tuple-element.59.type_ref, bf16[4,192,512]{2,1,0:T(8,128)(2,1)S(1)} %collective-permute-done.32.halo_ref, ...), custom_call_target="tpu_custom_call" | custom-call | flops 1 | bytes 1 | tf_op jit(solution)/shard_map/near/pallas_call | solution.py:245
  118.2 6.7 %back.5 = bf16[8,192,512]{2,1,0:T(8,128)(2,1)} custom-call(s32[1]{0:T(128)} %bitcast.first_ref, s32[3]{0:T(128)S(1)} %pad_add_fusion.place_ref, bf16[4,48,256]{2,1,0:T(8,128)(2,1)S(1)} %reflect.3.refs_0_, bf16[4,48,256]{2,1,0:T(8,128)(2,1)S(1)} %collective-permute-done.25.refs_1_, bf16[4,48,256]{2,1,0:T(8,128)(2,1)S(1)} %collective-permute-done.26.refs_2_, ...), custom_call_target="tpu_custom_call" | custom-call | flops 1 | bytes 1 | tf_op jit(solution)/shard_map/back/pallas_call | solution.py:321
  (66 shorter events, 0.6 us)
Async XLA Ops:
  2.5 33.9 %collective-permute-start.3 = (bf16[4,192,512]{2,1,0:T(8,128)(2,1)S(1)}, bf16[4,192,512]{2,1,0:T(8,128)(2,1)}, u32[]{:S(2)}, u32[]{:S(2)}) collective-permute-start(bf16[4,192,512]{2,1,0:T(8,128)(2,1)S(1)} %solve.2.refs_0_.own_ref.inner_ref), channel_id=1, source_target_pairs={{1,2},{2,1},{3,4},{4,3},{5,6},{6,5},{7,8},{8,7},{9,10},{10,9},{11,... | collective-permute-start | bytes 2359304 | tf_op jit(solution)/shard_map/ppermute | solution.py:420
  4.1 3.6 %copy-start.10 = (bf16[8,2048]{1,0:T(8,128)(2,1)S(1)}, bf16[8,2048]{1,0:T(8,128)(2,1)}, u32[]{:S(2)}) copy-start(bf16[8,2048]{1,0:T(8,128)(2,1)} %param.15) | copy-start | bytes 98308
  4.1 3.6 %copy-start.1 = (bf16[2048,512]{1,0:T(8,128)(2,1)S(1)}, bf16[2048,512]{1,0:T(8,128)(2,1)}, u32[]{:S(2)}) copy-start(bf16[2048,512]{1,0:T(8,128)(2,1)} %refs_9_.5) | copy-start | bytes 6291460
  6.8 0.9 copy-start.5
  7.7 1.1 copy-start.6
  11.5 10.6 %collective-permute-start = (bf16[8,96,256]{2,1,0:T(8,128)(2,1)}, bf16[8,96,256]{2,1,0:T(8,128)(2,1)}, u32[]{:S(2)}, u32[]{:S(2)}) collective-permute-start(bf16[8,96,256]{2,1,0:T(8,128)(2,1)} %outward.5), channel_id=1, source_target_pairs={{0,8},{1,9},{2,10},{3,11},{4,12},{5,13},{6,14},{7,15},{8,0},{9,1},... | collective-permute-start | bytes 1179656 | tf_op jit(solution)/shard_map/ppermute | solution.py:373
  18.0 1.1 copy-start.7
  19.1 2.9 %copy-start.11 = (s32[8,6]{1,0:T(8,128)S(1)}, s32[8,6]{1,0:T(8,128)}, u32[]{:S(2)}) copy-start(s32[8,6]{1,0:T(8,128)} %param.12) | copy-start | bytes 580
  19.1 5.7 %copy-start.13 = (s32[8]{0:T(128)S(1)}, s32[8]{0:T(128)}, u32[]{:S(2)}) copy-start(s32[8]{0:T(128)} %param.13) | copy-start | bytes 100
  19.1 5.8 %copy-start.12 = (s32[8,6]{1,0:T(8,128)S(1)}, s32[8,6]{1,0:T(8,128)}, u32[]{:S(2)}) copy-start(s32[8,6]{1,0:T(8,128)} %param.14) | copy-start | bytes 580
  21.9 19.6 %copy-start.2 = (bf16[8,512,192]{1,2,0:T(8,128)(2,1)S(1)}, bf16[8,512,192]{1,2,0:T(8,128)(2,1)}, u32[]{:S(2)}) copy-start(bf16[8,512,192]{1,2,0:T(8,128)(2,1)} %param.9) | copy-start | bytes 4718596
  23.3 6.9 %collective-permute-start.1 = (bf16[8,48,256]{2,1,0:T(8,128)(2,1)S(1)}, bf16[8,48,256]{2,1,0:T(8,128)(2,1)S(1)}, u32[]{:S(2)}, u32[]{:S(2)}) collective-permute-start(bf16[8,48,256]{2,1,0:T(8,128)(2,1)S(1)} %get-tuple-element.32), channel_id=1, source_target_pairs={{0,16},{1,17},{2,18},{3,19},{4,20},{5,21},{6,22},{7,23},{8,24},{9,... | collective-permute-start | bytes 589832 | tf_op jit(solution)/shard_map/ppermute | solution.py:373
  24.9 12.4 %collective-permute-start.7 = (bf16[2,128,128]{2,1,0:T(8,128)(2,1)S(1)}, bf16[2,128,128]{2,1,0:T(8,128)(2,1)S(1)}, u32[]{:S(2)}, u32[]{:S(2)}) collective-permute-start(bf16[2,128,128]{2,1,0:T(8,128)(2,1)S(1)} %convert_element_type.7), channel_id=1, source_target_pairs={{0,2},{1,3},{2,0},{3,1},{4,6},{5,7},{6,4},{7,5},{8,10},{9,11},{10,... | collective-permute-start | bytes 196616 | tf_op jit(solution)/shard_map/ppermute | solution.py:373
  25.0 12.3 %collective-permute-start.8 = (bf16[2,128,128]{2,1,0:T(8,128)(2,1)S(1)}, bf16[2,128,128]{2,1,0:T(8,128)(2,1)S(1)}, u32[]{:S(2)}, u32[]{:S(2)}) collective-permute-start(bf16[2,128,128]{2,1,0:T(8,128)(2,1)S(1)} %convert_element_type.7), channel_id=1, source_target_pairs={{0,4},{1,5},{2,6},{3,7},{4,0},{5,1},{6,2},{7,3},{8,12},{9,13},{10,... | collective-permute-start | bytes 196616 | tf_op jit(solution)/shard_map/ppermute | solution.py:373
  25.9 15.6 %collective-permute-start.9 = (bf16[2,128,128]{2,1,0:T(8,128)(2,1)S(1)}, bf16[2,128,128]{2,1,0:T(8,128)(2,1)S(1)}, u32[]{:S(2)}, u32[]{:S(2)}) collective-permute-start(bf16[2,128,128]{2,1,0:T(8,128)(2,1)S(1)} %convert_element_type.7), channel_id=1, source_target_pairs={{0,6},{1,7},{2,4},{3,5},{4,2},{5,3},{6,0},{7,1},{8,14},{9,15},{10,... | collective-permute-start | bytes 196616 | tf_op jit(solution)/shard_map/ppermute | solution.py:373
  30.7 5.7 %collective-permute-start.2 = (bf16[4,48,256]{2,1,0:T(8,128)(2,1)S(1)}, bf16[4,48,256]{2,1,0:T(8,128)(2,1)S(1)}, u32[]{:S(2)}, u32[]{:S(2)}) collective-permute-start(bf16[4,48,256]{2,1,0:T(8,128)(2,1)S(1)} %get-tuple-element.34), channel_id=1, source_target_pairs={{0,17},{1,16},{2,19},{3,18},{4,21},{5,20},{6,23},{7,22},{8,25},{9,... | collective-permute-start | bytes 294920 | tf_op jit(solution)/shard_map/ppermute | solution.py:373
  36.5 22.4 %collective-permute-start.13 = (bf16[4,192,512]{2,1,0:T(8,128)(2,1)}, bf16[4,192,512]{2,1,0:T(8,128)(2,1)S(1)}, u32[]{:S(2)}, u32[]{:S(2)}) collective-permute-start(bf16[4,192,512]{2,1,0:T(8,128)(2,1)} %copy-done.5), channel_id=1, source_target_pairs={{0,1},{1,0},{2,3},{3,2},{4,5},{5,4},{6,7},{7,6},{8,9},{9,8},{10,11... | collective-permute-start | bytes 2359304 | tf_op jit(solution)/shard_map/ppermute | solution.py:440
  37.4 12.1 %collective-permute-start.4 = (bf16[4,48,256]{2,1,0:T(8,128)(2,1)S(1)}, bf16[4,48,256]{2,1,0:T(8,128)(2,1)S(1)}, u32[]{:S(2)}, u32[]{:S(2)}) collective-permute-start(bf16[4,48,256]{2,1,0:T(8,128)(2,1)S(1)} %add.115.refs_0_), channel_id=1, source_target_pairs={{0,4},{1,5},{2,6},{3,7},{4,0},{5,1},{6,2},{7,3},{8,12},{9,13},{10,... | collective-permute-start | bytes 294920 | tf_op jit(solution)/shard_map/ppermute | solution.py:373
  38.0 11.5 %collective-permute-start.5 = (bf16[4,48,256]{2,1,0:T(8,128)(2,1)S(1)}, bf16[4,48,256]{2,1,0:T(8,128)(2,1)S(1)}, u32[]{:S(2)}, u32[]{:S(2)}) collective-permute-start(bf16[4,48,256]{2,1,0:T(8,128)(2,1)S(1)} %add.115.refs_0_), channel_id=1, source_target_pairs={{0,6},{1,7},{2,4},{3,5},{4,2},{5,3},{6,0},{7,1},{8,14},{9,15},{10,... | collective-permute-start | bytes 294920 | tf_op jit(solution)/shard_map/ppermute | solution.py:373
  41.0 8.5 %collective-permute-start.6 = (bf16[4,48,256]{2,1,0:T(8,128)(2,1)S(1)}, bf16[4,48,256]{2,1,0:T(8,128)(2,1)S(1)}, u32[]{:S(2)}, u32[]{:S(2)}) collective-permute-start(bf16[4,48,256]{2,1,0:T(8,128)(2,1)S(1)} %add.115.refs_0_), channel_id=1, source_target_pairs={{0,2},{1,3},{2,0},{3,1},{4,6},{5,7},{6,4},{7,5},{8,10},{9,11},{10,... | collective-permute-start | bytes 294920 | tf_op jit(solution)/shard_map/ppermute | solution.py:373
  41.5 1.6 %copy-start.3 = (bf16[4,512,512]{2,1,0:T(8,128)(2,1)S(1)}, bf16[4,512,512]{2,1,0:T(8,128)(2,1)}, u32[]{:S(2)}) copy-start(bf16[4,512,512]{2,1,0:T(8,128)(2,1)} %translations_ref.7) | copy-start | bytes 6291460
  43.1 1.1 copy-start.8
  44.3 14.6 %copy-start.4 = (bf16[4,512,512]{2,1,0:T(8,128)(2,1)S(1)}, bf16[4,512,512]{2,1,0:T(8,128)(2,1)}, u32[]{:S(2)}) copy-start(bf16[4,512,512]{2,1,0:T(8,128)(2,1)} %translations_ref.7) | copy-start | bytes 6291460
  44.3 14.6 %copy-start.9 = (bf16[4,192,512]{2,1,0:T(8,128)(2,1)S(1)}, bf16[4,192,512]{2,1,0:T(8,128)(2,1)}, u32[]{:S(2)}) copy-start(bf16[4,192,512]{2,1,0:T(8,128)(2,1)} %copy-done.5) | copy-start | bytes 2359300
  49.8 5.7 %collective-permute-start.10 = (bf16[4,48,256]{2,1,0:T(8,128)(2,1)S(1)}, bf16[4,48,256]{2,1,0:T(8,128)(2,1)S(1)}, u32[]{:S(2)}, u32[]{:S(2)}) collective-permute-start(bf16[4,48,256]{2,1,0:T(8,128)(2,1)S(1)} %reflect.2.refs_0_), channel_id=1, source_target_pairs={{0,17},{1,16},{2,19},{3,18},{4,21},{5,20},{6,23},{7,22},{8,25},{9,... | collective-permute-start | bytes 294920 | tf_op jit(solution)/shard_map/ppermute | solution.py:373
  51.1 7.6 %collective-permute-start.11 = (bf16[4,48,256]{2,1,0:T(8,128)(2,1)S(1)}, bf16[4,48,256]{2,1,0:T(8,128)(2,1)S(1)}, u32[]{:S(2)}, u32[]{:S(2)}) collective-permute-start(bf16[4,48,256]{2,1,0:T(8,128)(2,1)S(1)} %reflect.2.refs_0_), channel_id=1, source_target_pairs={{0,16},{1,17},{2,18},{3,19},{4,20},{5,21},{6,22},{7,23},{8,24},{9,... | collective-permute-start | bytes 294920 | tf_op jit(solution)/shard_map/ppermute | solution.py:373
  55.5 7.1 %collective-permute-start.12 = (bf16[4,48,256]{2,1,0:T(8,128)(2,1)S(1)}, bf16[4,48,256]{2,1,0:T(8,128)(2,1)S(1)}, u32[]{:S(2)}, u32[]{:S(2)}) collective-permute-start(bf16[4,48,256]{2,1,0:T(8,128)(2,1)S(1)} %collective-permute-done.10.refs_1_), channel_id=1, source_target_pairs={{0,16},{1,17},{2,18},{3,19},{4,20},{5,21},{6,22},{7,23},{8,24},{9,... | collective-permute-start | bytes 294920 | tf_op jit(solution)/shard_map/ppermute | solution.py:373
  58.2 5.1 %collective-permute-start.14 = (bf16[4,48,256]{2,1,0:T(8,128)(2,1)S(1)}, bf16[4,48,256]{2,1,0:T(8,128)(2,1)S(1)}, u32[]{:S(2)}, u32[]{:S(2)}) collective-permute-start(bf16[4,48,256]{2,1,0:T(8,128)(2,1)S(1)} %reflect.2.refs_0_), channel_id=1, source_target_pairs={{0,8},{1,9},{2,10},{3,11},{4,12},{5,13},{6,14},{7,15},{8,0},{9,1},... | collective-permute-start | bytes 294920 | tf_op jit(solution)/shard_map/ppermute | solution.py:373
  58.2 5.1 %collective-permute-start.15 = (bf16[4,48,256]{2,1,0:T(8,128)(2,1)S(1)}, bf16[4,48,256]{2,1,0:T(8,128)(2,1)S(1)}, u32[]{:S(2)}, u32[]{:S(2)}) collective-permute-start(bf16[4,48,256]{2,1,0:T(8,128)(2,1)S(1)} %collective-permute-done.10.refs_1_), channel_id=1, source_target_pairs={{0,8},{1,9},{2,10},{3,11},{4,12},{5,13},{6,14},{7,15},{8,0},{9,1},... | collective-permute-start | bytes 294920 | tf_op jit(solution)/shard_map/ppermute | solution.py:373
  58.8 4.6 %collective-permute-start.16 = (bf16[4,48,256]{2,1,0:T(8,128)(2,1)S(1)}, bf16[4,48,256]{2,1,0:T(8,128)(2,1)S(1)}, u32[]{:S(2)}, u32[]{:S(2)}) collective-permute-start(bf16[4,48,256]{2,1,0:T(8,128)(2,1)S(1)} %collective-permute-done.11.refs_2_), channel_id=1, source_target_pairs={{0,8},{1,9},{2,10},{3,11},{4,12},{5,13},{6,14},{7,15},{8,0},{9,1},... | collective-permute-start | bytes 294920 | tf_op jit(solution)/shard_map/ppermute | solution.py:373
  58.8 5.3 %copy-start = (bf16[8,512,512]{2,1,0:T(8,128)(2,1)S(1)}, bf16[8,512,512]{2,1,0:T(8,128)(2,1)}, u32[]{:S(2)}) copy-start(bf16[8,512,512]{2,1,0:T(8,128)(2,1)} %refs_10_.5) | copy-start | bytes 12582916
  62.6 1.6 %collective-permute-start.17 = (bf16[4,48,256]{2,1,0:T(8,128)(2,1)S(1)}, bf16[4,48,256]{2,1,0:T(8,128)(2,1)S(1)}, u32[]{:S(2)}, u32[]{:S(2)}) collective-permute-start(bf16[4,48,256]{2,1,0:T(8,128)(2,1)S(1)} %collective-permute-done.12.refs_3_), channel_id=1, source_target_pairs={{0,8},{1,9},{2,10},{3,11},{4,12},{5,13},{6,14},{7,15},{8,0},{9,1},... | collective-permute-start | bytes 294920 | tf_op jit(solution)/shard_map/ppermute | solution.py:373
  67.5 26.5 %collective-permute-start.21 = (bf16[4,192,512]{2,1,0:T(8,128)(2,1)S(1)}, bf16[4,192,512]{2,1,0:T(8,128)(2,1)S(1)}, u32[]{:S(2)}, u32[]{:S(2)}) collective-permute-start(bf16[4,192,512]{2,1,0:T(8,128)(2,1)S(1)} %back.3.refs_0_.own_ref.inner_ref), channel_id=1, source_target_pairs={{1,2},{2,1},{3,4},{4,3},{5,6},{6,5},{7,8},{8,7},{9,10},{10,9},{11,... | collective-permute-start | bytes 2359304 | tf_op jit(solution)/shard_map/ppermute | solution.py:420
  73.4 5.5 %collective-permute-start.18 = (bf16[8,96,256]{2,1,0:T(8,128)(2,1)S(1)}, bf16[8,96,256]{2,1,0:T(8,128)(2,1)S(1)}, u32[]{:S(2)}, u32[]{:S(2)}) collective-permute-start(bf16[8,96,256]{2,1,0:T(8,128)(2,1)S(1)} %outward.7), channel_id=1, source_target_pairs={{0,8},{1,9},{2,10},{3,11},{4,12},{5,13},{6,14},{7,15},{8,0},{9,1},... | collective-permute-start | bytes 1179656 | tf_op jit(solution)/shard_map/ppermute | solution.py:373
  79.5 7.1 %collective-permute-start.19 = (bf16[8,48,256]{2,1,0:T(8,128)(2,1)S(1)}, bf16[8,48,256]{2,1,0:T(8,128)(2,1)S(1)}, u32[]{:S(2)}, u32[]{:S(2)}) collective-permute-start(bf16[8,48,256]{2,1,0:T(8,128)(2,1)S(1)} %get-tuple-element.47), channel_id=1, source_target_pairs={{0,16},{1,17},{2,18},{3,19},{4,20},{5,21},{6,22},{7,23},{8,24},{9,... | collective-permute-start | bytes 589832 | tf_op jit(solution)/shard_map/ppermute | solution.py:373
  87.2 6.8 %collective-permute-start.20 = (bf16[4,48,256]{2,1,0:T(8,128)(2,1)S(1)}, bf16[4,48,256]{2,1,0:T(8,128)(2,1)S(1)}, u32[]{:S(2)}, u32[]{:S(2)}) collective-permute-start(bf16[4,48,256]{2,1,0:T(8,128)(2,1)S(1)} %get-tuple-element.49), channel_id=1, source_target_pairs={{0,17},{1,16},{2,19},{3,18},{4,21},{5,20},{6,23},{7,22},{8,25},{9,... | collective-permute-start | bytes 294920 | tf_op jit(solution)/shard_map/ppermute | solution.py:373
  94.0 20.6 %collective-permute-start.32 = (bf16[4,192,512]{2,1,0:T(8,128)(2,1)S(1)}, bf16[4,192,512]{2,1,0:T(8,128)(2,1)S(1)}, u32[]{:S(2)}, u32[]{:S(2)}) collective-permute-start(bf16[4,192,512]{2,1,0:T(8,128)(2,1)S(1)} %back.4.refs_1_.inner_ref.own_ref), channel_id=1, source_target_pairs={{0,1},{1,0},{2,3},{3,2},{4,5},{5,4},{6,7},{7,6},{8,9},{9,8},{10,11... | collective-permute-start | bytes 2359304 | tf_op jit(solution)/shard_map/ppermute | solution.py:440
  94.4 9.3 %collective-permute-start.22 = (bf16[4,48,256]{2,1,0:T(8,128)(2,1)S(1)}, bf16[4,48,256]{2,1,0:T(8,128)(2,1)S(1)}, u32[]{:S(2)}, u32[]{:S(2)}) collective-permute-start(bf16[4,48,256]{2,1,0:T(8,128)(2,1)S(1)} %add.116.refs_0_), channel_id=1, source_target_pairs={{0,4},{1,5},{2,6},{3,7},{4,0},{5,1},{6,2},{7,3},{8,12},{9,13},{10,... | collective-permute-start | bytes 294920 | tf_op jit(solution)/shard_map/ppermute | solution.py:373
  95.0 8.6 %collective-permute-start.23 = (bf16[4,48,256]{2,1,0:T(8,128)(2,1)S(1)}, bf16[4,48,256]{2,1,0:T(8,128)(2,1)S(1)}, u32[]{:S(2)}, u32[]{:S(2)}) collective-permute-start(bf16[4,48,256]{2,1,0:T(8,128)(2,1)S(1)} %add.116.refs_0_), channel_id=1, source_target_pairs={{0,6},{1,7},{2,4},{3,5},{4,2},{5,3},{6,0},{7,1},{8,14},{9,15},{10,... | collective-permute-start | bytes 294920 | tf_op jit(solution)/shard_map/ppermute | solution.py:373
  97.1 6.7 %collective-permute-start.24 = (bf16[4,48,256]{2,1,0:T(8,128)(2,1)S(1)}, bf16[4,48,256]{2,1,0:T(8,128)(2,1)S(1)}, u32[]{:S(2)}, u32[]{:S(2)}) collective-permute-start(bf16[4,48,256]{2,1,0:T(8,128)(2,1)S(1)} %add.116.refs_0_), channel_id=1, source_target_pairs={{0,2},{1,3},{2,0},{3,1},{4,6},{5,7},{6,4},{7,5},{8,10},{9,11},{10,... | collective-permute-start | bytes 294920 | tf_op jit(solution)/shard_map/ppermute | solution.py:373
  104.1 5.9 %collective-permute-start.25 = (bf16[4,48,256]{2,1,0:T(8,128)(2,1)S(1)}, bf16[4,48,256]{2,1,0:T(8,128)(2,1)S(1)}, u32[]{:S(2)}, u32[]{:S(2)}) collective-permute-start(bf16[4,48,256]{2,1,0:T(8,128)(2,1)S(1)} %reflect.3.refs_0_), channel_id=1, source_target_pairs={{0,17},{1,16},{2,19},{3,18},{4,21},{5,20},{6,23},{7,22},{8,25},{9,... | collective-permute-start | bytes 294920 | tf_op jit(solution)/shard_map/ppermute | solution.py:373
  105.2 7.2 %collective-permute-start.26 = (bf16[4,48,256]{2,1,0:T(8,128)(2,1)S(1)}, bf16[4,48,256]{2,1,0:T(8,128)(2,1)S(1)}, u32[]{:S(2)}, u32[]{:S(2)}) collective-permute-start(bf16[4,48,256]{2,1,0:T(8,128)(2,1)S(1)} %reflect.3.refs_0_), channel_id=1, source_target_pairs={{0,16},{1,17},{2,18},{3,19},{4,20},{5,21},{6,22},{7,23},{8,24},{9,... | collective-permute-start | bytes 294920 | tf_op jit(solution)/shard_map/ppermute | solution.py:373
  110.0 4.6 %collective-permute-start.27 = (bf16[4,48,256]{2,1,0:T(8,128)(2,1)S(1)}, bf16[4,48,256]{2,1,0:T(8,128)(2,1)S(1)}, u32[]{:S(2)}, u32[]{:S(2)}) collective-permute-start(bf16[4,48,256]{2,1,0:T(8,128)(2,1)S(1)} %collective-permute-done.25.refs_1_), channel_id=1, source_target_pairs={{0,16},{1,17},{2,18},{3,19},{4,20},{5,21},{6,22},{7,23},{8,24},{9,... | collective-permute-start | bytes 294920 | tf_op jit(solution)/shard_map/ppermute | solution.py:373
  112.0 6.2 %collective-permute-start.28 = (bf16[4,48,256]{2,1,0:T(8,128)(2,1)S(1)}, bf16[4,48,256]{2,1,0:T(8,128)(2,1)S(1)}, u32[]{:S(2)}, u32[]{:S(2)}) collective-permute-start(bf16[4,48,256]{2,1,0:T(8,128)(2,1)S(1)} %reflect.3.refs_0_), channel_id=1, source_target_pairs={{0,8},{1,9},{2,10},{3,11},{4,12},{5,13},{6,14},{7,15},{8,0},{9,1},... | collective-permute-start | bytes 294920 | tf_op jit(solution)/shard_map/ppermute | solution.py:373
  112.0 6.2 %collective-permute-start.29 = (bf16[4,48,256]{2,1,0:T(8,128)(2,1)S(1)}, bf16[4,48,256]{2,1,0:T(8,128)(2,1)S(1)}, u32[]{:S(2)}, u32[]{:S(2)}) collective-permute-start(bf16[4,48,256]{2,1,0:T(8,128)(2,1)S(1)} %collective-permute-done.25.refs_1_), channel_id=1, source_target_pairs={{0,8},{1,9},{2,10},{3,11},{4,12},{5,13},{6,14},{7,15},{8,0},{9,1},... | collective-permute-start | bytes 294920 | tf_op jit(solution)/shard_map/ppermute | solution.py:373
  112.5 5.7 %collective-permute-start.30 = (bf16[4,48,256]{2,1,0:T(8,128)(2,1)S(1)}, bf16[4,48,256]{2,1,0:T(8,128)(2,1)S(1)}, u32[]{:S(2)}, u32[]{:S(2)}) collective-permute-start(bf16[4,48,256]{2,1,0:T(8,128)(2,1)S(1)} %collective-permute-done.26.refs_2_), channel_id=1, source_target_pairs={{0,8},{1,9},{2,10},{3,11},{4,12},{5,13},{6,14},{7,15},{8,0},{9,1},... | collective-permute-start | bytes 294920 | tf_op jit(solution)/shard_map/ppermute | solution.py:373
  114.6 3.6 %collective-permute-start.31 = (bf16[4,48,256]{2,1,0:T(8,128)(2,1)S(1)}, bf16[4,48,256]{2,1,0:T(8,128)(2,1)S(1)}, u32[]{:S(2)}, u32[]{:S(2)}) collective-permute-start(bf16[4,48,256]{2,1,0:T(8,128)(2,1)S(1)} %collective-permute-done.27.refs_3_), channel_id=1, source_target_pairs={{0,8},{1,9},{2,10},{3,11},{4,12},{5,13},{6,14},{7,15},{8,0},{9,1},... | collective-permute-start | bytes 294920 | tf_op jit(solution)/shard_map/ppermute | solution.py:373

commit v5 on v4

--- a/solution.py
+++ b/solution.py
@@ -28,7 +28,9 @@
     return pl.CostEstimate(flops=1, bytes_accessed=1, transcendentals=0)
 
 
-def solve_kernel(first_ref, source_ref, t_ref, out_ref, sources, matrices, arrived):
+def solve_kernel(staged, first_ref, source_ref, t_ref, *refs):
+    out_ref = refs[staged]
+    sources, matrices, arrived, staging = refs[-4:]
     count = out_ref.shape[0]
     copies = []
     for p in range(count):
@@ -40,34 +42,43 @@
         for copy in pair:
             copy.start()
         copies.append(pair)
+    moves = [
+        pltpu.make_async_copy(refs[n], refs[staged + 1 + n], staging.at[n]) for n in range(staged)
+    ]
+    for move in moves:
+        move.start()
     for p in range(count):
         for copy in copies[p]:
             copy.wait()
         out_ref[p] = lax.dot_general(
             sources[p], matrices[p], LAST, preferred_element_type=F32
         ).astype(BF16)
-
-
-def solve(first, source, t_matrices, count):
+    for move in moves:
+        move.wait()
+
+
+def solve(first, source, t_matrices, count, staged=()):
     m, size = source.shape[1:]
-    return pl.pallas_call(
-        solve_kernel,
-        grid_spec=pltpu.PrefetchScalarGridSpec(
-            num_scalar_prefetch=1,
-            grid=(1,),
-            in_specs=[pl.BlockSpec(memory_space=pl.ANY)] * 2,
-            out_specs=pl.BlockSpec((count, m, size), lambda p, first: (0, 0, 0)),
-            scratch_shapes=[
-                pltpu.VMEM((count, m, size), BF16),
-                pltpu.VMEM((count, size, size), BF16),
-                pltpu.SemaphoreType.DMA((2 * count,)),
-            ],
-        ),
-        out_shape=jax.ShapeDtypeStruct((count, m, size), BF16),
-        compiler_params=params(16),
+
+    def body(*refs):
+        solve_kernel(len(staged), *refs)
+
+    return pl.pallas_call(
+        body,
+        in_specs=[SCALARS] + [ANYWHERE] * (2 + len(staged)),
+        out_specs=[VECTORS] * (1 + len(staged)),
+        scratch_shapes=[
+            pltpu.VMEM((count, m, size), BF16),
+            pltpu.VMEM((count, size, size), BF16),
+            pltpu.SemaphoreType.DMA((2 * count,)),
+            pltpu.SemaphoreType.DMA((max(1, len(staged)),)),
+        ],
+        out_shape=[jax.ShapeDtypeStruct((count, m, size), BF16)]
+        + [jax.ShapeDtypeStruct(array.shape, array.dtype) for array in staged],
+        compiler_params=params(12),
         cost_estimate=cost(count * m * size * size, 2 * count * size * (2 * m + size)),
         name="solve",
-    )(first, source, t_matrices)
+    )(first, source, t_matrices, *staged)
 
 
 def outward_kernel(part_ref, *refs):
@@ -286,7 +297,7 @@
 
     total = partials[0][...]
     if len(partials) > 1:
-        total = jnp.where(pl.program_id(0) // 2 == first_ref[0], total, partials[1][...])
+        total = jnp.where(pl.program_id(0) == first_ref[0], total, partials[1][...])
     total = total.reshape(group * m, size)
     for c in range(chunks):
         waves_here = waves[c].reshape(m, width)
@@ -309,7 +320,7 @@
     count, m, size = partials[0].shape
     levels, rows, width = pieces[0].shape
     total_rows = basis.shape[0]
-    group = 2
+    group = 2 if len(partials) == 1 else count
     steps = count // group * len(partials)
 
     def body(first_ref, place_ref, *refs):
@@ -413,8 +424,12 @@
     ).astype(F32)
 
     held = [pltpu.with_memory_space_constraint(a, pltpu.HBM) for a in (incident_t, t_matrices)]
-    o_coeffs = solve(o_first, *held, reach)
-    e_coeffs = solve(e_first, *held, reach)
+    wave_basis = pltpu.with_memory_space_constraint(wave_basis, pltpu.HBM)
+    translations = pltpu.with_memory_space_constraint(translations, pltpu.HBM)
+    (o_coeffs,) = solve(o_first, *held, reach)
+    e_coeffs, wave_basis, translations = solve(
+        e_first, *held, reach, (wave_basis, translations,)
+    )
     for sweep in range(ITERS):
         last = sweep == ITERS - 1
         o_halo = lax.ppermute(o_coeffs, AXES, o_pairs)

time: 126 us -> 125 us (level)
  starting transfers between devices: 47.9 us -> 49.5 us
  waiting for transfers between devices: 22.8 us -> 21.4 us
    ppermute x29, waiting for transfers between devices: 22.8 us -> 21.4 us  [flip(): return lax.ppermute(array, AXES, [(i, i ^ mask) for i in range(devices)])]
    unnamed x28 -> x26, local copies, waits for them, and re-layouts: 5.89 us -> 5.22 us
  transfers between devices with their start and end apart: 33 -> 33, of which waited for: 10 -> 10; matrix products, arithmetic and copies ran while one was open for 1% -> 1% of each run, Pallas kernels for 27% -> 28%
where the time goes in v5:
time: 125 us
  starting transfers between devices  49.5 us (40%)
  Pallas kernels  47.2 us (38%)
  waiting for transfers between devices  21.4 us (17%)
  local copies, waits for them, and re-layouts  5.49 us (4%)
    ppermute x29, starting transfers between devices, flip(): return lax.ppermute(array, AXES, [(i, i ^ mask) for i in range(devices)])  45.5 us
    ppermute x29, waiting for transfers between devices, flip(): return lax.ppermute(array, AXES, [(i, i ^ mask) for i in range(devices)])  21.4 us
    pallas_call x4, Pallas kernels, near(): pl.pallas_call(near_kernel, grid_spec=pltpu.PrefetchScalarGridSpec(num_sc...  16.5 us
    pallas_call x3, Pallas kernels, back(): pl.pallas_call(body, grid_spec=pltpu.PrefetchScalarGridSpec(num_scalar_pr...  13.1 us
    pallas_call x4, Pallas kernels, outward(): pl.pallas_call(outward_kernel, in_specs=[SCALARS] + [VECTORS] * (len(piec...  8.15 us
    pallas_call x2, Pallas kernels, solve(): pl.pallas_call(body, in_specs=[SCALARS] + [ANYWHERE] * (2 + len(staged)),...  5.78 us
    unnamed x26, local copies, waits for them, and re-layouts  5.22 us
  transfers between devices with their start and end apart: 33, of which 10 were waited for; matrix products, arithmetic and copies ran while one was open for 1% of the time, Pallas kernels for 28%

profile of v5, /device:TPU:0, one launch (start us, length us, event | category | flops | bytes accessed | tf_op | source)
XLA Modules:
  0.0 125.0 jit_solution(11356350005806838245)
XLA Ops:
  0.0 2.5 %solve.2.refs_0_.own_ref.inner_ref = bf16[4,192,512]{2,1,0:T(8,128)(2,1)S(1)} custom-call(s32[1]{0:T(128)} %bitcast.refs_0_.first_ref, bf16[8,192,512]{2,1,0:T(8,128)(2,1)} %bitcast.21, bf16[8,512,512]{2,1,0:T(8,128)(2,1)} %refs_10_.5), custom_call_target="tpu_custom_call" | custom-call | flops 1 | bytes 1 | tf_op jit(solution)/shard_map/solve/pallas_call | solution.py:66
  2.6 1.6 %collective-permute-start.3 = (bf16[4,192,512]{2,1,0:T(8,128)(2,1)S(1)}, bf16[4,192,512]{2,1,0:T(8,128)(2,1)}, u32[]{:S(2)}, u32[]{:S(2)}) collective-permute-start(bf16[4,192,512]{2,1,0:T(8,128)(2,1)S(1)} %solve.2.refs_0_.own_ref.inner_ref), channel_id=1, source_target_pairs={{1,2},{2,1},{3,4},{4,3},{5,6},{6,5},{7,8},{8,7},{9,10},{10,9},{11,... | collective-permute-start | bytes 2359304 | tf_op jit(solution)/shard_map/ppermute | solution.py:435
  4.2 3.2 %solve.3 = (bf16[4,192,512]{2,1,0:T(8,128)(2,1)S(1)}, bf16[2048,512]{1,0:T(8,128)(2,1)S(1)}, bf16[4,512,512]{2,1,0:T(8,128)(2,1)S(1)}) custom-call(s32[1]{0:T(128)} %bitcast.5.refs_0_.first_ref, bf16[8,192,512]{2,1,0:T(8,128)(2,1)} %bitcast.22, bf16[8,512,512]{2,1,0:T(8,128)(2,1)} %refs_10_.5, bf16[2048,512]{1,0:T(8,128)(2,1)} %refs_3_.1, ...), custom_call_target="tpu_custom_call" | custom-call | flops 1 | bytes 1 | tf_op jit(solution)/shard_map/solve/pallas_call | solution.py:66
  7.4 1.3 %copy-done.2 = bf16[4,512,512]{2,1,0:T(8,128)(2,1)} copy-done((bf16[4,512,512]{2,1,0:T(8,128)(2,1)}, bf16[4,512,512]{2,1,0:T(8,128)(2,1)S(1)}, u32[]{:S(2)}) %copy-start.2) | copy-done | bytes 2097176
  8.8 2.6 %outward.5 = bf16[8,96,256]{2,1,0:T(8,128)(2,1)} custom-call(s32[1]{0:T(128)} %bitcast.7.part_ref, bf16[4,192,512]{2,1,0:T(8,128)(2,1)S(1)} %solve.2.refs_0_.own_ref.inner_ref, bf16[4,192,512]{2,1,0:T(8,128)(2,1)S(1)} %get-tuple-element.47.refs_1_.inner_ref.own_ref, bf16[2048,512]{1,0:T(8,128)(2,1)S(1)} %get-tuple-element.35.refs_2_.refs_9_, ...), custom_call_target="tpu_custom_call" | custom-call | flops 1 | bytes 1 | tf_op jit(solution)/shard_map/outward/pallas_call | solution.py:110
  11.4 6.5 %collective-permute-start = (bf16[8,96,256]{2,1,0:T(8,128)(2,1)}, bf16[8,96,256]{2,1,0:T(8,128)(2,1)}, u32[]{:S(2)}, u32[]{:S(2)}) collective-permute-start(bf16[8,96,256]{2,1,0:T(8,128)(2,1)} %outward.5), channel_id=1, source_target_pairs={{0,8},{1,9},{2,10},{3,11},{4,12},{5,13},{6,14},{7,15},{8,0},{9,1},... | collective-permute-start | bytes 1179656 | tf_op jit(solution)/shard_map/ppermute | solution.py:384
  17.9 1.1 copy-done.6
  19.0 1.8 %outward.4 = bf16[8,96,256]{2,1,0:T(8,128)(2,1)S(1)} custom-call(s32[1]{0:T(128)} %bitcast.3.part_ref, bf16[4,192,512]{2,1,0:T(8,128)(2,1)S(1)} %solve.2.refs_0_.own_ref.inner_ref, bf16[4,192,512]{2,1,0:T(8,128)(2,1)S(1)} %copy-done.6, bf16[2048,512]{1,0:T(8,128)(2,1)S(1)} %get-tuple-element.35.refs_2_.refs_9_, f32[8,2048]{1,0:T(8,128)S(1)} %maximum_convert_fusion.refs_3_), custom_call_target="tpu_custom_call" | custom-call | flops 1 | bytes 1 | tf_op jit(solution)/shard_map/outward/pallas_call | solution.py:110
  20.9 0.9 convert_element_type.7
  21.8 0.1 pad_add_fusion.place_ref
  22.0 1.2 split.2
  23.2 1.6 %collective-permute-start.1 = (bf16[8,48,256]{2,1,0:T(8,128)(2,1)S(1)}, bf16[8,48,256]{2,1,0:T(8,128)(2,1)S(1)}, u32[]{:S(2)}, u32[]{:S(2)}) collective-permute-start(bf16[8,48,256]{2,1,0:T(8,128)(2,1)S(1)} %get-tuple-element.37), channel_id=1, source_target_pairs={{0,16},{1,17},{2,18},{3,19},{4,20},{5,21},{6,22},{7,23},{8,24},{9,... | collective-permute-start | bytes 589832 | tf_op jit(solution)/shard_map/ppermute | solution.py:384
  24.7 0.1 fusion.8
  24.8 0.1 collective-permute-start.7
  24.9 0.9 collective-permute-start.8
  25.8 3.5 %collective-permute-start.9 = (bf16[2,128,128]{2,1,0:T(8,128)(2,1)S(1)}, bf16[2,128,128]{2,1,0:T(8,128)(2,1)S(1)}, u32[]{:S(2)}, u32[]{:S(2)}) collective-permute-start(bf16[2,128,128]{2,1,0:T(8,128)(2,1)S(1)} %convert_element_type.7), channel_id=1, source_target_pairs={{0,6},{1,7},{2,4},{3,5},{4,2},{5,3},{6,0},{7,1},{8,14},{9,15},{10,... | collective-permute-start | bytes 196616 | tf_op jit(solution)/shard_map/ppermute | solution.py:384
  29.3 0.8 collective-permute-done.1.got_ref
  30.0 0.6 deal.2
  30.6 2.9 %collective-permute-start.2 = (bf16[4,48,256]{2,1,0:T(8,128)(2,1)S(1)}, bf16[4,48,256]{2,1,0:T(8,128)(2,1)S(1)}, u32[]{:S(2)}, u32[]{:S(2)}) collective-permute-start(bf16[4,48,256]{2,1,0:T(8,128)(2,1)S(1)} %get-tuple-element.39), channel_id=1, source_target_pairs={{0,17},{1,16},{2,19},{3,18},{4,21},{5,20},{6,23},{7,22},{8,25},{9,... | collective-permute-start | bytes 294920 | tf_op jit(solution)/shard_map/ppermute | solution.py:384
  33.6 2.8 %collective-permute-done.2.refs_1_ = bf16[4,48,256]{2,1,0:T(8,128)(2,1)S(1)} collective-permute-done((bf16[4,48,256]{2,1,0:T(8,128)(2,1)S(1)}, bf16[4,48,256]{2,1,0:T(8,128)(2,1)S(1)}, u32[]{:S(2)}, u32[]{:S(2)}) %collective-permute-start.2) | collective-permute-done | bytes 98336 | tf_op jit(solution)/shard_map/ppermute | solution.py:384
  36.4 0.8 collective-permute-start.13
  37.3 0.6 collective-permute-start.4
  37.9 3.1 %collective-permute-start.5 = (bf16[4,48,256]{2,1,0:T(8,128)(2,1)S(1)}, bf16[4,48,256]{2,1,0:T(8,128)(2,1)S(1)}, u32[]{:S(2)}, u32[]{:S(2)}) collective-permute-start(bf16[4,48,256]{2,1,0:T(8,128)(2,1)S(1)} %add.115.refs_0_), channel_id=1, source_target_pairs={{0,6},{1,7},{2,4},{3,5},{4,2},{5,3},{6,0},{7,1},{8,14},{9,15},{10,... | collective-permute-start | bytes 294920 | tf_op jit(solution)/shard_map/ppermute | solution.py:384
  41.0 0.5 collective-permute-start.6
  41.5 1.6 %copy-done.3 = bf16[4,512,512]{2,1,0:T(8,128)(2,1)S(1)} copy-done((bf16[4,512,512]{2,1,0:T(8,128)(2,1)S(1)}, bf16[4,512,512]{2,1,0:T(8,128)(2,1)}, u32[]{:S(2)}) %copy-start.3) | copy-done | bytes 2097176
  43.1 1.1 copy-done.7
  44.2 4.9 %near.4.refs_11_ = f32[4,192,512]{2,1,0:T(8,128)S(1)} custom-call(s32[1]{0:T(128)} %bitcast.refs_0_.first_ref, s32[4,6]{1,0:T(4,128)S(1)} %constant_dynamic-slice_fusion.3.slot_ref, s32[4]{0:T(128)S(1)} %get-tuple-element.70.count_ref, s32[4,6]{1,0:T(4,128)S(1)} %get-tuple-element.66.type_ref, bf16[4,192,512]{2,1,0:T(8,128)(2,1)} %collective-permute-done.3.halo_ref, ...), custom_call_target="tpu_custom_call" | custom-call | flops 1 | bytes 1 | tf_op jit(solution)/shard_map/near/pallas_call | solution.py:256
  49.2 0.3 reflect.2.refs_0_
  49.5 1.3 %collective-permute-start.10 = (bf16[4,48,256]{2,1,0:T(8,128)(2,1)S(1)}, bf16[4,48,256]{2,1,0:T(8,128)(2,1)S(1)}, u32[]{:S(2)}, u32[]{:S(2)}) collective-permute-start(bf16[4,48,256]{2,1,0:T(8,128)(2,1)S(1)} %reflect.2.refs_0_), channel_id=1, source_target_pairs={{0,17},{1,16},{2,19},{3,18},{4,21},{5,20},{6,23},{7,22},{8,25},{9,... | collective-permute-start | bytes 294920 | tf_op jit(solution)/shard_map/ppermute | solution.py:384
  50.7 2.0 %collective-permute-start.11 = (bf16[4,48,256]{2,1,0:T(8,128)(2,1)S(1)}, bf16[4,48,256]{2,1,0:T(8,128)(2,1)S(1)}, u32[]{:S(2)}, u32[]{:S(2)}) collective-permute-start(bf16[4,48,256]{2,1,0:T(8,128)(2,1)S(1)} %reflect.2.refs_0_), channel_id=1, source_target_pairs={{0,16},{1,17},{2,18},{3,19},{4,20},{5,21},{6,22},{7,23},{8,24},{9,... | collective-permute-start | bytes 294920 | tf_op jit(solution)/shard_map/ppermute | solution.py:384
  52.7 2.4 %collective-permute-done.10.refs_1_ = bf16[4,48,256]{2,1,0:T(8,128)(2,1)S(1)} collective-permute-done((bf16[4,48,256]{2,1,0:T(8,128)(2,1)S(1)}, bf16[4,48,256]{2,1,0:T(8,128)(2,1)S(1)}, u32[]{:S(2)}, u32[]{:S(2)}) %collective-permute-start.10) | collective-permute-done | bytes 98336 | tf_op jit(solution)/shard_map/ppermute | solution.py:384
  55.1 2.5 %collective-permute-start.12 = (bf16[4,48,256]{2,1,0:T(8,128)(2,1)S(1)}, bf16[4,48,256]{2,1,0:T(8,128)(2,1)S(1)}, u32[]{:S(2)}, u32[]{:S(2)}) collective-permute-start(bf16[4,48,256]{2,1,0:T(8,128)(2,1)S(1)} %collective-permute-done.10.refs_1_), channel_id=1, source_target_pairs={{0,16},{1,17},{2,18},{3,19},{4,20},{5,21},{6,22},{7,23},{8,24},{9,... | collective-permute-start | bytes 294920 | tf_op jit(solution)/shard_map/ppermute | solution.py:384
  57.6 0.5 collective-permute-start.15
  58.2 3.9 %near.5.refs_11_ = f32[4,192,512]{2,1,0:T(8,128)S(1)} custom-call(s32[1]{0:T(128)} %bitcast.5.refs_0_.first_ref, s32[4,6]{1,0:T(4,128)S(1)} %constant_dynamic-slice_fusion.1.slot_ref, s32[4]{0:T(128)S(1)} %get-tuple-element.69.count_ref, s32[4,6]{1,0:T(4,128)S(1)} %get-tuple-element.65.type_ref, bf16[4,192,512]{2,1,0:T(8,128)(2,1)S(1)} %collective-permute-done.13.halo_ref, ...), custom_call_target="tpu_custom_call" | custom-call | flops 1 | bytes 1 | tf_op jit(solution)/shard_map/near/pallas_call | solution.py:256
  62.2 0.5 collective-permute-start.17
  62.7 0.9 collective-permute-done.17.refs_7_
  63.6 3.3 %back.3.refs_0_.own_ref.inner_ref = bf16[4,192,512]{2,1,0:T(8,128)(2,1)S(1)} custom-call(s32[1]{0:T(128)} %bitcast.refs_0_.first_ref, s32[3]{0:T(128)S(1)} %pad_add_fusion.place_ref, bf16[4,48,256]{2,1,0:T(8,128)(2,1)S(1)} %reflect.2.refs_0_, bf16[4,48,256]{2,1,0:T(8,128)(2,1)S(1)} %collective-permute-done.10.refs_1_, ...), custom_call_target="tpu_custom_call" | custom-call | flops 1 | bytes 1 | tf_op jit(solution)/shard_map/back/pallas_call | solution.py:332
  66.9 0.7 collective-permute-start.21
  67.6 3.3 %back.4.refs_1_.inner_ref.own_ref = bf16[4,192,512]{2,1,0:T(8,128)(2,1)S(1)} custom-call(s32[1]{0:T(128)} %bitcast.5.refs_0_.first_ref, s32[3]{0:T(128)S(1)} %pad_add_fusion.place_ref, bf16[4,48,256]{2,1,0:T(8,128)(2,1)S(1)} %reflect.2.refs_0_, bf16[4,48,256]{2,1,0:T(8,128)(2,1)S(1)} %collective-permute-done.10.refs_1_, ...), custom_call_target="tpu_custom_call" | custom-call | flops 1 | bytes 1 | tf_op jit(solution)/shard_map/back/pallas_call | solution.py:332
  70.9 1.9 %outward.7 = bf16[8,96,256]{2,1,0:T(8,128)(2,1)S(1)} custom-call(s32[1]{0:T(128)} %bitcast.7.part_ref, bf16[4,192,512]{2,1,0:T(8,128)(2,1)S(1)} %back.3.refs_0_.own_ref.inner_ref, bf16[4,192,512]{2,1,0:T(8,128)(2,1)S(1)} %back.4.refs_1_.inner_ref.own_ref, bf16[2048,512]{1,0:T(8,128)(2,1)S(1)} %get-tuple-element.35.refs_2_.refs_9_, ...), custom_call_target="tpu_custom_call" | custom-call | flops 1 | bytes 1 | tf_op jit(solution)/shard_map/outward/pallas_call | solution.py:110
  72.8 4.1 %collective-permute-start.18 = (bf16[8,96,256]{2,1,0:T(8,128)(2,1)S(1)}, bf16[8,96,256]{2,1,0:T(8,128)(2,1)S(1)}, u32[]{:S(2)}, u32[]{:S(2)}) collective-permute-start(bf16[8,96,256]{2,1,0:T(8,128)(2,1)S(1)} %outward.7), channel_id=1, source_target_pairs={{0,8},{1,9},{2,10},{3,11},{4,12},{5,13},{6,14},{7,15},{8,0},{9,1},... | collective-permute-start | bytes 1179656 | tf_op jit(solution)/shard_map/ppermute | solution.py:384
  76.9 1.9 %outward.6 = bf16[8,96,256]{2,1,0:T(8,128)(2,1)S(1)} custom-call(s32[1]{0:T(128)} %bitcast.3.part_ref, bf16[4,192,512]{2,1,0:T(8,128)(2,1)S(1)} %back.3.refs_0_.own_ref.inner_ref, bf16[4,192,512]{2,1,0:T(8,128)(2,1)S(1)} %back.4.refs_1_.inner_ref.own_ref, bf16[2048,512]{1,0:T(8,128)(2,1)S(1)} %get-tuple-element.35.refs_2_.refs_9_, ...), custom_call_target="tpu_custom_call" | custom-call | flops 1 | bytes 1 | tf_op jit(solution)/shard_map/outward/pallas_call | solution.py:110
  78.8 0.6 split.3
  79.4 1.9 %collective-permute-start.19 = (bf16[8,48,256]{2,1,0:T(8,128)(2,1)S(1)}, bf16[8,48,256]{2,1,0:T(8,128)(2,1)S(1)}, u32[]{:S(2)}, u32[]{:S(2)}) collective-permute-start(bf16[8,48,256]{2,1,0:T(8,128)(2,1)S(1)} %get-tuple-element.53), channel_id=1, source_target_pairs={{0,16},{1,17},{2,18},{3,19},{4,20},{5,21},{6,22},{7,23},{8,24},{9,... | collective-permute-start | bytes 589832 | tf_op jit(solution)/shard_map/ppermute | solution.py:384
  81.3 5.1 %collective-permute-done.19.got_ref = bf16[8,48,256]{2,1,0:T(8,128)(2,1)S(1)} collective-permute-done((bf16[8,48,256]{2,1,0:T(8,128)(2,1)S(1)}, bf16[8,48,256]{2,1,0:T(8,128)(2,1)S(1)}, u32[]{:S(2)}, u32[]{:S(2)}) %collective-permute-start.19) | collective-permute-done | bytes 196640 | tf_op jit(solution)/shard_map/ppermute | solution.py:384
  86.4 0.6 deal.3
  87.0 3.8 %collective-permute-start.20 = (bf16[4,48,256]{2,1,0:T(8,128)(2,1)S(1)}, bf16[4,48,256]{2,1,0:T(8,128)(2,1)S(1)}, u32[]{:S(2)}, u32[]{:S(2)}) collective-permute-start(bf16[4,48,256]{2,1,0:T(8,128)(2,1)S(1)} %get-tuple-element.55), channel_id=1, source_target_pairs={{0,17},{1,16},{2,19},{3,18},{4,21},{5,20},{6,23},{7,22},{8,25},{9,... | collective-permute-start | bytes 294920 | tf_op jit(solution)/shard_map/ppermute | solution.py:384
  90.8 2.6 %collective-permute-done.20.refs_1_ = bf16[4,48,256]{2,1,0:T(8,128)(2,1)S(1)} collective-permute-done((bf16[4,48,256]{2,1,0:T(8,128)(2,1)S(1)}, bf16[4,48,256]{2,1,0:T(8,128)(2,1)S(1)}, u32[]{:S(2)}, u32[]{:S(2)}) %collective-permute-start.20) | collective-permute-done | bytes 98336 | tf_op jit(solution)/shard_map/ppermute | solution.py:384
  93.5 0.9 collective-permute-start.32
  94.4 0.7 collective-permute-start.22
  95.1 1.7 %collective-permute-start.23 = (bf16[4,48,256]{2,1,0:T(8,128)(2,1)S(1)}, bf16[4,48,256]{2,1,0:T(8,128)(2,1)S(1)}, u32[]{:S(2)}, u32[]{:S(2)}) collective-permute-start(bf16[4,48,256]{2,1,0:T(8,128)(2,1)S(1)} %add.116.refs_0_), channel_id=1, source_target_pairs={{0,6},{1,7},{2,4},{3,5},{4,2},{5,3},{6,0},{7,1},{8,14},{9,15},{10,... | collective-permute-start | bytes 294920 | tf_op jit(solution)/shard_map/ppermute | solution.py:384
  96.8 1.0 collective-permute-start.24
  97.9 3.8 %near.6.refs_11_ = f32[4,192,512]{2,1,0:T(8,128)S(1)} custom-call(s32[1]{0:T(128)} %bitcast.refs_0_.first_ref, s32[4,6]{1,0:T(4,128)S(1)} %constant_dynamic-slice_fusion.3.slot_ref, s32[4]{0:T(128)S(1)} %get-tuple-element.70.count_ref, s32[4,6]{1,0:T(4,128)S(1)} %get-tuple-element.66.type_ref, bf16[4,192,512]{2,1,0:T(8,128)(2,1)S(1)} %collective-permute-done.21.halo_ref, ...), custom_call_target="tpu_custom_call" | custom-call | flops 1 | bytes 1 | tf_op jit(solution)/shard_map/near/pallas_call | solution.py:256
  101.7 1.6 %collective-permute-done.22.refs_1_ = bf16[4,48,256]{2,1,0:T(8,128)(2,1)S(1)} collective-permute-done((bf16[4,48,256]{2,1,0:T(8,128)(2,1)S(1)}, bf16[4,48,256]{2,1,0:T(8,128)(2,1)S(1)}, u32[]{:S(2)}, u32[]{:S(2)}) %collective-permute-start.22) | collective-permute-done | bytes 98336 | tf_op jit(solution)/shard_map/ppermute | solution.py:384
  103.2 0.2 collective-permute-done.24.refs_3_
  103.4 0.3 reflect.3.refs_0_
  103.7 1.5 %collective-permute-start.25 = (bf16[4,48,256]{2,1,0:T(8,128)(2,1)S(1)}, bf16[4,48,256]{2,1,0:T(8,128)(2,1)S(1)}, u32[]{:S(2)}, u32[]{:S(2)}) collective-permute-start(bf16[4,48,256]{2,1,0:T(8,128)(2,1)S(1)} %reflect.3.refs_0_), channel_id=1, source_target_pairs={{0,17},{1,16},{2,19},{3,18},{4,21},{5,20},{6,23},{7,22},{8,25},{9,... | collective-permute-start | bytes 294920 | tf_op jit(solution)/shard_map/ppermute | solution.py:384
  105.2 1.3 %collective-permute-start.26 = (bf16[4,48,256]{2,1,0:T(8,128)(2,1)S(1)}, bf16[4,48,256]{2,1,0:T(8,128)(2,1)S(1)}, u32[]{:S(2)}, u32[]{:S(2)}) collective-permute-start(bf16[4,48,256]{2,1,0:T(8,128)(2,1)S(1)} %reflect.3.refs_0_), channel_id=1, source_target_pairs={{0,16},{1,17},{2,18},{3,19},{4,20},{5,21},{6,22},{7,23},{8,24},{9,... | collective-permute-start | bytes 294920 | tf_op jit(solution)/shard_map/ppermute | solution.py:384
  106.5 3.0 %collective-permute-done.25.refs_1_ = bf16[4,48,256]{2,1,0:T(8,128)(2,1)S(1)} collective-permute-done((bf16[4,48,256]{2,1,0:T(8,128)(2,1)S(1)}, bf16[4,48,256]{2,1,0:T(8,128)(2,1)S(1)}, u32[]{:S(2)}, u32[]{:S(2)}) %collective-permute-start.25) | collective-permute-done | bytes 98336 | tf_op jit(solution)/shard_map/ppermute | solution.py:384
  109.5 2.4 %collective-permute-start.27 = (bf16[4,48,256]{2,1,0:T(8,128)(2,1)S(1)}, bf16[4,48,256]{2,1,0:T(8,128)(2,1)S(1)}, u32[]{:S(2)}, u32[]{:S(2)}) collective-permute-start(bf16[4,48,256]{2,1,0:T(8,128)(2,1)S(1)} %collective-permute-done.25.refs_1_), channel_id=1, source_target_pairs={{0,16},{1,17},{2,18},{3,19},{4,20},{5,21},{6,22},{7,23},{8,24},{9,... | collective-permute-start | bytes 294920 | tf_op jit(solution)/shard_map/ppermute | solution.py:384
  112.0 0.5 collective-permute-start.29
  112.5 2.1 %collective-permute-done.27.refs_3_ = bf16[4,48,256]{2,1,0:T(8,128)(2,1)S(1)} collective-permute-done((bf16[4,48,256]{2,1,0:T(8,128)(2,1)S(1)}, bf16[4,48,256]{2,1,0:T(8,128)(2,1)S(1)}, u32[]{:S(2)}, u32[]{:S(2)}) %collective-permute-start.27) | collective-permute-done | bytes 98336 | tf_op jit(solution)/shard_map/ppermute | solution.py:384
  114.6 4.0 %near.7.refs_12_ = f32[4,192,512]{2,1,0:T(8,128)S(1)} custom-call(s32[1]{0:T(128)} %bitcast.5.refs_0_.first_ref, s32[4,6]{1,0:T(4,128)S(1)} %constant_dynamic-slice_fusion.1.slot_ref, s32[4]{0:T(128)S(1)} %get-tuple-element.69.count_ref, s32[4,6]{1,0:T(4,128)S(1)} %get-tuple-element.65.type_ref, bf16[4,192,512]{2,1,0:T(8,128)(2,1)S(1)} %collective-permute-done.32.halo_ref, ...), custom_call_target="tpu_custom_call" | custom-call | flops 1 | bytes 1 | tf_op jit(solution)/shard_map/near/pallas_call | solution.py:256
  118.6 6.5 %back.5 = bf16[8,192,512]{2,1,0:T(8,128)(2,1)} custom-call(s32[1]{0:T(128)} %bitcast.refs_0_.first_ref, s32[3]{0:T(128)S(1)} %pad_add_fusion.place_ref, bf16[4,48,256]{2,1,0:T(8,128)(2,1)S(1)} %reflect.3.refs_0_, bf16[4,48,256]{2,1,0:T(8,128)(2,1)S(1)} %collective-permute-done.25.refs_1_, bf16[4,48,256]{2,1,0:T(8,128)(2,1)S(1)} %collective-permute-done.26.refs_2_, ...), custom_call_target="tpu_custom_call" | custom-call | flops 1 | bytes 1 | tf_op jit(solution)/shard_map/back/pallas_call | solution.py:332
  (64 shorter events, 0.5 us)
Async XLA Ops:
  0.0 4.1 %copy-start.9 = (bf16[8,2048]{1,0:T(8,128)(2,1)S(1)}, bf16[8,2048]{1,0:T(8,128)(2,1)}, u32[]{:S(2)}) copy-start(bf16[8,2048]{1,0:T(8,128)(2,1)} %param.15) | copy-start | bytes 98308
  2.6 33.8 %collective-permute-start.3 = (bf16[4,192,512]{2,1,0:T(8,128)(2,1)S(1)}, bf16[4,192,512]{2,1,0:T(8,128)(2,1)}, u32[]{:S(2)}, u32[]{:S(2)}) collective-permute-start(bf16[4,192,512]{2,1,0:T(8,128)(2,1)S(1)} %solve.2.refs_0_.own_ref.inner_ref), channel_id=1, source_target_pairs={{1,2},{2,1},{3,4},{4,3},{5,6},{6,5},{7,8},{8,7},{9,10},{10,9},{11,... | collective-permute-start | bytes 2359304 | tf_op jit(solution)/shard_map/ppermute | solution.py:435
  7.4 1.3 %copy-start.2 = (bf16[4,512,512]{2,1,0:T(8,128)(2,1)}, bf16[4,512,512]{2,1,0:T(8,128)(2,1)S(1)}, u32[]{:S(2)}) copy-start(bf16[4,512,512]{2,1,0:T(8,128)(2,1)S(1)} %get-tuple-element.42.translations_ref) | copy-start | bytes 6291460
  8.8 2.6 %copy-start.5 = (bf16[4,192,512]{2,1,0:T(8,128)(2,1)}, bf16[4,192,512]{2,1,0:T(8,128)(2,1)S(1)}, u32[]{:S(2)}) copy-start(bf16[4,192,512]{2,1,0:T(8,128)(2,1)S(1)} %get-tuple-element.47.refs_1_.inner_ref.own_ref) | copy-start | bytes 2359300
  11.4 10.6 %collective-permute-start = (bf16[8,96,256]{2,1,0:T(8,128)(2,1)}, bf16[8,96,256]{2,1,0:T(8,128)(2,1)}, u32[]{:S(2)}, u32[]{:S(2)}) collective-permute-start(bf16[8,96,256]{2,1,0:T(8,128)(2,1)} %outward.5), channel_id=1, source_target_pairs={{0,8},{1,9},{2,10},{3,11},{4,12},{5,13},{6,14},{7,15},{8,0},{9,1},... | collective-permute-start | bytes 1179656 | tf_op jit(solution)/shard_map/ppermute | solution.py:384
  17.9 1.1 copy-start.6
  19.0 2.9 %copy-start.10 = (s32[8,6]{1,0:T(8,128)S(1)}, s32[8,6]{1,0:T(8,128)}, u32[]{:S(2)}) copy-start(s32[8,6]{1,0:T(8,128)} %param.12) | copy-start | bytes 580
  19.0 5.7 %copy-start.12 = (s32[8]{0:T(128)S(1)}, s32[8]{0:T(128)}, u32[]{:S(2)}) copy-start(s32[8]{0:T(128)} %param.13) | copy-start | bytes 100
  19.0 5.8 %copy-start.11 = (s32[8,6]{1,0:T(8,128)S(1)}, s32[8,6]{1,0:T(8,128)}, u32[]{:S(2)}) copy-start(s32[8,6]{1,0:T(8,128)} %param.14) | copy-start | bytes 580
  21.8 19.7 %copy-start.1 = (bf16[8,512,192]{1,2,0:T(8,128)(2,1)S(1)}, bf16[8,512,192]{1,2,0:T(8,128)(2,1)}, u32[]{:S(2)}) copy-start(bf16[8,512,192]{1,2,0:T(8,128)(2,1)} %param.9) | copy-start | bytes 4718596
  23.2 6.9 %collective-permute-start.1 = (bf16[8,48,256]{2,1,0:T(8,128)(2,1)S(1)}, bf16[8,48,256]{2,1,0:T(8,128)(2,1)S(1)}, u32[]{:S(2)}, u32[]{:S(2)}) collective-permute-start(bf16[8,48,256]{2,1,0:T(8,128)(2,1)S(1)} %get-tuple-element.37), channel_id=1, source_target_pairs={{0,16},{1,17},{2,18},{3,19},{4,20},{5,21},{6,22},{7,23},{8,24},{9,... | collective-permute-start | bytes 589832 | tf_op jit(solution)/shard_map/ppermute | solution.py:384
  24.8 12.4 %collective-permute-start.7 = (bf16[2,128,128]{2,1,0:T(8,128)(2,1)S(1)}, bf16[2,128,128]{2,1,0:T(8,128)(2,1)S(1)}, u32[]{:S(2)}, u32[]{:S(2)}) collective-permute-start(bf16[2,128,128]{2,1,0:T(8,128)(2,1)S(1)} %convert_element_type.7), channel_id=1, source_target_pairs={{0,2},{1,3},{2,0},{3,1},{4,6},{5,7},{6,4},{7,5},{8,10},{9,11},{10,... | collective-permute-start | bytes 196616 | tf_op jit(solution)/shard_map/ppermute | solution.py:384
  24.9 12.4 %collective-permute-start.8 = (bf16[2,128,128]{2,1,0:T(8,128)(2,1)S(1)}, bf16[2,128,128]{2,1,0:T(8,128)(2,1)S(1)}, u32[]{:S(2)}, u32[]{:S(2)}) collective-permute-start(bf16[2,128,128]{2,1,0:T(8,128)(2,1)S(1)} %convert_element_type.7), channel_id=1, source_target_pairs={{0,4},{1,5},{2,6},{3,7},{4,0},{5,1},{6,2},{7,3},{8,12},{9,13},{10,... | collective-permute-start | bytes 196616 | tf_op jit(solution)/shard_map/ppermute | solution.py:384
  25.8 15.7 %collective-permute-start.9 = (bf16[2,128,128]{2,1,0:T(8,128)(2,1)S(1)}, bf16[2,128,128]{2,1,0:T(8,128)(2,1)S(1)}, u32[]{:S(2)}, u32[]{:S(2)}) collective-permute-start(bf16[2,128,128]{2,1,0:T(8,128)(2,1)S(1)} %convert_element_type.7), channel_id=1, source_target_pairs={{0,6},{1,7},{2,4},{3,5},{4,2},{5,3},{6,0},{7,1},{8,14},{9,15},{10,... | collective-permute-start | bytes 196616 | tf_op jit(solution)/shard_map/ppermute | solution.py:384
  30.6 5.7 %collective-permute-start.2 = (bf16[4,48,256]{2,1,0:T(8,128)(2,1)S(1)}, bf16[4,48,256]{2,1,0:T(8,128)(2,1)S(1)}, u32[]{:S(2)}, u32[]{:S(2)}) collective-permute-start(bf16[4,48,256]{2,1,0:T(8,128)(2,1)S(1)} %get-tuple-element.39), channel_id=1, source_target_pairs={{0,17},{1,16},{2,19},{3,18},{4,21},{5,20},{6,23},{7,22},{8,25},{9,... | collective-permute-start | bytes 294920 | tf_op jit(solution)/shard_map/ppermute | solution.py:384
  36.4 21.8 %collective-permute-start.13 = (bf16[4,192,512]{2,1,0:T(8,128)(2,1)}, bf16[4,192,512]{2,1,0:T(8,128)(2,1)S(1)}, u32[]{:S(2)}, u32[]{:S(2)}) collective-permute-start(bf16[4,192,512]{2,1,0:T(8,128)(2,1)} %copy-done.5), channel_id=1, source_target_pairs={{0,1},{1,0},{2,3},{3,2},{4,5},{5,4},{6,7},{7,6},{8,9},{9,8},{10,11... | collective-permute-start | bytes 2359304 | tf_op jit(solution)/shard_map/ppermute | solution.py:455
  37.3 11.8 %collective-permute-start.4 = (bf16[4,48,256]{2,1,0:T(8,128)(2,1)S(1)}, bf16[4,48,256]{2,1,0:T(8,128)(2,1)S(1)}, u32[]{:S(2)}, u32[]{:S(2)}) collective-permute-start(bf16[4,48,256]{2,1,0:T(8,128)(2,1)S(1)} %add.115.refs_0_), channel_id=1, source_target_pairs={{0,4},{1,5},{2,6},{3,7},{4,0},{5,1},{6,2},{7,3},{8,12},{9,13},{10,... | collective-permute-start | bytes 294920 | tf_op jit(solution)/shard_map/ppermute | solution.py:384
  37.9 11.2 %collective-permute-start.5 = (bf16[4,48,256]{2,1,0:T(8,128)(2,1)S(1)}, bf16[4,48,256]{2,1,0:T(8,128)(2,1)S(1)}, u32[]{:S(2)}, u32[]{:S(2)}) collective-permute-start(bf16[4,48,256]{2,1,0:T(8,128)(2,1)S(1)} %add.115.refs_0_), channel_id=1, source_target_pairs={{0,6},{1,7},{2,4},{3,5},{4,2},{5,3},{6,0},{7,1},{8,14},{9,15},{10,... | collective-permute-start | bytes 294920 | tf_op jit(solution)/shard_map/ppermute | solution.py:384
  41.0 8.2 %collective-permute-start.6 = (bf16[4,48,256]{2,1,0:T(8,128)(2,1)S(1)}, bf16[4,48,256]{2,1,0:T(8,128)(2,1)S(1)}, u32[]{:S(2)}, u32[]{:S(2)}) collective-permute-start(bf16[4,48,256]{2,1,0:T(8,128)(2,1)S(1)} %add.115.refs_0_), channel_id=1, source_target_pairs={{0,2},{1,3},{2,0},{3,1},{4,6},{5,7},{6,4},{7,5},{8,10},{9,11},{10,... | collective-permute-start | bytes 294920 | tf_op jit(solution)/shard_map/ppermute | solution.py:384
  41.5 1.6 %copy-start.3 = (bf16[4,512,512]{2,1,0:T(8,128)(2,1)S(1)}, bf16[4,512,512]{2,1,0:T(8,128)(2,1)}, u32[]{:S(2)}) copy-start(bf16[4,512,512]{2,1,0:T(8,128)(2,1)} %copy-done.2) | copy-start | bytes 6291460
  43.1 1.1 copy-start.7
  44.2 14.0 %copy-start.8 = (bf16[4,192,512]{2,1,0:T(8,128)(2,1)S(1)}, bf16[4,192,512]{2,1,0:T(8,128)(2,1)}, u32[]{:S(2)}) copy-start(bf16[4,192,512]{2,1,0:T(8,128)(2,1)} %copy-done.5) | copy-start | bytes 2359300
  49.5 5.7 %collective-permute-start.10 = (bf16[4,48,256]{2,1,0:T(8,128)(2,1)S(1)}, bf16[4,48,256]{2,1,0:T(8,128)(2,1)S(1)}, u32[]{:S(2)}, u32[]{:S(2)}) collective-permute-start(bf16[4,48,256]{2,1,0:T(8,128)(2,1)S(1)} %reflect.2.refs_0_), channel_id=1, source_target_pairs={{0,17},{1,16},{2,19},{3,18},{4,21},{5,20},{6,23},{7,22},{8,25},{9,... | collective-permute-start | bytes 294920 | tf_op jit(solution)/shard_map/ppermute | solution.py:384
  50.7 7.4 %collective-permute-start.11 = (bf16[4,48,256]{2,1,0:T(8,128)(2,1)S(1)}, bf16[4,48,256]{2,1,0:T(8,128)(2,1)S(1)}, u32[]{:S(2)}, u32[]{:S(2)}) collective-permute-start(bf16[4,48,256]{2,1,0:T(8,128)(2,1)S(1)} %reflect.2.refs_0_), channel_id=1, source_target_pairs={{0,16},{1,17},{2,18},{3,19},{4,20},{5,21},{6,22},{7,23},{8,24},{9,... | collective-permute-start | bytes 294920 | tf_op jit(solution)/shard_map/ppermute | solution.py:384
  55.1 7.0 %collective-permute-start.12 = (bf16[4,48,256]{2,1,0:T(8,128)(2,1)S(1)}, bf16[4,48,256]{2,1,0:T(8,128)(2,1)S(1)}, u32[]{:S(2)}, u32[]{:S(2)}) collective-permute-start(bf16[4,48,256]{2,1,0:T(8,128)(2,1)S(1)} %collective-permute-done.10.refs_1_), channel_id=1, source_target_pairs={{0,16},{1,17},{2,18},{3,19},{4,20},{5,21},{6,22},{7,23},{8,24},{9,... | collective-permute-start | bytes 294920 | tf_op jit(solution)/shard_map/ppermute | solution.py:384
  57.6 5.1 %collective-permute-start.14 = (bf16[4,48,256]{2,1,0:T(8,128)(2,1)S(1)}, bf16[4,48,256]{2,1,0:T(8,128)(2,1)S(1)}, u32[]{:S(2)}, u32[]{:S(2)}) collective-permute-start(bf16[4,48,256]{2,1,0:T(8,128)(2,1)S(1)} %reflect.2.refs_0_), channel_id=1, source_target_pairs={{0,8},{1,9},{2,10},{3,11},{4,12},{5,13},{6,14},{7,15},{8,0},{9,1},... | collective-permute-start | bytes 294920 | tf_op jit(solution)/shard_map/ppermute | solution.py:384
  57.6 5.1 %collective-permute-start.15 = (bf16[4,48,256]{2,1,0:T(8,128)(2,1)S(1)}, bf16[4,48,256]{2,1,0:T(8,128)(2,1)S(1)}, u32[]{:S(2)}, u32[]{:S(2)}) collective-permute-start(bf16[4,48,256]{2,1,0:T(8,128)(2,1)S(1)} %collective-permute-done.10.refs_1_), channel_id=1, source_target_pairs={{0,8},{1,9},{2,10},{3,11},{4,12},{5,13},{6,14},{7,15},{8,0},{9,1},... | collective-permute-start | bytes 294920 | tf_op jit(solution)/shard_map/ppermute | solution.py:384
  58.1 4.6 %collective-permute-start.16 = (bf16[4,48,256]{2,1,0:T(8,128)(2,1)S(1)}, bf16[4,48,256]{2,1,0:T(8,128)(2,1)S(1)}, u32[]{:S(2)}, u32[]{:S(2)}) collective-permute-start(bf16[4,48,256]{2,1,0:T(8,128)(2,1)S(1)} %collective-permute-done.11.refs_2_), channel_id=1, source_target_pairs={{0,8},{1,9},{2,10},{3,11},{4,12},{5,13},{6,14},{7,15},{8,0},{9,1},... | collective-permute-start | bytes 294920 | tf_op jit(solution)/shard_map/ppermute | solution.py:384
  58.2 5.4 %copy-start = (bf16[8,512,512]{2,1,0:T(8,128)(2,1)S(1)}, bf16[8,512,512]{2,1,0:T(8,128)(2,1)}, u32[]{:S(2)}) copy-start(bf16[8,512,512]{2,1,0:T(8,128)(2,1)} %refs_10_.5) | copy-start | bytes 12582916
  62.2 1.4 %collective-permute-start.17 = (bf16[4,48,256]{2,1,0:T(8,128)(2,1)S(1)}, bf16[4,48,256]{2,1,0:T(8,128)(2,1)S(1)}, u32[]{:S(2)}, u32[]{:S(2)}) collective-permute-start(bf16[4,48,256]{2,1,0:T(8,128)(2,1)S(1)} %collective-permute-done.12.refs_3_), channel_id=1, source_target_pairs={{0,8},{1,9},{2,10},{3,11},{4,12},{5,13},{6,14},{7,15},{8,0},{9,1},... | collective-permute-start | bytes 294920 | tf_op jit(solution)/shard_map/ppermute | solution.py:384
  66.9 26.5 %collective-permute-start.21 = (bf16[4,192,512]{2,1,0:T(8,128)(2,1)S(1)}, bf16[4,192,512]{2,1,0:T(8,128)(2,1)S(1)}, u32[]{:S(2)}, u32[]{:S(2)}) collective-permute-start(bf16[4,192,512]{2,1,0:T(8,128)(2,1)S(1)} %back.3.refs_0_.own_ref.inner_ref), channel_id=1, source_target_pairs={{1,2},{2,1},{3,4},{4,3},{5,6},{6,5},{7,8},{8,7},{9,10},{10,9},{11,... | collective-permute-start | bytes 2359304 | tf_op jit(solution)/shard_map/ppermute | solution.py:435
  72.8 6.0 %collective-permute-start.18 = (bf16[8,96,256]{2,1,0:T(8,128)(2,1)S(1)}, bf16[8,96,256]{2,1,0:T(8,128)(2,1)S(1)}, u32[]{:S(2)}, u32[]{:S(2)}) collective-permute-start(bf16[8,96,256]{2,1,0:T(8,128)(2,1)S(1)} %outward.7), channel_id=1, source_target_pairs={{0,8},{1,9},{2,10},{3,11},{4,12},{5,13},{6,14},{7,15},{8,0},{9,1},... | collective-permute-start | bytes 1179656 | tf_op jit(solution)/shard_map/ppermute | solution.py:384
  76.9 21.0 %copy-start.4 = (bf16[4,512,512]{2,1,0:T(8,128)(2,1)S(1)}, bf16[4,512,512]{2,1,0:T(8,128)(2,1)}, u32[]{:S(2)}) copy-start(bf16[4,512,512]{2,1,0:T(8,128)(2,1)} %copy-done.2) | copy-start | bytes 6291460
  79.4 7.0 %collective-permute-start.19 = (bf16[8,48,256]{2,1,0:T(8,128)(2,1)S(1)}, bf16[8,48,256]{2,1,0:T(8,128)(2,1)S(1)}, u32[]{:S(2)}, u32[]{:S(2)}) collective-permute-start(bf16[8,48,256]{2,1,0:T(8,128)(2,1)S(1)} %get-tuple-element.53), channel_id=1, source_target_pairs={{0,16},{1,17},{2,18},{3,19},{4,20},{5,21},{6,22},{7,23},{8,24},{9,... | collective-permute-start | bytes 589832 | tf_op jit(solution)/shard_map/ppermute | solution.py:384
  87.0 6.4 %collective-permute-start.20 = (bf16[4,48,256]{2,1,0:T(8,128)(2,1)S(1)}, bf16[4,48,256]{2,1,0:T(8,128)(2,1)S(1)}, u32[]{:S(2)}, u32[]{:S(2)}) collective-permute-start(bf16[4,48,256]{2,1,0:T(8,128)(2,1)S(1)} %get-tuple-element.55), channel_id=1, source_target_pairs={{0,17},{1,16},{2,19},{3,18},{4,21},{5,20},{6,23},{7,22},{8,25},{9,... | collective-permute-start | bytes 294920 | tf_op jit(solution)/shard_map/ppermute | solution.py:384
  93.5 21.1 %collective-permute-start.32 = (bf16[4,192,512]{2,1,0:T(8,128)(2,1)S(1)}, bf16[4,192,512]{2,1,0:T(8,128)(2,1)S(1)}, u32[]{:S(2)}, u32[]{:S(2)}) collective-permute-start(bf16[4,192,512]{2,1,0:T(8,128)(2,1)S(1)} %back.4.refs_1_.inner_ref.own_ref), channel_id=1, source_target_pairs={{0,1},{1,0},{2,3},{3,2},{4,5},{5,4},{6,7},{7,6},{8,9},{9,8},{10,11... | collective-permute-start | bytes 2359304 | tf_op jit(solution)/shard_map/ppermute | solution.py:455
  94.4 8.8 %collective-permute-start.22 = (bf16[4,48,256]{2,1,0:T(8,128)(2,1)S(1)}, bf16[4,48,256]{2,1,0:T(8,128)(2,1)S(1)}, u32[]{:S(2)}, u32[]{:S(2)}) collective-permute-start(bf16[4,48,256]{2,1,0:T(8,128)(2,1)S(1)} %add.116.refs_0_), channel_id=1, source_target_pairs={{0,4},{1,5},{2,6},{3,7},{4,0},{5,1},{6,2},{7,3},{8,12},{9,13},{10,... | collective-permute-start | bytes 294920 | tf_op jit(solution)/shard_map/ppermute | solution.py:384
  95.1 8.1 %collective-permute-start.23 = (bf16[4,48,256]{2,1,0:T(8,128)(2,1)S(1)}, bf16[4,48,256]{2,1,0:T(8,128)(2,1)S(1)}, u32[]{:S(2)}, u32[]{:S(2)}) collective-permute-start(bf16[4,48,256]{2,1,0:T(8,128)(2,1)S(1)} %add.116.refs_0_), channel_id=1, source_target_pairs={{0,6},{1,7},{2,4},{3,5},{4,2},{5,3},{6,0},{7,1},{8,14},{9,15},{10,... | collective-permute-start | bytes 294920 | tf_op jit(solution)/shard_map/ppermute | solution.py:384
  96.8 6.5 %collective-permute-start.24 = (bf16[4,48,256]{2,1,0:T(8,128)(2,1)S(1)}, bf16[4,48,256]{2,1,0:T(8,128)(2,1)S(1)}, u32[]{:S(2)}, u32[]{:S(2)}) collective-permute-start(bf16[4,48,256]{2,1,0:T(8,128)(2,1)S(1)} %add.116.refs_0_), channel_id=1, source_target_pairs={{0,2},{1,3},{2,0},{3,1},{4,6},{5,7},{6,4},{7,5},{8,10},{9,11},{10,... | collective-permute-start | bytes 294920 | tf_op jit(solution)/shard_map/ppermute | solution.py:384
  103.7 5.9 %collective-permute-start.25 = (bf16[4,48,256]{2,1,0:T(8,128)(2,1)S(1)}, bf16[4,48,256]{2,1,0:T(8,128)(2,1)S(1)}, u32[]{:S(2)}, u32[]{:S(2)}) collective-permute-start(bf16[4,48,256]{2,1,0:T(8,128)(2,1)S(1)} %reflect.3.refs_0_), channel_id=1, source_target_pairs={{0,17},{1,16},{2,19},{3,18},{4,21},{5,20},{6,23},{7,22},{8,25},{9,... | collective-permute-start | bytes 294920 | tf_op jit(solution)/shard_map/ppermute | solution.py:384
  105.2 7.3 %collective-permute-start.26 = (bf16[4,48,256]{2,1,0:T(8,128)(2,1)S(1)}, bf16[4,48,256]{2,1,0:T(8,128)(2,1)S(1)}, u32[]{:S(2)}, u32[]{:S(2)}) collective-permute-start(bf16[4,48,256]{2,1,0:T(8,128)(2,1)S(1)} %reflect.3.refs_0_), channel_id=1, source_target_pairs={{0,16},{1,17},{2,18},{3,19},{4,20},{5,21},{6,22},{7,23},{8,24},{9,... | collective-permute-start | bytes 294920 | tf_op jit(solution)/shard_map/ppermute | solution.py:384
  109.5 5.0 %collective-permute-start.27 = (bf16[4,48,256]{2,1,0:T(8,128)(2,1)S(1)}, bf16[4,48,256]{2,1,0:T(8,128)(2,1)S(1)}, u32[]{:S(2)}, u32[]{:S(2)}) collective-permute-start(bf16[4,48,256]{2,1,0:T(8,128)(2,1)S(1)} %collective-permute-done.25.refs_1_), channel_id=1, source_target_pairs={{0,16},{1,17},{2,18},{3,19},{4,20},{5,21},{6,22},{7,23},{8,24},{9,... | collective-permute-start | bytes 294920 | tf_op jit(solution)/shard_map/ppermute | solution.py:384
  112.0 6.6 %collective-permute-start.28 = (bf16[4,48,256]{2,1,0:T(8,128)(2,1)S(1)}, bf16[4,48,256]{2,1,0:T(8,128)(2,1)S(1)}, u32[]{:S(2)}, u32[]{:S(2)}) collective-permute-start(bf16[4,48,256]{2,1,0:T(8,128)(2,1)S(1)} %reflect.3.refs_0_), channel_id=1, source_target_pairs={{0,8},{1,9},{2,10},{3,11},{4,12},{5,13},{6,14},{7,15},{8,0},{9,1},... | collective-permute-start | bytes 294920 | tf_op jit(solution)/shard_map/ppermute | solution.py:384
  112.0 6.6 %collective-permute-start.29 = (bf16[4,48,256]{2,1,0:T(8,128)(2,1)S(1)}, bf16[4,48,256]{2,1,0:T(8,128)(2,1)S(1)}, u32[]{:S(2)}, u32[]{:S(2)}) collective-permute-start(bf16[4,48,256]{2,1,0:T(8,128)(2,1)S(1)} %collective-permute-done.25.refs_1_), channel_id=1, source_target_pairs={{0,8},{1,9},{2,10},{3,11},{4,12},{5,13},{6,14},{7,15},{8,0},{9,1},... | collective-permute-start | bytes 294920 | tf_op jit(solution)/shard_map/ppermute | solution.py:384
  112.5 6.1 %collective-permute-start.30 = (bf16[4,48,256]{2,1,0:T(8,128)(2,1)S(1)}, bf16[4,48,256]{2,1,0:T(8,128)(2,1)S(1)}, u32[]{:S(2)}, u32[]{:S(2)}) collective-permute-start(bf16[4,48,256]{2,1,0:T(8,128)(2,1)S(1)} %collective-permute-done.26.refs_2_), channel_id=1, source_target_pairs={{0,8},{1,9},{2,10},{3,11},{4,12},{5,13},{6,14},{7,15},{8,0},{9,1},... | collective-permute-start | bytes 294920 | tf_op jit(solution)/shard_map/ppermute | solution.py:384
  114.6 4.0 %collective-permute-start.31 = (bf16[4,48,256]{2,1,0:T(8,128)(2,1)S(1)}, bf16[4,48,256]{2,1,0:T(8,128)(2,1)S(1)}, u32[]{:S(2)}, u32[]{:S(2)}) collective-permute-start(bf16[4,48,256]{2,1,0:T(8,128)(2,1)S(1)} %collective-permute-done.27.refs_3_), channel_id=1, source_target_pairs={{0,8},{1,9},{2,10},{3,11},{4,12},{5,13},{6,14},{7,15},{8,0},{9,1},... | collective-permute-start | bytes 294920 | tf_op jit(solution)/shard_map/ppermute | solution.py:384

commit v6 on v5

--- a/solution.py
+++ b/solution.py
@@ -76,7 +76,7 @@
         out_shape=[jax.ShapeDtypeStruct((count, m, size), BF16)]
         + [jax.ShapeDtypeStruct(array.shape, array.dtype) for array in staged],
         compiler_params=params(12),
-        cost_estimate=cost(count * m * size * size, 2 * count * size * (2 * m + size)),
+        cost_estimate=cost(count * m * size * size, 2 * count * size * (2 * m + size), real=True),
         name="solve",
     )(first, source, t_matrices, *staged)
 
@@ -273,7 +273,7 @@
         ),
         out_shape=jax.ShapeDtypeStruct((group, m, size), F32),
         compiler_params=params(32),
-        cost_estimate=cost(kinds * group * m * size * size, 2 * size * size * kinds),
+        cost_estimate=cost(kinds * group * m * size * size, 2 * size * size * kinds, real=True),
         name="near",
     )(first, slots, counts, types, halo, own, inner, incident, translations)
 

time: 125 us -> 126 us (level)
  transfers between devices with their start and end apart: 33 -> 33, of which waited for: 10 -> 9; matrix products, arithmetic and copies ran while one was open for 1% -> 1% of each run, Pallas kernels for 28% -> 27%
where the time goes in v6:
time: 126 us; the launch traced here: 125 us
  starting transfers between devices  49.6 us (39%)
  Pallas kernels  46.7 us (37%)
  waiting for transfers between devices  22 us (17%)
  local copies, waits for them, and re-layouts  5.5 us (4%)
    ppermute x29, starting transfers between devices, flip(): return lax.ppermute(array, AXES, [(i, i ^ mask) for i in range(devices)])  45.5 us
    ppermute x29, waiting for transfers between devices, flip(): return lax.ppermute(array, AXES, [(i, i ^ mask) for i in range(devices)])  22 us
    pallas_call x4, Pallas kernels, near(): pl.pallas_call(near_kernel, grid_spec=pltpu.PrefetchScalarGridSpec(num_sc...  16 us
    pallas_call x3, Pallas kernels, back(): pl.pallas_call(body, grid_spec=pltpu.PrefetchScalarGridSpec(num_scalar_pr...  13.1 us
    pallas_call x4, Pallas kernels, outward(): pl.pallas_call(outward_kernel, in_specs=[SCALARS] + [VECTORS] * (len(piec...  8.15 us
    pallas_call x2, Pallas kernels, solve(): pl.pallas_call(body, in_specs=[SCALARS] + [ANYWHERE] * (2 + len(staged)),...  5.78 us
    unnamed x26, local copies, waits for them, and re-layouts  5.23 us
  transfers between devices with their start and end apart: 33, of which 9 were waited for; matrix products, arithmetic and copies ran while one was open for 1% of the time, Pallas kernels for 27%

profile of v6, /device:TPU:0, one launch (start us, length us, event | category | flops | bytes accessed | tf_op | source)
XLA Modules:
  0.0 125.2 jit_solution(536672054532655729)
XLA Ops:
  0.0 2.5 %solve.2.refs_0_.own_ref.inner_ref = bf16[4,192,512]{2,1,0:T(8,128)(2,1)S(1)} custom-call(s32[1]{0:T(128)} %bitcast.refs_0_.first_ref, bf16[8,192,512]{2,1,0:T(8,128)(2,1)} %bitcast.21, bf16[8,512,512]{2,1,0:T(8,128)(2,1)} %refs_10_.5), custom_call_target="tpu_custom_call" | custom-call | flops 402653184 | bytes 3670016 | tf_op jit(solution)/shard_map/solve/pallas_call | solution.py:66
  2.6 1.6 %collective-permute-start.3 = (bf16[4,192,512]{2,1,0:T(8,128)(2,1)S(1)}, bf16[4,192,512]{2,1,0:T(8,128)(2,1)}, u32[]{:S(2)}, u32[]{:S(2)}) collective-permute-start(bf16[4,192,512]{2,1,0:T(8,128)(2,1)S(1)} %solve.2.refs_0_.own_ref.inner_ref), channel_id=1, source_target_pairs={{1,2},{2,1},{3,4},{4,3},{5,6},{6,5},{7,8},{8,7},{9,10},{10,9},{11,... | collective-permute-start | bytes 2359304 | tf_op jit(solution)/shard_map/ppermute | solution.py:435
  4.2 3.2 %solve.3 = (bf16[4,192,512]{2,1,0:T(8,128)(2,1)S(1)}, bf16[2048,512]{1,0:T(8,128)(2,1)S(1)}, bf16[4,512,512]{2,1,0:T(8,128)(2,1)S(1)}) custom-call(s32[1]{0:T(128)} %bitcast.5.refs_0_.first_ref, bf16[8,192,512]{2,1,0:T(8,128)(2,1)} %bitcast.22, bf16[8,512,512]{2,1,0:T(8,128)(2,1)} %refs_10_.5, bf16[2048,512]{1,0:T(8,128)(2,1)} %refs_3_.1, ...), custom_call_target="tpu_custom_call" | custom-call | flops 402653184 | bytes 3670016 | tf_op jit(solution)/shard_map/solve/pallas_call | solution.py:66
  7.4 1.3 %copy-done.2 = bf16[4,512,512]{2,1,0:T(8,128)(2,1)} copy-done((bf16[4,512,512]{2,1,0:T(8,128)(2,1)}, bf16[4,512,512]{2,1,0:T(8,128)(2,1)S(1)}, u32[]{:S(2)}) %copy-start.2) | copy-done | bytes 2097176
  8.8 2.6 %outward.5 = bf16[8,96,256]{2,1,0:T(8,128)(2,1)} custom-call(s32[1]{0:T(128)} %bitcast.7.part_ref, bf16[4,192,512]{2,1,0:T(8,128)(2,1)S(1)} %solve.2.refs_0_.own_ref.inner_ref, bf16[4,192,512]{2,1,0:T(8,128)(2,1)S(1)} %get-tuple-element.47.refs_1_.inner_ref.own_ref, bf16[2048,512]{1,0:T(8,128)(2,1)S(1)} %get-tuple-element.35.refs_2_.refs_9_, ...), custom_call_target="tpu_custom_call" | custom-call | flops 1 | bytes 1 | tf_op jit(solution)/shard_map/outward/pallas_call | solution.py:110
  11.4 6.5 %collective-permute-start = (bf16[8,96,256]{2,1,0:T(8,128)(2,1)}, bf16[8,96,256]{2,1,0:T(8,128)(2,1)}, u32[]{:S(2)}, u32[]{:S(2)}) collective-permute-start(bf16[8,96,256]{2,1,0:T(8,128)(2,1)} %outward.5), channel_id=1, source_target_pairs={{0,8},{1,9},{2,10},{3,11},{4,12},{5,13},{6,14},{7,15},{8,0},{9,1},... | collective-permute-start | bytes 1179656 | tf_op jit(solution)/shard_map/ppermute | solution.py:384
  17.9 1.1 copy-done.6
  19.0 1.8 %outward.4 = bf16[8,96,256]{2,1,0:T(8,128)(2,1)S(1)} custom-call(s32[1]{0:T(128)} %bitcast.3.part_ref, bf16[4,192,512]{2,1,0:T(8,128)(2,1)S(1)} %solve.2.refs_0_.own_ref.inner_ref, bf16[4,192,512]{2,1,0:T(8,128)(2,1)S(1)} %copy-done.6, bf16[2048,512]{1,0:T(8,128)(2,1)S(1)} %get-tuple-element.35.refs_2_.refs_9_, f32[8,2048]{1,0:T(8,128)S(1)} %maximum_convert_fusion.refs_3_), custom_call_target="tpu_custom_call" | custom-call | flops 1 | bytes 1 | tf_op jit(solution)/shard_map/outward/pallas_call | solution.py:110
  20.9 0.9 convert_element_type.7
  21.8 0.1 pad_add_fusion.place_ref
  22.0 1.2 split.2
  23.2 1.6 %collective-permute-start.1 = (bf16[8,48,256]{2,1,0:T(8,128)(2,1)S(1)}, bf16[8,48,256]{2,1,0:T(8,128)(2,1)S(1)}, u32[]{:S(2)}, u32[]{:S(2)}) collective-permute-start(bf16[8,48,256]{2,1,0:T(8,128)(2,1)S(1)} %get-tuple-element.37), channel_id=1, source_target_pairs={{0,16},{1,17},{2,18},{3,19},{4,20},{5,21},{6,22},{7,23},{8,24},{9,... | collective-permute-start | bytes 589832 | tf_op jit(solution)/shard_map/ppermute | solution.py:384
  24.7 0.1 fusion.8
  24.8 0.1 collective-permute-start.7
  24.9 0.9 collective-permute-start.8
  25.8 3.5 %collective-permute-start.9 = (bf16[2,128,128]{2,1,0:T(8,128)(2,1)S(1)}, bf16[2,128,128]{2,1,0:T(8,128)(2,1)S(1)}, u32[]{:S(2)}, u32[]{:S(2)}) collective-permute-start(bf16[2,128,128]{2,1,0:T(8,128)(2,1)S(1)} %convert_element_type.7), channel_id=1, source_target_pairs={{0,6},{1,7},{2,4},{3,5},{4,2},{5,3},{6,0},{7,1},{8,14},{9,15},{10,... | collective-permute-start | bytes 196616 | tf_op jit(solution)/shard_map/ppermute | solution.py:384
  29.3 0.8 collective-permute-done.1.got_ref
  30.0 0.6 deal.2
  30.6 2.9 %collective-permute-start.2 = (bf16[4,48,256]{2,1,0:T(8,128)(2,1)S(1)}, bf16[4,48,256]{2,1,0:T(8,128)(2,1)S(1)}, u32[]{:S(2)}, u32[]{:S(2)}) collective-permute-start(bf16[4,48,256]{2,1,0:T(8,128)(2,1)S(1)} %get-tuple-element.39), channel_id=1, source_target_pairs={{0,17},{1,16},{2,19},{3,18},{4,21},{5,20},{6,23},{7,22},{8,25},{9,... | collective-permute-start | bytes 294920 | tf_op jit(solution)/shard_map/ppermute | solution.py:384
  33.6 2.8 %collective-permute-done.2.refs_1_ = bf16[4,48,256]{2,1,0:T(8,128)(2,1)S(1)} collective-permute-done((bf16[4,48,256]{2,1,0:T(8,128)(2,1)S(1)}, bf16[4,48,256]{2,1,0:T(8,128)(2,1)S(1)}, u32[]{:S(2)}, u32[]{:S(2)}) %collective-permute-start.2) | collective-permute-done | bytes 98336 | tf_op jit(solution)/shard_map/ppermute | solution.py:384
  36.4 0.8 collective-permute-start.13
  37.3 0.6 collective-permute-start.4
  37.9 3.1 %collective-permute-start.5 = (bf16[4,48,256]{2,1,0:T(8,128)(2,1)S(1)}, bf16[4,48,256]{2,1,0:T(8,128)(2,1)S(1)}, u32[]{:S(2)}, u32[]{:S(2)}) collective-permute-start(bf16[4,48,256]{2,1,0:T(8,128)(2,1)S(1)} %add.115.refs_0_), channel_id=1, source_target_pairs={{0,6},{1,7},{2,4},{3,5},{4,2},{5,3},{6,0},{7,1},{8,14},{9,15},{10,... | collective-permute-start | bytes 294920 | tf_op jit(solution)/shard_map/ppermute | solution.py:384
  41.0 0.5 collective-permute-start.6
  41.5 1.6 %copy-done.3 = bf16[4,512,512]{2,1,0:T(8,128)(2,1)S(1)} copy-done((bf16[4,512,512]{2,1,0:T(8,128)(2,1)S(1)}, bf16[4,512,512]{2,1,0:T(8,128)(2,1)}, u32[]{:S(2)}) %copy-start.3) | copy-done | bytes 2097176
  43.1 1.1 copy-done.7
  44.2 4.7 %near.4.refs_11_ = f32[4,192,512]{2,1,0:T(8,128)S(1)} custom-call(s32[1]{0:T(128)} %bitcast.refs_0_.first_ref, s32[4,6]{1,0:T(4,128)S(1)} %constant_dynamic-slice_fusion.3.slot_ref, s32[4]{0:T(128)S(1)} %get-tuple-element.70.count_ref, s32[4,6]{1,0:T(4,128)S(1)} %get-tuple-element.66.type_ref, bf16[4,192,512]{2,1,0:T(8,128)(2,1)} %collective-permute-done.3.halo_ref, ...), custom_call_target="tpu_custom_call" | custom-call | flops 1610612736 | bytes 2097152 | tf_op jit(solution)/shard_map/near/pallas_call | solution.py:256
  49.0 0.3 reflect.2.refs_0_
  49.3 1.7 %collective-permute-start.10 = (bf16[4,48,256]{2,1,0:T(8,128)(2,1)S(1)}, bf16[4,48,256]{2,1,0:T(8,128)(2,1)S(1)}, u32[]{:S(2)}, u32[]{:S(2)}) collective-permute-start(bf16[4,48,256]{2,1,0:T(8,128)(2,1)S(1)} %reflect.2.refs_0_), channel_id=1, source_target_pairs={{0,17},{1,16},{2,19},{3,18},{4,21},{5,20},{6,23},{7,22},{8,25},{9,... | collective-permute-start | bytes 294920 | tf_op jit(solution)/shard_map/ppermute | solution.py:384
  51.0 1.9 %collective-permute-start.11 = (bf16[4,48,256]{2,1,0:T(8,128)(2,1)S(1)}, bf16[4,48,256]{2,1,0:T(8,128)(2,1)S(1)}, u32[]{:S(2)}, u32[]{:S(2)}) collective-permute-start(bf16[4,48,256]{2,1,0:T(8,128)(2,1)S(1)} %reflect.2.refs_0_), channel_id=1, source_target_pairs={{0,16},{1,17},{2,18},{3,19},{4,20},{5,21},{6,22},{7,23},{8,24},{9,... | collective-permute-start | bytes 294920 | tf_op jit(solution)/shard_map/ppermute | solution.py:384
  52.9 2.1 %collective-permute-done.10.refs_1_ = bf16[4,48,256]{2,1,0:T(8,128)(2,1)S(1)} collective-permute-done((bf16[4,48,256]{2,1,0:T(8,128)(2,1)S(1)}, bf16[4,48,256]{2,1,0:T(8,128)(2,1)S(1)}, u32[]{:S(2)}, u32[]{:S(2)}) %collective-permute-start.10) | collective-permute-done | bytes 98336 | tf_op jit(solution)/shard_map/ppermute | solution.py:384
  55.0 2.2 %collective-permute-start.12 = (bf16[4,48,256]{2,1,0:T(8,128)(2,1)S(1)}, bf16[4,48,256]{2,1,0:T(8,128)(2,1)S(1)}, u32[]{:S(2)}, u32[]{:S(2)}) collective-permute-start(bf16[4,48,256]{2,1,0:T(8,128)(2,1)S(1)} %collective-permute-done.10.refs_1_), channel_id=1, source_target_pairs={{0,16},{1,17},{2,18},{3,19},{4,20},{5,21},{6,22},{7,23},{8,24},{9,... | collective-permute-start | bytes 294920 | tf_op jit(solution)/shard_map/ppermute | solution.py:384
  57.2 0.5 collective-permute-start.16
  57.7 3.8 %near.5.refs_11_ = f32[4,192,512]{2,1,0:T(8,128)S(1)} custom-call(s32[1]{0:T(128)} %bitcast.5.refs_0_.first_ref, s32[4,6]{1,0:T(4,128)S(1)} %constant_dynamic-slice_fusion.1.slot_ref, s32[4]{0:T(128)S(1)} %get-tuple-element.69.count_ref, s32[4,6]{1,0:T(4,128)S(1)} %get-tuple-element.65.type_ref, bf16[4,192,512]{2,1,0:T(8,128)(2,1)S(1)} %collective-permute-done.13.halo_ref, ...), custom_call_target="tpu_custom_call" | custom-call | flops 1610612736 | bytes 2097152 | tf_op jit(solution)/shard_map/near/pallas_call | solution.py:256
  61.6 0.2 collective-permute-start.17
  61.8 0.1 copy.10.refs_8_
  61.9 1.1 collective-permute-done.17.refs_7_
  62.9 3.3 %back.3.refs_0_.own_ref.inner_ref = bf16[4,192,512]{2,1,0:T(8,128)(2,1)S(1)} custom-call(s32[1]{0:T(128)} %bitcast.refs_0_.first_ref, s32[3]{0:T(128)S(1)} %pad_add_fusion.place_ref, bf16[4,48,256]{2,1,0:T(8,128)(2,1)S(1)} %reflect.2.refs_0_, bf16[4,48,256]{2,1,0:T(8,128)(2,1)S(1)} %collective-permute-done.10.refs_1_, ...), custom_call_target="tpu_custom_call" | custom-call | flops 1 | bytes 1 | tf_op jit(solution)/shard_map/back/pallas_call | solution.py:332
  66.2 0.7 collective-permute-start.21
  67.0 3.3 %back.4.refs_1_.inner_ref.own_ref = bf16[4,192,512]{2,1,0:T(8,128)(2,1)S(1)} custom-call(s32[1]{0:T(128)} %bitcast.5.refs_0_.first_ref, s32[3]{0:T(128)S(1)} %pad_add_fusion.place_ref, bf16[4,48,256]{2,1,0:T(8,128)(2,1)S(1)} %reflect.2.refs_0_, bf16[4,48,256]{2,1,0:T(8,128)(2,1)S(1)} %collective-permute-done.10.refs_1_, ...), custom_call_target="tpu_custom_call" | custom-call | flops 1 | bytes 1 | tf_op jit(solution)/shard_map/back/pallas_call | solution.py:332
  70.3 1.9 %outward.7 = bf16[8,96,256]{2,1,0:T(8,128)(2,1)S(1)} custom-call(s32[1]{0:T(128)} %bitcast.7.part_ref, bf16[4,192,512]{2,1,0:T(8,128)(2,1)S(1)} %back.3.refs_0_.own_ref.inner_ref, bf16[4,192,512]{2,1,0:T(8,128)(2,1)S(1)} %back.4.refs_1_.inner_ref.own_ref, bf16[2048,512]{1,0:T(8,128)(2,1)S(1)} %get-tuple-element.35.refs_2_.refs_9_, ...), custom_call_target="tpu_custom_call" | custom-call | flops 1 | bytes 1 | tf_op jit(solution)/shard_map/outward/pallas_call | solution.py:110
  72.1 4.5 %collective-permute-start.18 = (bf16[8,96,256]{2,1,0:T(8,128)(2,1)S(1)}, bf16[8,96,256]{2,1,0:T(8,128)(2,1)S(1)}, u32[]{:S(2)}, u32[]{:S(2)}) collective-permute-start(bf16[8,96,256]{2,1,0:T(8,128)(2,1)S(1)} %outward.7), channel_id=1, source_target_pairs={{0,8},{1,9},{2,10},{3,11},{4,12},{5,13},{6,14},{7,15},{8,0},{9,1},... | collective-permute-start | bytes 1179656 | tf_op jit(solution)/shard_map/ppermute | solution.py:384
  76.6 1.9 %outward.6 = bf16[8,96,256]{2,1,0:T(8,128)(2,1)S(1)} custom-call(s32[1]{0:T(128)} %bitcast.3.part_ref, bf16[4,192,512]{2,1,0:T(8,128)(2,1)S(1)} %back.3.refs_0_.own_ref.inner_ref, bf16[4,192,512]{2,1,0:T(8,128)(2,1)S(1)} %back.4.refs_1_.inner_ref.own_ref, bf16[2048,512]{1,0:T(8,128)(2,1)S(1)} %get-tuple-element.35.refs_2_.refs_9_, ...), custom_call_target="tpu_custom_call" | custom-call | flops 1 | bytes 1 | tf_op jit(solution)/shard_map/outward/pallas_call | solution.py:110
  78.5 0.6 split.3
  79.1 1.2 collective-permute-start.19
  80.4 5.7 %collective-permute-done.19.got_ref = bf16[8,48,256]{2,1,0:T(8,128)(2,1)S(1)} collective-permute-done((bf16[8,48,256]{2,1,0:T(8,128)(2,1)S(1)}, bf16[8,48,256]{2,1,0:T(8,128)(2,1)S(1)}, u32[]{:S(2)}, u32[]{:S(2)}) %collective-permute-start.19) | collective-permute-done | bytes 196640 | tf_op jit(solution)/shard_map/ppermute | solution.py:384
  86.0 0.6 deal.3
  86.6 4.2 %collective-permute-start.20 = (bf16[4,48,256]{2,1,0:T(8,128)(2,1)S(1)}, bf16[4,48,256]{2,1,0:T(8,128)(2,1)S(1)}, u32[]{:S(2)}, u32[]{:S(2)}) collective-permute-start(bf16[4,48,256]{2,1,0:T(8,128)(2,1)S(1)} %get-tuple-element.55), channel_id=1, source_target_pairs={{0,17},{1,16},{2,19},{3,18},{4,21},{5,20},{6,23},{7,22},{8,25},{9,... | collective-permute-start | bytes 294920 | tf_op jit(solution)/shard_map/ppermute | solution.py:384
  90.8 2.6 %collective-permute-done.20.refs_1_ = bf16[4,48,256]{2,1,0:T(8,128)(2,1)S(1)} collective-permute-done((bf16[4,48,256]{2,1,0:T(8,128)(2,1)S(1)}, bf16[4,48,256]{2,1,0:T(8,128)(2,1)S(1)}, u32[]{:S(2)}, u32[]{:S(2)}) %collective-permute-start.20) | collective-permute-done | bytes 98336 | tf_op jit(solution)/shard_map/ppermute | solution.py:384
  93.4 1.0 collective-permute-start.32
  94.4 0.6 collective-permute-start.22
  95.0 1.5 %collective-permute-start.23 = (bf16[4,48,256]{2,1,0:T(8,128)(2,1)S(1)}, bf16[4,48,256]{2,1,0:T(8,128)(2,1)S(1)}, u32[]{:S(2)}, u32[]{:S(2)}) collective-permute-start(bf16[4,48,256]{2,1,0:T(8,128)(2,1)S(1)} %add.116.refs_0_), channel_id=1, source_target_pairs={{0,6},{1,7},{2,4},{3,5},{4,2},{5,3},{6,0},{7,1},{8,14},{9,15},{10,... | collective-permute-start | bytes 294920 | tf_op jit(solution)/shard_map/ppermute | solution.py:384
  96.5 1.3 %collective-permute-start.24 = (bf16[4,48,256]{2,1,0:T(8,128)(2,1)S(1)}, bf16[4,48,256]{2,1,0:T(8,128)(2,1)S(1)}, u32[]{:S(2)}, u32[]{:S(2)}) collective-permute-start(bf16[4,48,256]{2,1,0:T(8,128)(2,1)S(1)} %add.116.refs_0_), channel_id=1, source_target_pairs={{0,2},{1,3},{2,0},{3,1},{4,6},{5,7},{6,4},{7,5},{8,10},{9,11},{10,... | collective-permute-start | bytes 294920 | tf_op jit(solution)/shard_map/ppermute | solution.py:384
  97.9 3.6 %near.6.refs_11_ = f32[4,192,512]{2,1,0:T(8,128)S(1)} custom-call(s32[1]{0:T(128)} %bitcast.refs_0_.first_ref, s32[4,6]{1,0:T(4,128)S(1)} %constant_dynamic-slice_fusion.3.slot_ref, s32[4]{0:T(128)S(1)} %get-tuple-element.70.count_ref, s32[4,6]{1,0:T(4,128)S(1)} %get-tuple-element.66.type_ref, bf16[4,192,512]{2,1,0:T(8,128)(2,1)S(1)} %collective-permute-done.21.halo_ref, ...), custom_call_target="tpu_custom_call" | custom-call | flops 1610612736 | bytes 2097152 | tf_op jit(solution)/shard_map/near/pallas_call | solution.py:256
  101.5 1.6 %collective-permute-done.22.refs_1_ = bf16[4,48,256]{2,1,0:T(8,128)(2,1)S(1)} collective-permute-done((bf16[4,48,256]{2,1,0:T(8,128)(2,1)S(1)}, bf16[4,48,256]{2,1,0:T(8,128)(2,1)S(1)}, u32[]{:S(2)}, u32[]{:S(2)}) %collective-permute-start.22) | collective-permute-done | bytes 98336 | tf_op jit(solution)/shard_map/ppermute | solution.py:384
  103.2 0.3 reflect.3.refs_0_
  103.4 1.7 %collective-permute-start.25 = (bf16[4,48,256]{2,1,0:T(8,128)(2,1)S(1)}, bf16[4,48,256]{2,1,0:T(8,128)(2,1)S(1)}, u32[]{:S(2)}, u32[]{:S(2)}) collective-permute-start(bf16[4,48,256]{2,1,0:T(8,128)(2,1)S(1)} %reflect.3.refs_0_), channel_id=1, source_target_pairs={{0,17},{1,16},{2,19},{3,18},{4,21},{5,20},{6,23},{7,22},{8,25},{9,... | collective-permute-start | bytes 294920 | tf_op jit(solution)/shard_map/ppermute | solution.py:384
  105.1 1.3 %collective-permute-start.26 = (bf16[4,48,256]{2,1,0:T(8,128)(2,1)S(1)}, bf16[4,48,256]{2,1,0:T(8,128)(2,1)S(1)}, u32[]{:S(2)}, u32[]{:S(2)}) collective-permute-start(bf16[4,48,256]{2,1,0:T(8,128)(2,1)S(1)} %reflect.3.refs_0_), channel_id=1, source_target_pairs={{0,16},{1,17},{2,18},{3,19},{4,20},{5,21},{6,22},{7,23},{8,24},{9,... | collective-permute-start | bytes 294920 | tf_op jit(solution)/shard_map/ppermute | solution.py:384
  106.4 3.3 %collective-permute-done.25.refs_1_ = bf16[4,48,256]{2,1,0:T(8,128)(2,1)S(1)} collective-permute-done((bf16[4,48,256]{2,1,0:T(8,128)(2,1)S(1)}, bf16[4,48,256]{2,1,0:T(8,128)(2,1)S(1)}, u32[]{:S(2)}, u32[]{:S(2)}) %collective-permute-start.25) | collective-permute-done | bytes 98336 | tf_op jit(solution)/shard_map/ppermute | solution.py:384
  109.8 2.5 %collective-permute-start.27 = (bf16[4,48,256]{2,1,0:T(8,128)(2,1)S(1)}, bf16[4,48,256]{2,1,0:T(8,128)(2,1)S(1)}, u32[]{:S(2)}, u32[]{:S(2)}) collective-permute-start(bf16[4,48,256]{2,1,0:T(8,128)(2,1)S(1)} %collective-permute-done.25.refs_1_), channel_id=1, source_target_pairs={{0,16},{1,17},{2,18},{3,19},{4,20},{5,21},{6,22},{7,23},{8,24},{9,... | collective-permute-start | bytes 294920 | tf_op jit(solution)/shard_map/ppermute | solution.py:384
  112.3 0.5 collective-permute-start.29
  112.8 2.1 %collective-permute-done.27.refs_3_ = bf16[4,48,256]{2,1,0:T(8,128)(2,1)S(1)} collective-permute-done((bf16[4,48,256]{2,1,0:T(8,128)(2,1)S(1)}, bf16[4,48,256]{2,1,0:T(8,128)(2,1)S(1)}, u32[]{:S(2)}, u32[]{:S(2)}) %collective-permute-start.27) | collective-permute-done | bytes 98336 | tf_op jit(solution)/shard_map/ppermute | solution.py:384
  114.9 3.9 %near.7.refs_12_ = f32[4,192,512]{2,1,0:T(8,128)S(1)} custom-call(s32[1]{0:T(128)} %bitcast.5.refs_0_.first_ref, s32[4,6]{1,0:T(4,128)S(1)} %constant_dynamic-slice_fusion.1.slot_ref, s32[4]{0:T(128)S(1)} %get-tuple-element.69.count_ref, s32[4,6]{1,0:T(4,128)S(1)} %get-tuple-element.65.type_ref, bf16[4,192,512]{2,1,0:T(8,128)(2,1)S(1)} %collective-permute-done.32.halo_ref, ...), custom_call_target="tpu_custom_call" | custom-call | flops 1610612736 | bytes 2097152 | tf_op jit(solution)/shard_map/near/pallas_call | solution.py:256
  118.8 6.5 %back.5 = bf16[8,192,512]{2,1,0:T(8,128)(2,1)} custom-call(s32[1]{0:T(128)} %bitcast.refs_0_.first_ref, s32[3]{0:T(128)S(1)} %pad_add_fusion.place_ref, bf16[4,48,256]{2,1,0:T(8,128)(2,1)S(1)} %reflect.3.refs_0_, bf16[4,48,256]{2,1,0:T(8,128)(2,1)S(1)} %collective-permute-done.25.refs_1_, bf16[4,48,256]{2,1,0:T(8,128)(2,1)S(1)} %collective-permute-done.26.refs_2_, ...), custom_call_target="tpu_custom_call" | custom-call | flops 1 | bytes 1 | tf_op jit(solution)/shard_map/back/pallas_call | solution.py:332
  (64 shorter events, 0.4 us)
Async XLA Ops:
  0.0 4.1 %copy-start.9 = (bf16[8,2048]{1,0:T(8,128)(2,1)S(1)}, bf16[8,2048]{1,0:T(8,128)(2,1)}, u32[]{:S(2)}) copy-start(bf16[8,2048]{1,0:T(8,128)(2,1)} %param.15) | copy-start | bytes 98308
  2.6 33.8 %collective-permute-start.3 = (bf16[4,192,512]{2,1,0:T(8,128)(2,1)S(1)}, bf16[4,192,512]{2,1,0:T(8,128)(2,1)}, u32[]{:S(2)}, u32[]{:S(2)}) collective-permute-start(bf16[4,192,512]{2,1,0:T(8,128)(2,1)S(1)} %solve.2.refs_0_.own_ref.inner_ref), channel_id=1, source_target_pairs={{1,2},{2,1},{3,4},{4,3},{5,6},{6,5},{7,8},{8,7},{9,10},{10,9},{11,... | collective-permute-start | bytes 2359304 | tf_op jit(solution)/shard_map/ppermute | solution.py:435
  7.4 1.3 %copy-start.2 = (bf16[4,512,512]{2,1,0:T(8,128)(2,1)}, bf16[4,512,512]{2,1,0:T(8,128)(2,1)S(1)}, u32[]{:S(2)}) copy-start(bf16[4,512,512]{2,1,0:T(8,128)(2,1)S(1)} %get-tuple-element.42.translations_ref) | copy-start | bytes 6291460
  8.8 2.6 %copy-start.5 = (bf16[4,192,512]{2,1,0:T(8,128)(2,1)}, bf16[4,192,512]{2,1,0:T(8,128)(2,1)S(1)}, u32[]{:S(2)}) copy-start(bf16[4,192,512]{2,1,0:T(8,128)(2,1)S(1)} %get-tuple-element.47.refs_1_.inner_ref.own_ref) | copy-start | bytes 2359300
  11.4 10.6 %collective-permute-start = (bf16[8,96,256]{2,1,0:T(8,128)(2,1)}, bf16[8,96,256]{2,1,0:T(8,128)(2,1)}, u32[]{:S(2)}, u32[]{:S(2)}) collective-permute-start(bf16[8,96,256]{2,1,0:T(8,128)(2,1)} %outward.5), channel_id=1, source_target_pairs={{0,8},{1,9},{2,10},{3,11},{4,12},{5,13},{6,14},{7,15},{8,0},{9,1},... | collective-permute-start | bytes 1179656 | tf_op jit(solution)/shard_map/ppermute | solution.py:384
  17.9 1.1 copy-start.6
  19.0 2.9 %copy-start.10 = (s32[8,6]{1,0:T(8,128)S(1)}, s32[8,6]{1,0:T(8,128)}, u32[]{:S(2)}) copy-start(s32[8,6]{1,0:T(8,128)} %param.12) | copy-start | bytes 580
  19.0 5.7 %copy-start.12 = (s32[8]{0:T(128)S(1)}, s32[8]{0:T(128)}, u32[]{:S(2)}) copy-start(s32[8]{0:T(128)} %param.13) | copy-start | bytes 100
  19.0 5.8 %copy-start.11 = (s32[8,6]{1,0:T(8,128)S(1)}, s32[8,6]{1,0:T(8,128)}, u32[]{:S(2)}) copy-start(s32[8,6]{1,0:T(8,128)} %param.14) | copy-start | bytes 580
  21.8 19.7 %copy-start.1 = (bf16[8,512,192]{1,2,0:T(8,128)(2,1)S(1)}, bf16[8,512,192]{1,2,0:T(8,128)(2,1)}, u32[]{:S(2)}) copy-start(bf16[8,512,192]{1,2,0:T(8,128)(2,1)} %param.9) | copy-start | bytes 4718596
  23.2 6.9 %collective-permute-start.1 = (bf16[8,48,256]{2,1,0:T(8,128)(2,1)S(1)}, bf16[8,48,256]{2,1,0:T(8,128)(2,1)S(1)}, u32[]{:S(2)}, u32[]{:S(2)}) collective-permute-start(bf16[8,48,256]{2,1,0:T(8,128)(2,1)S(1)} %get-tuple-element.37), channel_id=1, source_target_pairs={{0,16},{1,17},{2,18},{3,19},{4,20},{5,21},{6,22},{7,23},{8,24},{9,... | collective-permute-start | bytes 589832 | tf_op jit(solution)/shard_map/ppermute | solution.py:384
  24.8 12.4 %collective-permute-start.7 = (bf16[2,128,128]{2,1,0:T(8,128)(2,1)S(1)}, bf16[2,128,128]{2,1,0:T(8,128)(2,1)S(1)}, u32[]{:S(2)}, u32[]{:S(2)}) collective-permute-start(bf16[2,128,128]{2,1,0:T(8,128)(2,1)S(1)} %convert_element_type.7), channel_id=1, source_target_pairs={{0,2},{1,3},{2,0},{3,1},{4,6},{5,7},{6,4},{7,5},{8,10},{9,11},{10,... | collective-permute-start | bytes 196616 | tf_op jit(solution)/shard_map/ppermute | solution.py:384
  24.9 12.4 %collective-permute-start.8 = (bf16[2,128,128]{2,1,0:T(8,128)(2,1)S(1)}, bf16[2,128,128]{2,1,0:T(8,128)(2,1)S(1)}, u32[]{:S(2)}, u32[]{:S(2)}) collective-permute-start(bf16[2,128,128]{2,1,0:T(8,128)(2,1)S(1)} %convert_element_type.7), channel_id=1, source_target_pairs={{0,4},{1,5},{2,6},{3,7},{4,0},{5,1},{6,2},{7,3},{8,12},{9,13},{10,... | collective-permute-start | bytes 196616 | tf_op jit(solution)/shard_map/ppermute | solution.py:384
  25.8 11.5 %collective-permute-start.9 = (bf16[2,128,128]{2,1,0:T(8,128)(2,1)S(1)}, bf16[2,128,128]{2,1,0:T(8,128)(2,1)S(1)}, u32[]{:S(2)}, u32[]{:S(2)}) collective-permute-start(bf16[2,128,128]{2,1,0:T(8,128)(2,1)S(1)} %convert_element_type.7), channel_id=1, source_target_pairs={{0,6},{1,7},{2,4},{3,5},{4,2},{5,3},{6,0},{7,1},{8,14},{9,15},{10,... | collective-permute-start | bytes 196616 | tf_op jit(solution)/shard_map/ppermute | solution.py:384
  30.6 5.7 %collective-permute-start.2 = (bf16[4,48,256]{2,1,0:T(8,128)(2,1)S(1)}, bf16[4,48,256]{2,1,0:T(8,128)(2,1)S(1)}, u32[]{:S(2)}, u32[]{:S(2)}) collective-permute-start(bf16[4,48,256]{2,1,0:T(8,128)(2,1)S(1)} %get-tuple-element.39), channel_id=1, source_target_pairs={{0,17},{1,16},{2,19},{3,18},{4,21},{5,20},{6,23},{7,22},{8,25},{9,... | collective-permute-start | bytes 294920 | tf_op jit(solution)/shard_map/ppermute | solution.py:384
  36.4 21.3 %collective-permute-start.13 = (bf16[4,192,512]{2,1,0:T(8,128)(2,1)}, bf16[4,192,512]{2,1,0:T(8,128)(2,1)S(1)}, u32[]{:S(2)}, u32[]{:S(2)}) collective-permute-start(bf16[4,192,512]{2,1,0:T(8,128)(2,1)} %copy-done.5), channel_id=1, source_target_pairs={{0,1},{1,0},{2,3},{3,2},{4,5},{5,4},{6,7},{7,6},{8,9},{9,8},{10,11... | collective-permute-start | bytes 2359304 | tf_op jit(solution)/shard_map/ppermute | solution.py:455
  37.3 11.6 %collective-permute-start.4 = (bf16[4,48,256]{2,1,0:T(8,128)(2,1)S(1)}, bf16[4,48,256]{2,1,0:T(8,128)(2,1)S(1)}, u32[]{:S(2)}, u32[]{:S(2)}) collective-permute-start(bf16[4,48,256]{2,1,0:T(8,128)(2,1)S(1)} %add.115.refs_0_), channel_id=1, source_target_pairs={{0,4},{1,5},{2,6},{3,7},{4,0},{5,1},{6,2},{7,3},{8,12},{9,13},{10,... | collective-permute-start | bytes 294920 | tf_op jit(solution)/shard_map/ppermute | solution.py:384
  37.9 11.0 %collective-permute-start.5 = (bf16[4,48,256]{2,1,0:T(8,128)(2,1)S(1)}, bf16[4,48,256]{2,1,0:T(8,128)(2,1)S(1)}, u32[]{:S(2)}, u32[]{:S(2)}) collective-permute-start(bf16[4,48,256]{2,1,0:T(8,128)(2,1)S(1)} %add.115.refs_0_), channel_id=1, source_target_pairs={{0,6},{1,7},{2,4},{3,5},{4,2},{5,3},{6,0},{7,1},{8,14},{9,15},{10,... | collective-permute-start | bytes 294920 | tf_op jit(solution)/shard_map/ppermute | solution.py:384
  41.0 8.0 %collective-permute-start.6 = (bf16[4,48,256]{2,1,0:T(8,128)(2,1)S(1)}, bf16[4,48,256]{2,1,0:T(8,128)(2,1)S(1)}, u32[]{:S(2)}, u32[]{:S(2)}) collective-permute-start(bf16[4,48,256]{2,1,0:T(8,128)(2,1)S(1)} %add.115.refs_0_), channel_id=1, source_target_pairs={{0,2},{1,3},{2,0},{3,1},{4,6},{5,7},{6,4},{7,5},{8,10},{9,11},{10,... | collective-permute-start | bytes 294920 | tf_op jit(solution)/shard_map/ppermute | solution.py:384
  41.5 1.6 %copy-start.3 = (bf16[4,512,512]{2,1,0:T(8,128)(2,1)S(1)}, bf16[4,512,512]{2,1,0:T(8,128)(2,1)}, u32[]{:S(2)}) copy-start(bf16[4,512,512]{2,1,0:T(8,128)(2,1)} %copy-done.2) | copy-start | bytes 6291460
  43.1 1.1 copy-start.7
  44.2 13.5 %copy-start.8 = (bf16[4,192,512]{2,1,0:T(8,128)(2,1)S(1)}, bf16[4,192,512]{2,1,0:T(8,128)(2,1)}, u32[]{:S(2)}) copy-start(bf16[4,192,512]{2,1,0:T(8,128)(2,1)} %copy-done.5) | copy-start | bytes 2359300
  49.3 5.7 %collective-permute-start.10 = (bf16[4,48,256]{2,1,0:T(8,128)(2,1)S(1)}, bf16[4,48,256]{2,1,0:T(8,128)(2,1)S(1)}, u32[]{:S(2)}, u32[]{:S(2)}) collective-permute-start(bf16[4,48,256]{2,1,0:T(8,128)(2,1)S(1)} %reflect.2.refs_0_), channel_id=1, source_target_pairs={{0,17},{1,16},{2,19},{3,18},{4,21},{5,20},{6,23},{7,22},{8,25},{9,... | collective-permute-start | bytes 294920 | tf_op jit(solution)/shard_map/ppermute | solution.py:384
  51.0 6.2 %collective-permute-start.11 = (bf16[4,48,256]{2,1,0:T(8,128)(2,1)S(1)}, bf16[4,48,256]{2,1,0:T(8,128)(2,1)S(1)}, u32[]{:S(2)}, u32[]{:S(2)}) collective-permute-start(bf16[4,48,256]{2,1,0:T(8,128)(2,1)S(1)} %reflect.2.refs_0_), channel_id=1, source_target_pairs={{0,16},{1,17},{2,18},{3,19},{4,20},{5,21},{6,22},{7,23},{8,24},{9,... | collective-permute-start | bytes 294920 | tf_op jit(solution)/shard_map/ppermute | solution.py:384
  52.9 8.9 %collective-permute-start.14 = (bf16[4,48,256]{2,1,0:T(8,128)(2,1)S(1)}, bf16[4,48,256]{2,1,0:T(8,128)(2,1)S(1)}, u32[]{:S(2)}, u32[]{:S(2)}) collective-permute-start(bf16[4,48,256]{2,1,0:T(8,128)(2,1)S(1)} %reflect.2.refs_0_), channel_id=1, source_target_pairs={{0,8},{1,9},{2,10},{3,11},{4,12},{5,13},{6,14},{7,15},{8,0},{9,1},... | collective-permute-start | bytes 294920 | tf_op jit(solution)/shard_map/ppermute | solution.py:384
  55.0 6.6 %collective-permute-start.12 = (bf16[4,48,256]{2,1,0:T(8,128)(2,1)S(1)}, bf16[4,48,256]{2,1,0:T(8,128)(2,1)S(1)}, u32[]{:S(2)}, u32[]{:S(2)}) collective-permute-start(bf16[4,48,256]{2,1,0:T(8,128)(2,1)S(1)} %collective-permute-done.10.refs_1_), channel_id=1, source_target_pairs={{0,16},{1,17},{2,18},{3,19},{4,20},{5,21},{6,22},{7,23},{8,24},{9,... | collective-permute-start | bytes 294920 | tf_op jit(solution)/shard_map/ppermute | solution.py:384
  57.2 4.6 %collective-permute-start.15 = (bf16[4,48,256]{2,1,0:T(8,128)(2,1)S(1)}, bf16[4,48,256]{2,1,0:T(8,128)(2,1)S(1)}, u32[]{:S(2)}, u32[]{:S(2)}) collective-permute-start(bf16[4,48,256]{2,1,0:T(8,128)(2,1)S(1)} %collective-permute-done.10.refs_1_), channel_id=1, source_target_pairs={{0,8},{1,9},{2,10},{3,11},{4,12},{5,13},{6,14},{7,15},{8,0},{9,1},... | collective-permute-start | bytes 294920 | tf_op jit(solution)/shard_map/ppermute | solution.py:384
  57.2 4.7 %collective-permute-start.16 = (bf16[4,48,256]{2,1,0:T(8,128)(2,1)S(1)}, bf16[4,48,256]{2,1,0:T(8,128)(2,1)S(1)}, u32[]{:S(2)}, u32[]{:S(2)}) collective-permute-start(bf16[4,48,256]{2,1,0:T(8,128)(2,1)S(1)} %collective-permute-done.11.refs_2_), channel_id=1, source_target_pairs={{0,8},{1,9},{2,10},{3,11},{4,12},{5,13},{6,14},{7,15},{8,0},{9,1},... | collective-permute-start | bytes 294920 | tf_op jit(solution)/shard_map/ppermute | solution.py:384
  57.7 5.2 %copy-start = (bf16[8,512,512]{2,1,0:T(8,128)(2,1)S(1)}, bf16[8,512,512]{2,1,0:T(8,128)(2,1)}, u32[]{:S(2)}) copy-start(bf16[8,512,512]{2,1,0:T(8,128)(2,1)} %refs_10_.5) | copy-start | bytes 12582916
  61.6 1.4 %collective-permute-start.17 = (bf16[4,48,256]{2,1,0:T(8,128)(2,1)S(1)}, bf16[4,48,256]{2,1,0:T(8,128)(2,1)S(1)}, u32[]{:S(2)}, u32[]{:S(2)}) collective-permute-start(bf16[4,48,256]{2,1,0:T(8,128)(2,1)S(1)} %collective-permute-done.12.refs_3_), channel_id=1, source_target_pairs={{0,8},{1,9},{2,10},{3,11},{4,12},{5,13},{6,14},{7,15},{8,0},{9,1},... | collective-permute-start | bytes 294920 | tf_op jit(solution)/shard_map/ppermute | solution.py:384
  66.2 27.2 %collective-permute-start.21 = (bf16[4,192,512]{2,1,0:T(8,128)(2,1)S(1)}, bf16[4,192,512]{2,1,0:T(8,128)(2,1)S(1)}, u32[]{:S(2)}, u32[]{:S(2)}) collective-permute-start(bf16[4,192,512]{2,1,0:T(8,128)(2,1)S(1)} %back.3.refs_0_.own_ref.inner_ref), channel_id=1, source_target_pairs={{1,2},{2,1},{3,4},{4,3},{5,6},{6,5},{7,8},{8,7},{9,10},{10,9},{11,... | collective-permute-start | bytes 2359304 | tf_op jit(solution)/shard_map/ppermute | solution.py:435
  72.1 6.3 %collective-permute-start.18 = (bf16[8,96,256]{2,1,0:T(8,128)(2,1)S(1)}, bf16[8,96,256]{2,1,0:T(8,128)(2,1)S(1)}, u32[]{:S(2)}, u32[]{:S(2)}) collective-permute-start(bf16[8,96,256]{2,1,0:T(8,128)(2,1)S(1)} %outward.7), channel_id=1, source_target_pairs={{0,8},{1,9},{2,10},{3,11},{4,12},{5,13},{6,14},{7,15},{8,0},{9,1},... | collective-permute-start | bytes 1179656 | tf_op jit(solution)/shard_map/ppermute | solution.py:384
  76.6 21.3 %copy-start.4 = (bf16[4,512,512]{2,1,0:T(8,128)(2,1)S(1)}, bf16[4,512,512]{2,1,0:T(8,128)(2,1)}, u32[]{:S(2)}) copy-start(bf16[4,512,512]{2,1,0:T(8,128)(2,1)} %copy-done.2) | copy-start | bytes 6291460
  79.1 6.9 %collective-permute-start.19 = (bf16[8,48,256]{2,1,0:T(8,128)(2,1)S(1)}, bf16[8,48,256]{2,1,0:T(8,128)(2,1)S(1)}, u32[]{:S(2)}, u32[]{:S(2)}) collective-permute-start(bf16[8,48,256]{2,1,0:T(8,128)(2,1)S(1)} %get-tuple-element.53), channel_id=1, source_target_pairs={{0,16},{1,17},{2,18},{3,19},{4,20},{5,21},{6,22},{7,23},{8,24},{9,... | collective-permute-start | bytes 589832 | tf_op jit(solution)/shard_map/ppermute | solution.py:384
  86.6 6.8 %collective-permute-start.20 = (bf16[4,48,256]{2,1,0:T(8,128)(2,1)S(1)}, bf16[4,48,256]{2,1,0:T(8,128)(2,1)S(1)}, u32[]{:S(2)}, u32[]{:S(2)}) collective-permute-start(bf16[4,48,256]{2,1,0:T(8,128)(2,1)S(1)} %get-tuple-element.55), channel_id=1, source_target_pairs={{0,17},{1,16},{2,19},{3,18},{4,21},{5,20},{6,23},{7,22},{8,25},{9,... | collective-permute-start | bytes 294920 | tf_op jit(solution)/shard_map/ppermute | solution.py:384
  93.4 21.4 %collective-permute-start.32 = (bf16[4,192,512]{2,1,0:T(8,128)(2,1)S(1)}, bf16[4,192,512]{2,1,0:T(8,128)(2,1)S(1)}, u32[]{:S(2)}, u32[]{:S(2)}) collective-permute-start(bf16[4,192,512]{2,1,0:T(8,128)(2,1)S(1)} %back.4.refs_1_.inner_ref.own_ref), channel_id=1, source_target_pairs={{0,1},{1,0},{2,3},{3,2},{4,5},{5,4},{6,7},{7,6},{8,9},{9,8},{10,11... | collective-permute-start | bytes 2359304 | tf_op jit(solution)/shard_map/ppermute | solution.py:455
  94.4 8.7 %collective-permute-start.22 = (bf16[4,48,256]{2,1,0:T(8,128)(2,1)S(1)}, bf16[4,48,256]{2,1,0:T(8,128)(2,1)S(1)}, u32[]{:S(2)}, u32[]{:S(2)}) collective-permute-start(bf16[4,48,256]{2,1,0:T(8,128)(2,1)S(1)} %add.116.refs_0_), channel_id=1, source_target_pairs={{0,4},{1,5},{2,6},{3,7},{4,0},{5,1},{6,2},{7,3},{8,12},{9,13},{10,... | collective-permute-start | bytes 294920 | tf_op jit(solution)/shard_map/ppermute | solution.py:384
  95.0 8.1 %collective-permute-start.23 = (bf16[4,48,256]{2,1,0:T(8,128)(2,1)S(1)}, bf16[4,48,256]{2,1,0:T(8,128)(2,1)S(1)}, u32[]{:S(2)}, u32[]{:S(2)}) collective-permute-start(bf16[4,48,256]{2,1,0:T(8,128)(2,1)S(1)} %add.116.refs_0_), channel_id=1, source_target_pairs={{0,6},{1,7},{2,4},{3,5},{4,2},{5,3},{6,0},{7,1},{8,14},{9,15},{10,... | collective-permute-start | bytes 294920 | tf_op jit(solution)/shard_map/ppermute | solution.py:384
  96.5 6.6 %collective-permute-start.24 = (bf16[4,48,256]{2,1,0:T(8,128)(2,1)S(1)}, bf16[4,48,256]{2,1,0:T(8,128)(2,1)S(1)}, u32[]{:S(2)}, u32[]{:S(2)}) collective-permute-start(bf16[4,48,256]{2,1,0:T(8,128)(2,1)S(1)} %add.116.refs_0_), channel_id=1, source_target_pairs={{0,2},{1,3},{2,0},{3,1},{4,6},{5,7},{6,4},{7,5},{8,10},{9,11},{10,... | collective-permute-start | bytes 294920 | tf_op jit(solution)/shard_map/ppermute | solution.py:384
  103.4 6.3 %collective-permute-start.25 = (bf16[4,48,256]{2,1,0:T(8,128)(2,1)S(1)}, bf16[4,48,256]{2,1,0:T(8,128)(2,1)S(1)}, u32[]{:S(2)}, u32[]{:S(2)}) collective-permute-start(bf16[4,48,256]{2,1,0:T(8,128)(2,1)S(1)} %reflect.3.refs_0_), channel_id=1, source_target_pairs={{0,17},{1,16},{2,19},{3,18},{4,21},{5,20},{6,23},{7,22},{8,25},{9,... | collective-permute-start | bytes 294920 | tf_op jit(solution)/shard_map/ppermute | solution.py:384
  105.1 7.7 %collective-permute-start.26 = (bf16[4,48,256]{2,1,0:T(8,128)(2,1)S(1)}, bf16[4,48,256]{2,1,0:T(8,128)(2,1)S(1)}, u32[]{:S(2)}, u32[]{:S(2)}) collective-permute-start(bf16[4,48,256]{2,1,0:T(8,128)(2,1)S(1)} %reflect.3.refs_0_), channel_id=1, source_target_pairs={{0,16},{1,17},{2,18},{3,19},{4,20},{5,21},{6,22},{7,23},{8,24},{9,... | collective-permute-start | bytes 294920 | tf_op jit(solution)/shard_map/ppermute | solution.py:384
  109.8 5.1 %collective-permute-start.27 = (bf16[4,48,256]{2,1,0:T(8,128)(2,1)S(1)}, bf16[4,48,256]{2,1,0:T(8,128)(2,1)S(1)}, u32[]{:S(2)}, u32[]{:S(2)}) collective-permute-start(bf16[4,48,256]{2,1,0:T(8,128)(2,1)S(1)} %collective-permute-done.25.refs_1_), channel_id=1, source_target_pairs={{0,16},{1,17},{2,18},{3,19},{4,20},{5,21},{6,22},{7,23},{8,24},{9,... | collective-permute-start | bytes 294920 | tf_op jit(solution)/shard_map/ppermute | solution.py:384
  112.2 6.5 %collective-permute-start.28 = (bf16[4,48,256]{2,1,0:T(8,128)(2,1)S(1)}, bf16[4,48,256]{2,1,0:T(8,128)(2,1)S(1)}, u32[]{:S(2)}, u32[]{:S(2)}) collective-permute-start(bf16[4,48,256]{2,1,0:T(8,128)(2,1)S(1)} %reflect.3.refs_0_), channel_id=1, source_target_pairs={{0,8},{1,9},{2,10},{3,11},{4,12},{5,13},{6,14},{7,15},{8,0},{9,1},... | collective-permute-start | bytes 294920 | tf_op jit(solution)/shard_map/ppermute | solution.py:384
  112.3 6.5 %collective-permute-start.29 = (bf16[4,48,256]{2,1,0:T(8,128)(2,1)S(1)}, bf16[4,48,256]{2,1,0:T(8,128)(2,1)S(1)}, u32[]{:S(2)}, u32[]{:S(2)}) collective-permute-start(bf16[4,48,256]{2,1,0:T(8,128)(2,1)S(1)} %collective-permute-done.25.refs_1_), channel_id=1, source_target_pairs={{0,8},{1,9},{2,10},{3,11},{4,12},{5,13},{6,14},{7,15},{8,0},{9,1},... | collective-permute-start | bytes 294920 | tf_op jit(solution)/shard_map/ppermute | solution.py:384
  112.8 6.0 %collective-permute-start.30 = (bf16[4,48,256]{2,1,0:T(8,128)(2,1)S(1)}, bf16[4,48,256]{2,1,0:T(8,128)(2,1)S(1)}, u32[]{:S(2)}, u32[]{:S(2)}) collective-permute-start(bf16[4,48,256]{2,1,0:T(8,128)(2,1)S(1)} %collective-permute-done.26.refs_2_), channel_id=1, source_target_pairs={{0,8},{1,9},{2,10},{3,11},{4,12},{5,13},{6,14},{7,15},{8,0},{9,1},... | collective-permute-start | bytes 294920 | tf_op jit(solution)/shard_map/ppermute | solution.py:384
  114.8 3.9 %collective-permute-start.31 = (bf16[4,48,256]{2,1,0:T(8,128)(2,1)S(1)}, bf16[4,48,256]{2,1,0:T(8,128)(2,1)S(1)}, u32[]{:S(2)}, u32[]{:S(2)}) collective-permute-start(bf16[4,48,256]{2,1,0:T(8,128)(2,1)S(1)} %collective-permute-done.27.refs_3_), channel_id=1, source_target_pairs={{0,8},{1,9},{2,10},{3,11},{4,12},{5,13},{6,14},{7,15},{8,0},{9,1},... | collective-permute-start | bytes 294920 | tf_op jit(solution)/shard_map/ppermute | solution.py:384
